TPU v7x, 32 devices: a whole 2x2x4 slice. The times are simulated.
32 devices in a mesh: ctx: 16 (over z, y, core), tp: 2 (over x).
Axes of the slice: x: 2, y: 2, z: 4, core: 2. Of those that a mesh axis runs over, the one named last changes fastest.
Arguments:
- tokens: bfloat16 [2, 1024, 896], P(None, 'ctx'), may hold values from -6 to 6
- cotangent: bfloat16 [2, 1024, 896], P(None, 'ctx'), may hold values from -6 to 6
- block_of: int32 [2, 32], replicated, may hold values from 0 to 31, as said below
- norm_gain: bfloat16 [896], P('ctx'), may hold values from 0.5 to 1.5
- ffn_gain: bfloat16 [896], P('ctx'), may hold values from 0.5 to 1.5
- w_query: bfloat16 [896, 896], P('ctx', 'tp'), may hold values from -0.1875 to 0.1875
- w_key: bfloat16 [896, 128], P('ctx', 'tp'), may hold values from -0.1875 to 0.1875
- w_value: bfloat16 [896, 128], P('ctx', 'tp'), may hold values from -0.1875 to 0.1875
- b_query: bfloat16 [896], P('tp'), may hold values from -3 to 3
- b_key: bfloat16 [128], P('tp'), may hold values from -3 to 3
- b_value: bfloat16 [128], P('tp'), may hold values from -3 to 3
- w_out: bfloat16 [896, 896], P('tp', 'ctx'), may hold values from -0.75 to 0.75
- w_gate: bfloat16 [896, 4864], P('ctx', 'tp'), may hold values from -0.1875 to 0.1875
- w_up: bfloat16 [896, 4864], P('ctx', 'tp'), may hold values from -0.1875 to 0.1875
- w_down: bfloat16 [4864, 896], P('tp', 'ctx'), may hold values from -0.078125 to 0.078125
Outputs:
- mixed: bfloat16 [2, 1024, 896], P(None, 'ctx')
- tokens_grad: bfloat16 [2, 1024, 896], P(None, 'ctx')
- norm_gain_grad: float32 [896], P('ctx')
- ffn_gain_grad: float32 [896], P('ctx')
- w_query_grad: float32 [896, 896], P('ctx', 'tp')
- w_key_grad: float32 [896, 128], P('ctx', 'tp')
- w_value_grad: float32 [896, 128], P('ctx', 'tp')
- b_query_grad: float32 [896], P('tp')
- b_key_grad: float32 [128], P('tp')
- b_value_grad: float32 [128], P('tp')
- w_out_grad: float32 [896, 896], P('tp', 'ctx')
- w_gate_grad: float32 [896, 4864], P('ctx', 'tp')
- w_up_grad: float32 [896, 4864], P('ctx', 'tp')
- w_down_grad: float32 [4864, 896], P('tp', 'ctx')
Inputs may be any that keep to these rules, and one draw needn't show every extreme that they name: For each sequence s and each d < 16, entries 2d and 2d+1 of block_of[s] hold the blocks d and 31-d, in either order.
All inputs are finite; a program needn't handle non-finite values.
Results may differ from a plain program's by a relative error of at most 0.025.
Values may be sent and summed in bfloat16 or wider, within the bound.
No kernel may reach another device: no remote copies, remote signals or barrier semaphores. Data moves between devices by JAX's collectives and lax.ppermute only.
A program may use at most 192 MiB of HBM per device.

v0:
```python
import jax
import jax.numpy as jnp
from jax import lax
from jax.sharding import PartitionSpec as P

HEADS = 14
KV_HEADS = 2
HEAD = 64


EPSILON = 1e-06
ROPE_BASE = 1000000.0


def rope_tables(positions, head_dim):
    halfway = head_dim // 2
    inverse = ROPE_BASE ** (-(jnp.arange(halfway, dtype=jnp.float32) * 2.0 / head_dim))
    angles = positions.astype(jnp.float32)[..., None] * inverse
    angles = jnp.concatenate([angles, angles], axis=-1)
    return (jnp.cos(angles), jnp.sin(angles))


def rotate(values, cosine, sine):
    halfway = values.shape[-1] // 2
    turned = jnp.concatenate([-values[..., halfway:], values[..., :halfway]], axis=-1)
    return values * cosine + turned * sine


def unrotate(grads, cosine, sine):
    halfway = grads.shape[-1] // 2
    moved = grads * sine
    back = jnp.concatenate([moved[..., halfway:], -moved[..., :halfway]], axis=-1)
    return grads * cosine + back


def norm_apply(values, gain):
    factor = lax.rsqrt(jnp.mean(values * values, axis=-1, keepdims=True) + EPSILON)
    return (values * factor * gain, factor)


def norm_back(values, factor, gain, grads):
    weighted = grads * gain
    inner = jnp.mean(weighted * values, axis=-1, keepdims=True)
    d_values = factor * weighted - values * factor * factor * factor * inner
    d_gain = jnp.sum(grads * values * factor, axis=(0, 1))
    return (d_values, d_gain)


def to_groups(values, kv_heads):
    seq_count, row_count = (values.shape[0], values.shape[1])
    shaped = values.reshape(seq_count, row_count, kv_heads, -1, HEAD)
    group = shaped.shape[3]
    return shaped.transpose(0, 2, 1, 3, 4).reshape(seq_count, kv_heads, row_count * group, HEAD)


def from_groups(values, row_count):
    seq_count, kv_heads = (values.shape[0], values.shape[1])
    shaped = values.reshape(seq_count, kv_heads, row_count, -1, values.shape[-1])
    return shaped.transpose(0, 2, 1, 3, 4).reshape(seq_count, row_count, -1)


def matmul(values, matrix):
    return jnp.einsum("srd,df->srf", values, matrix, preferred_element_type=jnp.float32)


def matmul_back(grads, matrix):
    return jnp.einsum("srf,df->srd", grads, matrix, preferred_element_type=jnp.float32)


def outer_sum(left, right):
    return jnp.einsum("srd,srf->df", left, right, preferred_element_type=jnp.float32)


def local(
    tokens,
    cotangent,
    block_of,
    norm_gain,
    ffn_gain,
    w_query,
    w_key,
    w_value,
    b_query,
    b_key,
    b_value,
    w_out,
    w_gate,
    w_up,
    w_down,
):
    seq_count, row_count, width = tokens.shape
    block_len = row_count // 2
    head_dim = HEAD
    group = HEADS // KV_HEADS
    factor = head_dim ** (-0.5)
    kv_local = w_key.shape[1] // head_dim
    query_local = w_query.shape[1] // head_dim
    gathered = (
        lax.all_gather(norm_gain, "ctx", axis=0, tiled=True),
        lax.all_gather(ffn_gain, "ctx", axis=0, tiled=True),
        lax.all_gather(w_query, "ctx", axis=0, tiled=True),
        lax.all_gather(w_key, "ctx", axis=0, tiled=True),
        lax.all_gather(w_value, "ctx", axis=0, tiled=True),
        lax.all_gather(w_out, "ctx", axis=1, tiled=True),
        lax.all_gather(w_gate, "ctx", axis=0, tiled=True),
        lax.all_gather(w_up, "ctx", axis=0, tiled=True),
        lax.all_gather(w_down, "ctx", axis=1, tiled=True),
    )
    (
        gain_one,
        gain_two,
        full_query,
        full_key,
        full_value,
        full_out,
        full_gate,
        full_up,
        full_down,
    ) = gathered
    gain_one = gain_one.astype(jnp.float32)
    gain_two = gain_two.astype(jnp.float32)
    own_blocks = lax.dynamic_slice_in_dim(block_of, lax.axis_index("ctx") * 2, 2, 1)
    offsets = jnp.arange(block_len, dtype=jnp.int32)
    row_pos = (own_blocks[:, :, None] * block_len + offsets).reshape(seq_count, row_count)
    key_pos = (block_of[:, :, None] * block_len + offsets).reshape(
        seq_count, block_of.shape[1] * block_len
    )
    cosine, sine = rope_tables(row_pos, head_dim)
    cosine = cosine[:, :, None, :]
    sine = sine[:, :, None, :]
    inputs = tokens.astype(jnp.float32)
    normed, scale_one = norm_apply(inputs, gain_one)
    normed_low = normed.astype(jnp.bfloat16)
    query_lin = matmul(normed_low, full_query) + b_query.astype(jnp.float32)
    key_lin = matmul(normed_low, full_key) + b_key.astype(jnp.float32)
    value_lin = (matmul(normed_low, full_value) + b_value.astype(jnp.float32)).astype(jnp.bfloat16)
    query_rot = rotate(query_lin.reshape(seq_count, row_count, query_local, head_dim), cosine, sine)
    key_rot = rotate(key_lin.reshape(seq_count, row_count, kv_local, head_dim), cosine, sine)
    queries = to_groups(query_rot.astype(jnp.bfloat16), kv_local)
    rows_pos = jnp.repeat(row_pos, group, axis=1)
    pair_local = jnp.concatenate(
        [key_rot.astype(jnp.bfloat16), value_lin.reshape(seq_count, row_count, kv_local, head_dim)],
        axis=-1,
    ).transpose(0, 2, 1, 3)
    query_rows = queries.shape[2]

    def key_blocks(piece, step, state):
        key_count = piece.shape[2]
        span = 512

        def inner(carry, index):
            part = lax.dynamic_slice_in_dim(piece, index * span, span, 2)
            part_pos = lax.dynamic_slice_in_dim(key_pos, index * span, span, 1)
            return step(carry, part, part_pos)

        return lax.scan(inner, state, jnp.arange(key_count // span, dtype=jnp.int32))

    def block_scores(part, part_pos):
        scores = (
            jnp.einsum(
                "abqd,abkd->abqk", queries, part[..., :head_dim], preferred_element_type=jnp.float32
            )
            * factor
        )
        allowed = part_pos[:, None, None, :] <= rows_pos[:, None, :, None]
        return (scores, allowed)

    def forward_step(state, part, part_pos):
        best, totals, summed = state
        scores, allowed = block_scores(part, part_pos)
        newest = jnp.maximum(best, jnp.max(jnp.where(allowed, scores, -1e30), axis=-1))
        raised = jnp.where(allowed, jnp.exp(scores - newest[..., None]), 0.0)
        fading = jnp.exp(best - newest)
        totals = totals * fading + jnp.sum(raised, axis=-1)
        summed = summed * fading[..., None] + jnp.einsum(
            "abqk,abkd->abqd",
            raised.astype(jnp.bfloat16),
            part[..., head_dim:],
            preferred_element_type=jnp.float32,
        )
        return ((newest, totals, summed), None)

    init_state = (
        jnp.full((seq_count, kv_local, query_rows), -1e30, jnp.float32),
        jnp.zeros((seq_count, kv_local, query_rows), jnp.float32),
        jnp.zeros((seq_count, kv_local, query_rows, head_dim), jnp.float32),
    )
    state = init_state
    state, unused = key_blocks(
        lax.all_gather(pair_local, "ctx", axis=2, tiled=True), forward_step, state
    )
    best, totals, summed = state
    out_rows = summed / totals[..., None]
    log_total = best + jnp.log(totals)
    out_flat = from_groups(out_rows.astype(jnp.bfloat16), row_count)
    attention = lax.psum(matmul(out_flat, full_out).astype(jnp.bfloat16), "tp").astype(jnp.float32)
    hidden = inputs + attention
    normed_two, scale_two = norm_apply(hidden, gain_two)
    normed_two_low = normed_two.astype(jnp.bfloat16)
    gate = matmul(normed_two_low, full_gate)
    up_values = matmul(normed_two_low, full_up)
    sigma = jax.nn.sigmoid(gate)
    active = (gate * sigma * up_values).astype(jnp.bfloat16)
    down_sum = lax.psum(matmul(active, full_down).astype(jnp.bfloat16), "tp").astype(jnp.float32)
    mixed = (hidden + down_sum).astype(jnp.bfloat16)
    d_down = outer_sum(active, cotangent)
    d_active = matmul_back(cotangent, full_down)
    d_gate = (d_active * up_values * sigma * (1.0 + gate * (1.0 - sigma))).astype(jnp.bfloat16)
    d_up = (d_active * gate * sigma).astype(jnp.bfloat16)
    d_wgate = outer_sum(normed_two_low, d_gate)
    d_wup = outer_sum(normed_two_low, d_up)
    d_normed_two = lax.psum(
        (matmul_back(d_gate, full_gate) + matmul_back(d_up, full_up)).astype(jnp.bfloat16), "tp"
    ).astype(jnp.float32)
    d_hidden_norm, d_gain_two = norm_back(hidden, scale_two, gain_two, d_normed_two)
    d_hidden = cotangent.astype(jnp.float32) + d_hidden_norm
    d_hidden_low = d_hidden.astype(jnp.bfloat16)
    d_wout = outer_sum(out_flat, d_hidden_low)
    d_out = to_groups(matmul_back(d_hidden_low, full_out).astype(jnp.bfloat16), kv_local)
    row_dots = jnp.sum(d_out.astype(jnp.float32) * out_rows, axis=-1)

    def backward_step(carry, part, part_pos):
        scores, allowed = block_scores(part, part_pos)
        chances = jnp.where(allowed, jnp.exp(scores - log_total[..., None]), 0.0)
        d_chances = jnp.einsum(
            "abqd,abkd->abqk", d_out, part[..., head_dim:], preferred_element_type=jnp.float32
        )
        d_scores = (chances * (d_chances - row_dots[..., None])).astype(jnp.bfloat16)
        carry = (
            carry
            + jnp.einsum(
                "abqk,abkd->abqd",
                d_scores,
                part[..., :head_dim],
                preferred_element_type=jnp.float32,
            )
            * factor
        )
        d_keys = (
            jnp.einsum("abqk,abqd->abkd", d_scores, queries, preferred_element_type=jnp.float32)
            * factor
        )
        d_values = jnp.einsum(
            "abqk,abqd->abkd",
            chances.astype(jnp.bfloat16),
            d_out,
            preferred_element_type=jnp.float32,
        )
        return (carry, jnp.concatenate([d_keys, d_values], axis=-1))

    piece = lax.all_gather(pair_local, "ctx", axis=2, tiled=True)
    d_query = jnp.zeros((seq_count, kv_local, query_rows, head_dim), jnp.float32)
    d_query, stacked = key_blocks(piece, backward_step, d_query)
    fresh = jnp.moveaxis(stacked, 0, 2).reshape(seq_count, kv_local, piece.shape[2], 2 * head_dim)
    d_pairs = fresh
    d_query_rows, d_pairs = (d_query, d_pairs)
    pair_grads = lax.psum_scatter(d_pairs, "ctx", scatter_dimension=2, tiled=True).transpose(
        0, 2, 1, 3
    )
    d_query_rot = from_groups(d_query_rows, row_count).reshape(
        seq_count, row_count, query_local, head_dim
    )
    d_query_low = (
        unrotate(d_query_rot, cosine, sine).reshape(seq_count, row_count, -1).astype(jnp.bfloat16)
    )
    d_key_low = (
        unrotate(pair_grads[..., :head_dim], cosine, sine)
        .reshape(seq_count, row_count, -1)
        .astype(jnp.bfloat16)
    )
    d_value_low = pair_grads[..., head_dim:].reshape(seq_count, row_count, -1).astype(jnp.bfloat16)
    d_wquery = outer_sum(normed_low, d_query_low)
    d_wkey = outer_sum(normed_low, d_key_low)
    d_wvalue = outer_sum(normed_low, d_value_low)
    bias_sums = lax.psum(
        (
            jnp.sum(d_query_low.astype(jnp.float32), axis=(0, 1)),
            jnp.sum(d_key_low.astype(jnp.float32), axis=(0, 1)),
            jnp.sum(d_value_low.astype(jnp.float32), axis=(0, 1)),
        ),
        "ctx",
    )
    d_normed = lax.psum(
        (
            matmul_back(d_query_low, full_query)
            + matmul_back(d_key_low, full_key)
            + matmul_back(d_value_low, full_value)
        ).astype(jnp.bfloat16),
        "tp",
    ).astype(jnp.float32)
    d_input_norm, d_gain_one = norm_back(inputs, scale_one, gain_one, d_normed)
    tokens_grad = (d_hidden + d_input_norm).astype(jnp.bfloat16)
    summed_grads = (
        lax.psum_scatter(d_gain_one, "ctx", scatter_dimension=0, tiled=True),
        lax.psum_scatter(d_gain_two, "ctx", scatter_dimension=0, tiled=True),
        lax.psum_scatter(d_wquery, "ctx", scatter_dimension=0, tiled=True),
        lax.psum_scatter(d_wkey, "ctx", scatter_dimension=0, tiled=True),
        lax.psum_scatter(d_wvalue, "ctx", scatter_dimension=0, tiled=True),
        lax.psum_scatter(d_wout, "ctx", scatter_dimension=1, tiled=True),
        lax.psum_scatter(d_wgate, "ctx", scatter_dimension=0, tiled=True),
        lax.psum_scatter(d_wup, "ctx", scatter_dimension=0, tiled=True),
        lax.psum_scatter(d_down, "ctx", scatter_dimension=1, tiled=True),
    )
    g_one, g_two, g_query, g_key, g_value, g_out, g_gate, g_up, g_down = summed_grads
    return (
        mixed,
        tokens_grad,
        g_one,
        g_two,
        g_query,
        g_key,
        g_value,
        bias_sums[0],
        bias_sums[1],
        bias_sums[2],
        g_out,
        g_gate,
        g_up,
        g_down,
    )


def solution(mesh):
    placed = (
        P(None, "ctx", None),
        P(None, "ctx", None),
        P(),
        P("ctx"),
        P("ctx"),
        P("ctx", "tp"),
        P("ctx", "tp"),
        P("ctx", "tp"),
        P("tp"),
        P("tp"),
        P("tp"),
        P("tp", "ctx"),
        P("ctx", "tp"),
        P("ctx", "tp"),
        P("tp", "ctx"),
    )
    return jax.shard_map(
        local,
        mesh=mesh,
        in_specs=placed,
        out_specs=(
            P(None, "ctx", None),
            P(None, "ctx", None),
            P("ctx"),
            P("ctx"),
            P("ctx", "tp"),
            P("ctx", "tp"),
            P("ctx", "tp"),
            P("tp"),
            P("tp"),
            P("tp"),
            P("tp", "ctx"),
            P("ctx", "tp"),
            P("ctx", "tp"),
            P("tp", "ctx"),
        ),
        check_vma=False,
    )
```

profile of v0, /device:TPU:0, one launch (start us, length us, event | category | flops | bytes accessed | tf_op | source)
XLA Modules:
  0.0 1070.4 jit_solution(9644504291170101193)
XLA Ops:
  8.1 1.3 fusion.124
  11.8 34.9 %all-reduce.11 = (bf16[896]{0:T(1024)(128)(2,1)S(1)}, bf16[896]{0:T(1024)(128)(2,1)S(1)}) all-reduce(bf16[896]{0:T(1024)(128)(2,1)S(1)} %dynamic-update-slice, bf16[896]{0:T(1024)(128)(2,1)S(1)} %dynamic-update-slice.1), channel_id=1, replica_groups=mesh['ctx'=16,'tp'=2] {'ctx'}, use_global_device_ids=true, to_apply=%add | all-reduce | flops 1792 | bytes 7168
  47.9 20.3 %all_gather.35 = bf16[896,448]{1,0:T(8,128)(2,1)S(1)} all-gather(bf16[56,448]{1,0:T(8,128)(2,1)} %param.24), channel_id=1, replica_groups=mesh['ctx'=16,'tp'=2] {'ctx'}, dimensions={0}, use_global_device_ids=true | all-gather | bytes 852992 | tf_op jit(solution)/shard_map/all_gather | solution.py:101
  70.9 19.4 %all_gather.33 = bf16[896,64]{1,0:T(8,128)(2,1)S(1)} all-gather(bf16[56,64]{1,0:T(8,128)(2,1)S(1)} %copy-done.37), channel_id=1, replica_groups=mesh['ctx'=16,'tp'=2] {'ctx'}, dimensions={0}, use_global_device_ids=true | all-gather | bytes 121856 | tf_op jit(solution)/shard_map/all_gather | solution.py:103
  90.7 18.0 %all_gather.32 = bf16[896,64]{1,0:T(8,128)(2,1)S(1)} all-gather(bf16[56,64]{1,0:T(8,128)(2,1)S(1)} %copy-done.38), channel_id=1, replica_groups=mesh['ctx'=16,'tp'=2] {'ctx'}, dimensions={0}, use_global_device_ids=true | all-gather | bytes 121856 | tf_op jit(solution)/shard_map/all_gather | solution.py:102
  110.5 20.3 %all-gather = bf16[2,1024,1,128]{3,0,2,1:T(2,128)(2,1)S(1)} all-gather(bf16[2,64,1,128]{3,0,2,1:T(2,128)(2,1)S(1)} %copy.93), channel_id=2, replica_groups=mesh['ctx'=16,'tp'=2] {'ctx'}, dimensions={1}, use_global_device_ids=true | all-gather | bytes 557056 | tf_op jit(solution)/shard_map/all_gather | solution.py:190
  134.7 11.7 %while.28 = (s32[]{:T(128)}, f32[2,1,448]{2,0,1:T(2,128)S(1)}, f32[2,1,448]{2,0,1:T(2,128)S(1)}, f32[2,1,448,64]{2,3,0,1:T(8,128)S(1)}, s32[2]{0:T(128)S(1)}, /*...) while((s32[]{:T(128)}, f32[2,1,448]{2,0,1:T(2,128)S(1)}, ...), condition=%wide.region_4.5_spmd.clone, body=%wide.region_1.4_spmd.clone.sunk | while | flops 124040456 | bytes 6440687 | solution.py:156
  136.9 1.5 fusion.160
  139.0 1.5 fusion.163
  142.7 1.5 fusion.160
  144.9 1.5 fusion.163
  147.0 20.0 %all_gather.36 = bf16[448,896]{0,1:T(8,128)(2,1)S(1)} all-gather(bf16[448,56]{0,1:T(8,128)(2,1)S(1)} %copy-done.31), channel_id=1, replica_groups=mesh['ctx'=16,'tp'=2] {'ctx'}, dimensions={1}, use_global_device_ids=true | all-gather | bytes 852992 | tf_op jit(solution)/shard_map/all_gather | solution.py:104
  172.5 17.5 %all-reduce.18.cloned.1.call-done = bf16[2,64,896]{2,1,0:T(8,128)(2,1)} async-done(((bf16[2,64,896]{2,1,0:T(8,128)(2,1)}), bf16[2,64,896]{2,1,0:T(8,128)(2,1)}) %all-reduce.18.cloned.1.call-update) | async-done | bytes 229392 | tf_op jit(solution)/shard_map/psum | solution.py:196
  192.2 28.7 %all-gather.9.cloned.1.call-done = bf16[2432,896]{0,1:T(8,128)(2,1)} async-done(((bf16[2432,56]{0,1:T(8,128)(2,1)}), bf16[2432,896]{0,1:T(8,128)(2,1)}) %all-gather.9.cloned.1.call-update) | async-done | bytes 4358160 | tf_op jit(solution)/shard_map/all_gather | solution.py:107
  220.9 4.1 fusion.34
  225.1 47.6 %all-gather.7.cloned.1.call-done = bf16[896,2432]{1,0:T(8,128)(2,1)} async-done(((bf16[56,2432]{1,0:T(8,128)(2,1)}), bf16[896,2432]{1,0:T(8,128)(2,1)}) %all-gather.7.cloned.1.call-update) | async-done | bytes 4358160 | tf_op jit(solution)/shard_map/all_gather | solution.py:106
  272.7 4.1 fusion.40
  276.8 47.6 %all-gather.5.cloned.1.call-done = bf16[896,2432]{1,0:T(8,128)(2,1)} async-done(((bf16[56,2432]{1,0:T(8,128)(2,1)}), bf16[896,2432]{1,0:T(8,128)(2,1)}) %all-gather.5.cloned.1.call-update) | async-done | bytes 4358160 | tf_op jit(solution)/shard_map/all_gather | solution.py:105
  324.5 4.2 multiply_convert_fusion.1
  330.1 1.6 copy-done.8
  331.6 2.0 fusion.50
  333.7 4.3 fusion.53
  338.0 17.0 %all-reduce.20.cloned.1.call-done = bf16[2,64,896]{2,1,0:T(8,128)(2,1)} async-done(((bf16[2,64,896]{2,1,0:T(8,128)(2,1)}), bf16[2,64,896]{2,1,0:T(8,128)(2,1)}) %all-reduce.20.cloned.1.call-update) | async-done | bytes 229392 | tf_op jit(solution)/shard_map/psum | solution.py:212
  355.1 1.7 fusion.78
  356.8 1.3 convolution_convert_fusion.1
  359.3 18.6 %while.29 = (s32[]{:T(128)}, f32[2,1,448,64]{2,3,0,1:T(8,128)S(1)}, f32[2,2,1,512,128]{3,4,1,2,0:T(8,128)}, s32[2]{0:T(128)}, s32[2,1024]{1,0:T(2,128)S(1)}, /*i...) while((s32[]{:T(128)}, f32[2,1,448,64]{2,3,0,1:T(8,128)S(1)}, ...), condition=%wide.region_12.13_spmd.clone, body=%wide.region_11.12_spmd.clone.sunk | while | flops 297639936 | bytes 19564860 | solution.py:156
  362.2 1.5 bitcast_select_fusion.2
  363.7 1.4 fusion.171
  365.1 1.3 fusion.172
  371.5 1.5 bitcast_select_fusion.2
  373.0 1.4 fusion.171
  374.4 1.3 fusion.172
  379.9 2.3 copy.113
  382.2 1.3 pad_maximum_fusion
  387.5 87.8 %all-reduce.22.cloned.1.call-done = f32[2,1,1024,128]{3,0,1,2:T(2,128)} async-done(((f32[2,1,1024,128]{3,0,1,2:T(2,128)}), f32[2,1,1024,128]{3,0,1,2:T(2,128)}) %all-reduce.22.cloned.1.call-update) | async-done | bytes 1048592
  481.0 1.7 convolution_bitcast_fusion.6
  482.9 1.9 convolution_bitcast_fusion.5
  484.9 4.7 convolution_bitcast_fusion.4
  490.7 4.7 convolution_bitcast_fusion.3
  496.5 4.8 convolution_bitcast_fusion.2
  505.9 61.2 %all-reduce.10 = (f32[896]{0:T(1024)S(1)}, f32[896]{0:T(1024)S(1)}, f32[448]{0:T(512)}, f32[64]{0:T(128)}, f32[64]{0:T(128)}) all-reduce(f32[896]{0:T(1024)S(1)} %get-tuple-element.271, f32[896]{0:T(1024)S(1)} %copy-done.36, f32[448]{0:T(512)S(1)} %reduce_sum.123, ...), channel_id=4, replica_groups=mesh['ctx'=16,'tp'=2] {'ctx'}, use_global_device_ids=true, to_apply=%region_17.18.clone | all-reduce | flops 2368 | bytes 18944
  568.3 2.2 fusion.73
  570.5 22.7 %reduce-scatter.24.cloned.1.call-done = f32[56,64]{1,0:T(8,128)} async-done(((f32[896,64]{1,0:T(8,128)}), f32[56,64]{1,0:T(8,128)}) %reduce-scatter.24.cloned.1.call-update) | async-done | bytes 14352
  593.2 64.1 %reduce-scatter.18.cloned.1.call-done = f32[56,448]{1,0:T(8,128)} async-done(((f32[896,448]{1,0:T(8,128)}), f32[56,448]{1,0:T(8,128)}) %reduce-scatter.18.cloned.1.call-update) | async-done | bytes 100368 | tf_op jit(solution)/shard_map/reduce_scatter | solution.py:296
  657.4 64.0 %reduce-scatter.20.cloned.1.call-done = f32[448,56]{0,1:T(8,128)} async-done(((f32[448,896]{0,1:T(8,128)}), f32[448,56]{0,1:T(8,128)}) %reduce-scatter.20.cloned.1.call-update) | async-done | bytes 100368 | tf_op jit(solution)/shard_map/reduce_scatter | solution.py:299
  721.4 113.8 %reduce-scatter.26.cloned.1.call-done = f32[56,2432]{1,0:T(8,128)} async-done(((f32[896,2432]{1,0:T(8,128)}), f32[56,2432]{1,0:T(8,128)}) %reduce-scatter.26.cloned.1.call-update) | async-done | bytes 544784
  835.2 113.9 %reduce-scatter.28.cloned.1.call-done = f32[56,2432]{1,0:T(8,128)} async-done(((f32[896,2432]{1,0:T(8,128)}), f32[56,2432]{1,0:T(8,128)}) %reduce-scatter.28.cloned.1.call-update) | async-done | bytes 544784
  949.1 114.0 %reduce-scatter.30.cloned.1.call-done = f32[2432,56]{0,1:T(8,128)} async-done(((f32[2432,896]{0,1:T(8,128)}), f32[2432,56]{0,1:T(8,128)}) %reduce-scatter.30.cloned.1.call-update) | async-done | bytes 544784
  (248 shorter events, 53.2 us)
Async XLA Ops:
  8.0 182.0 %all-reduce.18.cloned.1.call-start = ((), (), s32[]{:S(2)}) async-start(), calls=%async_computation.7 | async-start | bytes 458752 | tf_op jit(solution)/shard_map/psum | solution.py:196
  47.8 61.3 %copy-start.32 = (f32[2,64]{1,0:T(2,128)}, f32[2,64]{1,0:T(2,128)S(1)}, u32[]{:S(2)}) copy-start(f32[2,64]{1,0:T(2,128)S(1)} %add_rsqrt_fusion.1) | copy-start | bytes 1540
  47.8 22.8 %copy-start.41 = (s32[2,32]{1,0:T(2,128)S(1)}, s32[2,32]{1,0:T(2,128)}, u32[]{:S(2)}) copy-start(s32[2,32]{1,0:T(2,128)} %param.21) | copy-start | bytes 772
  47.8 23.1 %copy-start.37 = (bf16[56,64]{1,0:T(8,128)(2,1)S(1)}, bf16[56,64]{1,0:T(8,128)(2,1)}, u32[]{:S(2)}) copy-start(bf16[56,64]{1,0:T(8,128)(2,1)} %param.26) | copy-start | bytes 21508
  68.2 22.2 %copy-start.42 = (bf16[64]{0:T(256)(128)(2,1)S(1)}, bf16[64]{0:T(256)(128)(2,1)}, u32[]{:S(2)}) copy-start(bf16[64]{0:T(256)(128)(2,1)} %param.29) | copy-start | bytes 388
  68.2 22.5 %copy-start.38 = (bf16[56,64]{1,0:T(8,128)(2,1)S(1)}, bf16[56,64]{1,0:T(8,128)(2,1)}, u32[]{:S(2)}) copy-start(bf16[56,64]{1,0:T(8,128)(2,1)} %param.25) | copy-start | bytes 21508
  68.2 40.6 %copy-start.43 = (bf16[64]{0:T(256)(128)(2,1)S(1)}, bf16[64]{0:T(256)(128)(2,1)}, u32[]{:S(2)}) copy-start(bf16[64]{0:T(256)(128)(2,1)} %param.28) | copy-start | bytes 388
  68.2 40.6 %copy-start = (bf16[2,64,896]{2,1,0:T(8,128)(2,1)S(1)}, bf16[2,64,896]{2,1,0:T(8,128)(2,1)}, u32[]{:S(2)}) copy-start(bf16[2,64,896]{2,1,0:T(8,128)(2,1)} %param.19) | copy-start | bytes 688132
  90.4 20.0 %copy-start.26 = (bf16[896,64]{1,0:T(8,128)(2,1)}, bf16[896,64]{1,0:T(8,128)(2,1)S(1)}, u32[]{:S(2)}) copy-start(bf16[896,64]{1,0:T(8,128)(2,1)S(1)} %all_gather.33) | copy-start | bytes 344068
  108.7 1.6 copy-start.24
  134.7 12.3 %copy-start.31 = (bf16[448,56]{0,1:T(8,128)(2,1)S(1)}, bf16[448,56]{0,1:T(8,128)(2,1)}, u32[]{:S(2)}) copy-start(bf16[448,56]{0,1:T(8,128)(2,1)} %param.30) | copy-start | bytes 150532
  147.0 21.2 %copy-start.20 = (bf16[2,64,448]{2,1,0:T(8,128)(2,1)}, bf16[2,64,448]{2,1,0:T(8,128)(2,1)S(1)}, u32[]{:S(2)}) copy-start(bf16[2,64,448]{2,1,0:T(8,128)(2,1)S(1)} %reshape_transpose_reshape.7) | copy-start | bytes 344068
  168.2 52.7 %copy-start.11 = (bf16[2,64,896]{2,1,0:T(8,128)(2,1)S(1)}, bf16[2,64,896]{2,1,0:T(8,128)(2,1)}, u32[]{:S(2)}) copy-start(bf16[2,64,896]{2,1,0:T(8,128)(2,1)} %param.20) | copy-start | bytes 688132
  168.2 52.7 %all-gather.9.cloned.1.call-start = ((), (), s32[]{:S(2)}) async-start(), calls=%async_computation.10 | async-start | bytes 4630528 | tf_op jit(solution)/shard_map/all_gather | solution.py:107
  168.8 103.9 %all-gather.7.cloned.1.call-start = ((), (), s32[]{:S(2)}) async-start(), calls=%async_computation.9 | async-start | bytes 4630528 | tf_op jit(solution)/shard_map/all_gather | solution.py:106
  169.4 155.1 %all-gather.5.cloned.1.call-start = ((), (), s32[]{:S(2)}) async-start(), calls=%async_computation.8 | async-start | bytes 4630528 | tf_op jit(solution)/shard_map/all_gather | solution.py:105
  170.0 185.1 %all-reduce.20.cloned.1.call-start = ((), (), s32[]{:S(2)}) async-start(), calls=%async_computation.11 | async-start | bytes 458752 | tf_op jit(solution)/shard_map/psum | solution.py:212
  170.3 186.5 %copy-start.29 = (f32[896]{0:T(1024)}, f32[896]{0:T(1024)S(1)}, u32[]{:S(2)}) copy-start(f32[896]{0:T(1024)S(1)} %convert_element_type.166) | copy-start | bytes 10756
  191.1 165.7 %copy-start.34 = (f32[2,64]{1,0:T(2,128)}, f32[2,64]{1,0:T(2,128)S(1)}, u32[]{:S(2)}) copy-start(f32[2,64]{1,0:T(2,128)S(1)} %add_rsqrt_fusion) | copy-start | bytes 1540
  192.2 132.3 %copy-start.4 = (bf16[2,64,896]{2,1,0:T(8,128)(2,1)}, bf16[2,64,896]{2,1,0:T(8,128)(2,1)S(1)}, u32[]{:S(2)}) copy-start(bf16[2,64,896]{2,1,0:T(8,128)(2,1)S(1)} %multiply_convert_fusion.3) | copy-start | bytes 688132
  324.5 4.3 copy-start.1
  328.7 5.0 copy-start.13
  328.7 2.9 copy-start.8
  333.7 141.7 %all-reduce.22.cloned.1.call-start = ((), (), s32[]{:S(2)}) async-start(), calls=%async_computation.14 | async-start | bytes 2097152
  333.7 21.3 %copy-start.6 = (bf16[2,64,896]{2,1,0:T(8,128)(2,1)S(1)}, bf16[2,64,896]{2,1,0:T(8,128)(2,1)}, u32[]{:S(2)}) copy-start(bf16[2,64,896]{2,1,0:T(8,128)(2,1)} %all-reduce.18.cloned.1.call-done) | copy-start | bytes 688132
  356.8 2.0 copy-start.39
  382.2 122.6 %all-reduce.24.cloned.1.call-start = ((), (), s32[]{:S(2)}) async-start(), calls=%async_computation.20 | async-start | bytes 917504 | tf_op jit(solution)/shard_map/psum | solution.py:204
  383.7 3.3 copy-start.3
  385.9 90.9 %copy-start.25 = (bf16[896,64]{1,0:T(8,128)(2,1)S(1)}, bf16[896,64]{1,0:T(8,128)(2,1)}, u32[]{:S(2)}) copy-start(bf16[896,64]{1,0:T(8,128)(2,1)} %copy-done.24) | copy-start | bytes 344068
  387.5 89.6 %copy-start.27 = (bf16[896,64]{1,0:T(8,128)(2,1)S(1)}, bf16[896,64]{1,0:T(8,128)(2,1)}, u32[]{:S(2)}) copy-start(bf16[896,64]{1,0:T(8,128)(2,1)} %copy-done.26) | copy-start | bytes 344068
  387.5 90.6 %copy-start.33 = (f32[2,64]{1,0:T(2,128)S(1)}, f32[2,64]{1,0:T(2,128)}, u32[]{:S(2)}) copy-start(f32[2,64]{1,0:T(2,128)} %copy-done.32) | copy-start | bytes 1540
  478.1 92.4 %reduce-scatter.22.cloned.1.call-start = ((), (), s32[]{:S(2)}) async-start(), calls=%async_computation.15 | async-start | bytes 487424
  479.4 113.8 %reduce-scatter.24.cloned.1.call-start = ((), (), s32[]{:S(2)}) async-start(), calls=%async_computation.16 | async-start | bytes 487424
  480.9 2.0 copy-start.7
  480.9 2.0 copy-start.12
  480.9 2.0 copy-start.19
  480.9 2.0 copy-start.21
  480.9 2.0 copy-start.30
  480.9 1.9 copy-start.35
  481.0 1.9 copy-start.40
  481.0 176.4 %reduce-scatter.18.cloned.1.call-start = ((), (), s32[]{:S(2)}) async-start(), calls=%async_computation.12 | async-start | bytes 1949696 | tf_op jit(solution)/shard_map/reduce_scatter | solution.py:296
  482.8 2.1 copy-start.5
  482.8 2.1 copy-start.18
  482.8 238.6 %reduce-scatter.20.cloned.1.call-start = ((), (), s32[]{:S(2)}) async-start(), calls=%async_computation.13 | async-start | bytes 1949696 | tf_op jit(solution)/shard_map/reduce_scatter | solution.py:299
  484.8 350.4 %reduce-scatter.26.cloned.1.call-start = ((), (), s32[]{:S(2)}) async-start(), calls=%async_computation.17 | async-start | bytes 9261056
  489.6 459.5 %reduce-scatter.28.cloned.1.call-start = ((), (), s32[]{:S(2)}) async-start(), calls=%async_computation.18 | async-start | bytes 9261056
  495.4 567.7 %reduce-scatter.30.cloned.1.call-start = ((), (), s32[]{:S(2)}) async-start(), calls=%async_computation.19 | async-start | bytes 9261056
  501.3 4.6 copy-start.36
  (12 other events, 13.4 us)
Sparse Core Ops, SparseCore 0:
  168.3 21.6 all-reduce.17
  333.8 21.2 all-reduce.19
  478.2 26.5 all-reduce.23
Sparse Core Ops, SparseCore 1:
  170.8 50.0 all-gather.8
  222.9 49.7 all-gather.6
  274.7 49.7 all-gather.4
  382.3 93.0 all-reduce.21
  483.3 52.7 reduce-scatter.21
  540.6 52.6 reduce-scatter.23
  597.8 59.5 reduce-scatter.17
  662.0 59.4 reduce-scatter.19
  726.4 108.7 reduce-scatter.25
  840.3 108.7 reduce-scatter.27
  954.1 108.9 reduce-scatter.29
where the time goes:
time: 1070 us
  waiting for transfers between devices  742 us (69%)
  blocking collectives  194 us (18%)
  matrix products  61.9 us (6%)
  local copies, waits for them, and re-layouts  31.2 us (3%)
  other arithmetic  18.9 us (2%)
  between operations  18.4 us (2%)
    unnamed x20, waiting for transfers between devices  454 us
    unnamed x2, blocking collectives  96.1 us
    reduce_scatter x1, waiting for transfers between devices, local(): lax.psum_scatter(d_wquery, 'ctx', scatter_dimension=0, tiled=True)  64.1 us
    reduce_scatter x1, waiting for transfers between devices, local(): lax.psum_scatter(d_wout, 'ctx', scatter_dimension=1, tiled=True)  64 us
    all_gather x1, waiting for transfers between devices, local(): lax.all_gather(w_gate, 'ctx', axis=0, tiled=True)  47.6 us
    all_gather x1, waiting for transfers between devices, local(): lax.all_gather(w_up, 'ctx', axis=0, tiled=True)  47.6 us
    all_gather x1, waiting for transfers between devices, local(): lax.all_gather(w_down, 'ctx', axis=1, tiled=True)  28.7 us
  transfers between devices with their start and end apart: 14, of which 13 were waited for; matrix products, arithmetic and copies ran while one was open for 4% of the time, Pallas kernels for 0%

commit v1 on v0

v1 whole, which is shorter than its diff:
```python
import jax
import jax.numpy as jnp
from jax import lax
from jax.sharding import PartitionSpec as P

HEADS = 14
KV_HEADS = 2
HEAD = 64


EPSILON = 1e-06
ROPE_BASE = 1000000.0


def rope_tables(positions, head_dim):
    halfway = head_dim // 2
    inverse = ROPE_BASE ** (-(jnp.arange(halfway, dtype=jnp.float32) * 2.0 / head_dim))
    angles = positions.astype(jnp.float32)[..., None] * inverse
    angles = jnp.concatenate([angles, angles], axis=-1)
    return (jnp.cos(angles), jnp.sin(angles))


def rotate(values, cosine, sine):
    halfway = values.shape[-1] // 2
    turned = jnp.concatenate([-values[..., halfway:], values[..., :halfway]], axis=-1)
    return values * cosine + turned * sine


def unrotate(grads, cosine, sine):
    halfway = grads.shape[-1] // 2
    moved = grads * sine
    back = jnp.concatenate([moved[..., halfway:], -moved[..., :halfway]], axis=-1)
    return grads * cosine + back


def norm_apply(values, gain):
    factor = lax.rsqrt(jnp.mean(values * values, axis=-1, keepdims=True) + EPSILON)
    return (values * factor * gain, factor)


def norm_back(values, factor, gain, grads):
    weighted = grads * gain
    inner = jnp.mean(weighted * values, axis=-1, keepdims=True)
    d_values = factor * weighted - values * factor * factor * factor * inner
    d_gain = jnp.sum(grads * values * factor, axis=0)
    return (d_values, d_gain)


def dot(left, right, left_dim, right_dim):
    return lax.dot_general(
        left, right, (((left_dim,), (right_dim,)), ((), ())), preferred_element_type=jnp.float32
    )


class Groups:
    def __init__(self, count):
        self.count = count
        self.low = min(4, count)
        self.high = count // self.low
        self.near = [[h * self.low + k for k in range(self.low)] for h in range(self.high)]
        self.far = [[h * self.low + k for h in range(self.high)] for k in range(self.low)]

    def far_pairs(self, flip):
        return [(i, (i // self.low ^ flip) * self.low + i % self.low) for i in range(self.count)]

    def gather_near(self, values):
        return lax.all_gather(values, "ctx", axis=0, tiled=True, axis_index_groups=self.near)

    def gather_far(self, values):
        return lax.all_gather(values, "ctx", axis=0, tiled=True, axis_index_groups=self.far)

    def swap_near(self, values):
        return lax.all_to_all(values, "ctx", 0, 0, tiled=True, axis_index_groups=self.near)

    def from_far(self, values):
        return jnp.stack(
            [values]
            + [lax.ppermute(values, "ctx", self.far_pairs(m)) for m in range(1, self.high)]
        )

    def sum_far(self, pieces):
        total = pieces[0].astype(jnp.float32)
        for m in range(1, self.high):
            total = total + lax.ppermute(pieces[m], "ctx", self.far_pairs(m)).astype(jnp.float32)
        return total


def sum_tp(values):
    other = lax.ppermute(values, "tp", [(0, 1), (1, 0)])
    return values.astype(jnp.float32) + other.astype(jnp.float32)


def local(
    tokens,
    cotangent,
    block_of,
    norm_gain,
    ffn_gain,
    w_query,
    w_key,
    w_value,
    b_query,
    b_key,
    b_value,
    w_out,
    w_gate,
    w_up,
    w_down,
):
    seqs, rows, width = tokens.shape
    count = seqs * rows
    block_len = rows // 2
    ctx = lax.axis_size("ctx")
    groups = Groups(ctx)
    low, high = groups.low, groups.high
    device = lax.axis_index("ctx")
    factor = HEAD ** (-0.5)
    heads = w_query.shape[1] // HEAD
    share = width // ctx
    units = w_gate.shape[1]
    part = -(-units // (low * 128)) * 128

    gains = jnp.stack([norm_gain, ffn_gain], axis=1)
    w_attn = jnp.concatenate(
        [w_query, w_key, w_value, w_out.T, jnp.pad(gains, ((0, 0), (0, 126)))], axis=1
    )
    w_attn = lax.all_gather(w_attn, "ctx", axis=0, tiled=True)
    query_width = heads * HEAD
    qkv_width = query_width + 2 * HEAD
    w_qkv = w_attn[:, :qkv_width]
    w_out_t = w_attn[:, qkv_width : qkv_width + query_width]
    gains = w_attn[:, qkv_width + query_width : qkv_width + query_width + 2].astype(jnp.float32).T
    gain_one, gain_two = gains[0], gains[1]

    def pieces(matrix):
        return jnp.pad(matrix, ((0, 0), (0, low * part - units))).reshape(share, low, part)

    w_ffn = jnp.concatenate([pieces(w_gate), pieces(w_up), pieces(w_down.T)], axis=2)
    w_ffn = groups.swap_near(w_ffn.transpose(1, 0, 2)).reshape(low * share, 3 * part)
    w_ffn = groups.gather_far(w_ffn)
    w_gate_up, w_down_t = w_ffn[:, : 2 * part], w_ffn[:, 2 * part :]

    grads_in = cotangent.reshape(count, width)
    grads_near = groups.gather_near(grads_in)

    offsets = jnp.arange(block_len, dtype=jnp.int32)
    own_blocks = lax.dynamic_slice_in_dim(block_of, device * 2, 2, 1)
    row_pos = (own_blocks[:, :, None] * block_len + offsets).reshape(seqs, rows)
    owners = (device // low ^ jnp.arange(high, dtype=jnp.int32))[:, None] * low + jnp.arange(
        low, dtype=jnp.int32
    )
    key_blocks = block_of.reshape(seqs, ctx, 2)[:, owners.reshape(-1)]
    key_pos = (key_blocks[..., None] * block_len + offsets).reshape(seqs, ctx * rows)
    cosine, sine = rope_tables(row_pos.reshape(count), HEAD)
    cosine, sine = cosine[:, None, :], sine[:, None, :]

    inputs = tokens.astype(jnp.float32).reshape(count, width)
    normed, scale_one = norm_apply(inputs, gain_one)
    normed_low = normed.astype(jnp.bfloat16)
    bias = jnp.concatenate([b_query, b_key, b_value]).astype(jnp.float32)
    lin = dot(normed_low, w_qkv, 1, 0) + bias
    rotated = rotate(
        lin[:, : query_width + HEAD].reshape(count, heads + 1, HEAD), cosine, sine
    ).astype(jnp.bfloat16)
    queries = rotated[:, :heads].reshape(seqs, rows * heads, HEAD)
    query_pos = jnp.repeat(row_pos, heads, axis=1)
    pair = jnp.concatenate(
        [rotated[:, heads], lin[:, query_width + HEAD :].astype(jnp.bfloat16)], axis=1
    )
    near_pairs = groups.gather_near(pair)
    pairs = (
        groups.from_far(near_pairs)
        .reshape(high, low, seqs, rows, 2 * HEAD)
        .transpose(2, 0, 1, 3, 4)
        .reshape(seqs, ctx * rows, 2 * HEAD)
    )
    key_count = ctx * rows
    span = min(1024, key_count)

    def over_keys(step, state):
        if key_count == span:
            return step(state, pairs, key_pos)

        def inner(carry, index):
            some = lax.dynamic_slice_in_dim(pairs, index * span, span, 1)
            some_pos = lax.dynamic_slice_in_dim(key_pos, index * span, span, 1)
            return step(carry, some, some_pos)

        return lax.scan(inner, state, jnp.arange(key_count // span, dtype=jnp.int32))

    def block_scores(some, some_pos):
        scores = (
            jnp.einsum("aqd,akd->aqk", queries, some[..., :HEAD], preferred_element_type=jnp.float32)
            * factor
        )
        allowed = some_pos[:, None, :] <= query_pos[:, :, None]
        return scores, allowed

    def forward_step(state, some, some_pos):
        best, totals, summed = state
        scores, allowed = block_scores(some, some_pos)
        newest = jnp.maximum(best, jnp.max(jnp.where(allowed, scores, -1e30), axis=-1))
        raised = jnp.where(allowed, jnp.exp(scores - newest[..., None]), 0.0)
        fading = jnp.exp(best - newest)
        totals = totals * fading + jnp.sum(raised, axis=-1)
        summed = summed * fading[..., None] + jnp.einsum(
            "aqk,akd->aqd",
            raised.astype(jnp.bfloat16),
            some[..., HEAD:],
            preferred_element_type=jnp.float32,
        )
        return (newest, totals, summed), None

    state = (
        jnp.full((seqs, rows * heads), -1e30, jnp.float32),
        jnp.zeros((seqs, rows * heads), jnp.float32),
        jnp.zeros((seqs, rows * heads, HEAD), jnp.float32),
    )
    (best, totals, summed), _ = over_keys(forward_step, state)
    out_rows = summed / totals[..., None]
    log_total = best + jnp.log(totals)
    out_flat = out_rows.astype(jnp.bfloat16).reshape(count, query_width)
    attention = sum_tp(dot(out_flat, w_out_t, 1, 1).astype(jnp.bfloat16))
    hidden = inputs + attention

    normed_two, scale_two = norm_apply(hidden, gain_two)
    near_two = groups.gather_near(normed_two.astype(jnp.bfloat16))
    gate_up = dot(near_two, w_gate_up, 1, 0)
    gate, up_values = gate_up[:, :part], gate_up[:, part:]
    sigma = jax.nn.sigmoid(gate)
    active = (gate * sigma * up_values).astype(jnp.bfloat16)
    d_active = dot(grads_near, w_down_t, 1, 0)
    d_gate = (d_active * up_values * sigma * (1.0 + gate * (1.0 - sigma))).astype(jnp.bfloat16)
    d_up = (d_active * gate * sigma).astype(jnp.bfloat16)
    d_gate_up = jnp.concatenate([d_gate, d_up], axis=1)
    d_near = dot(d_gate_up, w_gate_up, 1, 1).astype(jnp.bfloat16)

    def home(values):
        swapped = groups.swap_near(values.reshape(low, count, width))
        return sum_tp(jnp.sum(swapped.astype(jnp.float32), axis=0).astype(jnp.bfloat16))

    d_normed_two = home(d_near)
    mixed = (hidden + home(dot(active, w_down_t, 1, 1).astype(jnp.bfloat16))).astype(jnp.bfloat16)
    d_w_ffn = jnp.concatenate(
        [dot(near_two, d_gate_up, 0, 0), dot(grads_near, active, 0, 0)], axis=1
    ).astype(jnp.bfloat16)
    d_w_ffn = lax.psum_scatter(
        d_w_ffn, "ctx", scatter_dimension=0, tiled=True, axis_index_groups=groups.far
    )
    d_w_ffn = groups.swap_near(d_w_ffn.reshape(low, share, 3 * part))
    d_w_ffn = d_w_ffn.transpose(1, 0, 2).astype(jnp.float32)

    def whole(index):
        some = d_w_ffn[:, :, index * part : (index + 1) * part]
        return some.reshape(share, low * part)[:, :units]

    g_gate, g_up, g_down = whole(0), whole(1), whole(2).T

    d_hidden_norm, d_gain_two = norm_back(hidden, scale_two, gain_two, d_normed_two)
    d_hidden = grads_in.astype(jnp.float32) + d_hidden_norm
    d_hidden_low = d_hidden.astype(jnp.bfloat16)
    d_out = dot(d_hidden_low, w_out_t, 1, 0).astype(jnp.bfloat16).reshape(seqs, rows * heads, HEAD)
    row_dots = jnp.sum(d_out.astype(jnp.float32) * out_rows, axis=-1)

    def backward_step(carry, some, some_pos):
        scores, allowed = block_scores(some, some_pos)
        chances = jnp.where(allowed, jnp.exp(scores - log_total[..., None]), 0.0)
        d_chances = jnp.einsum(
            "aqd,akd->aqk", d_out, some[..., HEAD:], preferred_element_type=jnp.float32
        )
        d_scores = (chances * (d_chances - row_dots[..., None])).astype(jnp.bfloat16)
        carry = (
            carry
            + jnp.einsum(
                "aqk,akd->aqd", d_scores, some[..., :HEAD], preferred_element_type=jnp.float32
            )
            * factor
        )
        d_keys = (
            jnp.einsum("aqk,aqd->akd", d_scores, queries, preferred_element_type=jnp.float32)
            * factor
        )
        d_values = jnp.einsum(
            "aqk,aqd->akd",
            chances.astype(jnp.bfloat16),
            d_out,
            preferred_element_type=jnp.float32,
        )
        return carry, jnp.concatenate([d_keys, d_values], axis=-1).astype(jnp.bfloat16)

    d_query, d_pairs = over_keys(
        backward_step, jnp.zeros((seqs, rows * heads, HEAD), jnp.float32)
    )
    if key_count != span:
        d_pairs = jnp.moveaxis(d_pairs, 0, 1)
    d_pairs = (
        d_pairs.reshape(seqs, high, low, rows, 2 * HEAD)
        .transpose(1, 2, 0, 3, 4)
        .reshape(high, low, count, 2 * HEAD)
    )
    near_sums = groups.sum_far([d_pairs[m] for m in range(high)]).astype(jnp.bfloat16)
    pair_grads = jnp.sum(groups.swap_near(near_sums).astype(jnp.float32), axis=0)
    d_rotated = jnp.concatenate(
        [d_query.reshape(count, heads, HEAD), pair_grads[:, None, :HEAD]], axis=1
    )
    d_lin = jnp.concatenate(
        [
            unrotate(d_rotated, cosine, sine).reshape(count, query_width + HEAD),
            pair_grads[:, HEAD:],
        ],
        axis=1,
    ).astype(jnp.bfloat16)
    d_normed = sum_tp(dot(d_lin, w_qkv, 1, 1).astype(jnp.bfloat16))
    d_input_norm, d_gain_one = norm_back(inputs, scale_one, gain_one, d_normed)
    tokens_grad = (d_hidden + d_input_norm).astype(jnp.bfloat16)
    d_w_attn = jnp.concatenate(
        [dot(normed_low, d_lin, 0, 0), dot(d_hidden_low, out_flat, 0, 0)], axis=1
    ).astype(jnp.bfloat16)
    d_w_attn = lax.psum_scatter(d_w_attn, "ctx", scatter_dimension=0, tiled=True).astype(
        jnp.float32
    )
    sums = jnp.concatenate([d_gain_one, d_gain_two, jnp.sum(d_lin.astype(jnp.float32), axis=0)])
    sums = jnp.sum(groups.gather_near(sums[None]), axis=0)
    sums = jnp.sum(groups.from_far(sums), axis=0)
    g_one = lax.dynamic_slice_in_dim(sums, device * share, share, 0)
    g_two = lax.dynamic_slice_in_dim(sums, width + device * share, share, 0)
    g_bias = sums[2 * width :]
    return (
        mixed.reshape(tokens.shape),
        tokens_grad.reshape(tokens.shape),
        g_one,
        g_two,
        d_w_attn[:, :query_width],
        d_w_attn[:, query_width : query_width + HEAD],
        d_w_attn[:, query_width + HEAD : qkv_width],
        g_bias[:query_width],
        g_bias[query_width : query_width + HEAD],
        g_bias[query_width + HEAD :],
        d_w_attn[:, qkv_width:].T,
        g_gate,
        g_up,
        g_down,
    )


def solution(mesh):
    placed = (
        P(None, "ctx", None),
        P(None, "ctx", None),
        P(),
        P("ctx"),
        P("ctx"),
        P("ctx", "tp"),
        P("ctx", "tp"),
        P("ctx", "tp"),
        P("tp"),
        P("tp"),
        P("tp"),
        P("tp", "ctx"),
        P("ctx", "tp"),
        P("ctx", "tp"),
        P("tp", "ctx"),
    )
    return jax.shard_map(
        local,
        mesh=mesh,
        in_specs=placed,
        out_specs=(
            P(None, "ctx", None),
            P(None, "ctx", None),
            P("ctx"),
            P("ctx"),
            P("ctx", "tp"),
            P("ctx", "tp"),
            P("ctx", "tp"),
            P("tp"),
            P("tp"),
            P("tp"),
            P("tp", "ctx"),
            P("ctx", "tp"),
            P("ctx", "tp"),
            P("tp", "ctx"),
        ),
        check_vma=False,
    )
```

time: 1070 us -> 308 us (0.29)
  waiting for transfers between devices: 742 us -> 142 us
  blocking collectives: 194 us -> 33.8 us
  starting transfers between devices: 1 us -> 37.9 us
  matrix products: 61.9 us -> 34.5 us
    unnamed x20 -> x5, waiting for transfers between devices: 454 us -> 27.7 us
    reduce_scatter x2 -> x1, waiting for transfers between devices: 128 us -> 0.01 us  [local(): lax.psum_scatter(d_w_ffn, 'ctx', scatter_dimension=0, tiled=True, axis_in...]
    all_gather x3 -> x2, waiting for transfers between devices: 124 us -> 37.2 us  [the longest x1 23.5 us: local(): w_attn = lax.all_gather(w_attn, 'ctx', axis=0, tiled=True)]
    unnamed x2 -> x1, blocking collectives: 96.1 us -> 10.5 us
    all_gather x5 -> x3, blocking collectives: 98.1 us -> 23.3 us  [gather_near(): lax.all_gather(values, 'ctx', axis=0, tiled=True, axis_index_groups=self....]
    ppermute x0 -> x13, waiting for transfers between devices: none -> 41.1 us  [the longest x6 25.2 us: from_far(): lax.ppermute(values, 'ctx', self.far_pairs(m))]
    all_to_all x0 -> x5, waiting for transfers between devices: none -> 36 us  [swap_near(): lax.all_to_all(values, 'ctx', 0, 0, tiled=True, axis_index_groups=self.near)]
    psum x3 -> x0, waiting for transfers between devices: 35.8 us -> none  [the longest x1 17.5 us: local(): lax.psum(matmul(out_flat, full_out).astype(jnp.bfloat16), 'tp')]
  transfers between devices with their start and end apart: 14 -> 22, of which waited for: 13 -> 15; matrix products, arithmetic and copies ran while one was open for 4% -> 19% of each run, Pallas kernels for 0% -> 0%
where the time goes in v1:
time: 308 us; the launch traced here: 306 us
  waiting for transfers between devices  142 us (46%)
  starting transfers between devices  37.9 us (12%)
  matrix products  34.5 us (11%)
  blocking collectives  33.8 us (11%)
  local copies, waits for them, and re-layouts  28.6 us (9%)
  between operations  15.4 us (5%)
  other arithmetic  14.3 us (5%)
    all_to_all x5, waiting for transfers between devices, swap_near(): lax.all_to_all(values, 'ctx', 0, 0, tiled=True, axis_index_groups=self.near)  36 us
    unnamed x5, waiting for transfers between devices  27.7 us
    ppermute x6, waiting for transfers between devices, from_far(): lax.ppermute(values, 'ctx', self.far_pairs(m))  25.2 us
    dot_general x12, matrix products, dot(): lax.dot_general(left, right, (((left_dim,), (right_dim,)), ((), ())), pre...  24.1 us
    all_gather x1, waiting for transfers between devices, local(): w_attn = lax.all_gather(w_attn, 'ctx', axis=0, tiled=True)  23.5 us
    all_gather x3, blocking collectives, gather_near(): lax.all_gather(values, 'ctx', axis=0, tiled=True, axis_index_groups=self....  23.3 us
    all_to_all x5, starting transfers between devices, swap_near(): lax.all_to_all(values, 'ctx', 0, 0, tiled=True, axis_index_groups=self.near)  18.3 us
    all_gather x1, waiting for transfers between devices, gather_far(): lax.all_gather(values, 'ctx', axis=0, tiled=True, axis_index_groups=self....  13.7 us
  transfers between devices with their start and end apart: 22, of which 15 were waited for; matrix products, arithmetic and copies ran while one was open for 19% of the time, Pallas kernels for 0%

profile of v1, /device:TPU:0, one launch (start us, length us, event | category | flops | bytes accessed | tf_op | source)
XLA Modules:
  0.0 306.5 jit_solution(16576593932167344615)
XLA Ops:
  8.1 1.6 concatenate.64
  13.4 4.2 %all-to-all-start = ((bf16[4,56,1920]{2,1,0:T(8,128)(2,1)}), bf16[4,56,1920]{2,1,0:T(8,128)(2,1)S(1)}, u32[]{:S(2)}, u32[]{:S(2)}) async-start(bf16[4,56,1920]{2,1,0:T(8,128)(2,1)} %copy.150), calls=%async_computation | async-start | bytes 1720320 | tf_op jit(solution)/shard_map/all_to_all | solution.py:73
  20.1 11.4 %all-to-all-done = bf16[4,56,1920]{2,1,0:T(8,128)(2,1)S(1)} async-done(((bf16[4,56,1920]{2,1,0:T(8,128)(2,1)}), bf16[4,56,1920]{2,1,0:T(8,128)(2,1)S(1)}, u32[]{:S(2)}, u32[]{:S(2)}) %all-to-all-start) | async-done | bytes 860192 | tf_op jit(solution)/shard_map/all_to_all | solution.py:73
  32.5 23.5 %all-gather.4.cloned.1.call-done = bf16[896,1152]{1,0:T(8,128)(2,1)} async-done(((bf16[56,1152]{1,0:T(8,128)(2,1)}), bf16[896,1152]{1,0:T(8,128)(2,1)}) %all-gather.4.cloned.1.call-update) | async-done | bytes 2064400 | tf_op jit(solution)/shard_map/all_gather | solution.py:127
  57.6 1.9 convolution_add_fusion
  59.7 5.4 %all_gather.19 = bf16[512,128]{0,1:T(8,128)(2,1)S(1)} all-gather(bf16[128,128]{0,1:T(8,128)(2,1)S(1)} %pad_maximum_fusion.10), channel_id=1, replica_groups={{0,2,4,6},{8,10,12,14},{16,18,20,22},{24,26,28,30},{1,3,5,7},{9,11,13,1..., dimensions={0}, use_global_device_ids=true | all-gather | bytes 163840 | tf_op jit(solution)/shard_map/all_gather | solution.py:67
  65.1 2.1 collective-permute-start.2
  67.2 2.3 collective-permute-start
  70.0 5.8 %collective-permute-done.2 = bf16[512,128]{0,1:T(8,128)(2,1)S(1)} collective-permute-done((bf16[512,128]{0,1:T(8,128)(2,1)S(1)}, bf16[512,128]{0,1:T(8,128)(2,1)S(1)}, u32[]{:S(2)}, u32[]{:S(2)}) %collective-permute-start.2) | collective-permute-done | bytes 131104 | tf_op jit(solution)/shard_map/ppermute | solution.py:78
  75.9 18.2 %collective-permute-done.1 = bf16[512,128]{0,1:T(8,128)(2,1)S(1)} collective-permute-done((bf16[512,128]{0,1:T(8,128)(2,1)S(1)}, bf16[512,128]{0,1:T(8,128)(2,1)S(1)}, u32[]{:S(2)}, u32[]{:S(2)}) %collective-permute-start.1) | collective-permute-done | bytes 131104 | tf_op jit(solution)/shard_map/ppermute | solution.py:78
  97.5 2.1 fusion.77
  100.0 1.8 convolution_convert_fusion.6
  101.8 1.5 collective-permute-start.3
  103.3 7.6 %all_gather.22 = bf16[512,896]{1,0:T(8,128)(2,1)S(1)} all-gather(bf16[128,896]{1,0:T(8,128)(2,1)S(1)} %bitcast.123), channel_id=1, replica_groups={{0,2,4,6},{8,10,12,14},{16,18,20,22},{24,26,28,30},{1,3,5,7},{9,11,13,1..., dimensions={0}, use_global_device_ids=true | all-gather | bytes 1146880 | tf_op jit(solution)/shard_map/all_gather | solution.py:67
  111.3 10.2 %all_gather.20 = bf16[512,896]{1,0:T(8,128)(2,1)S(1)} all-gather(bf16[128,896]{1,0:T(8,128)(2,1)S(1)} %multiply_convert_fusion.4), channel_id=1, replica_groups={{0,2,4,6},{8,10,12,14},{16,18,20,22},{24,26,28,30},{1,3,5,7},{9,11,13,1..., dimensions={0}, use_global_device_ids=true | all-gather | bytes 1146880 | tf_op jit(solution)/shard_map/all_gather | solution.py:67
  121.5 13.7 %all-gather.6.cloned.1.call-done = bf16[896,1920]{1,0:T(8,128)(2,1)} async-done(((bf16[224,1920]{1,0:T(8,128)(2,1)}), bf16[896,1920]{1,0:T(8,128)(2,1)}) %all-gather.6.cloned.1.call-update) | async-done | bytes 3440656 | tf_op jit(solution)/shard_map/all_gather | solution.py:70
  135.2 3.2 %fusion.6 = f32[512,1280]{1,0:T(8,128)S(1)} fusion(bf16[512,896]{1,0:T(8,128)(2,1)S(1)} %all_gather.20, bf16[896,1920]{1,0:T(8,128)(2,1)} %all-gather.6.cloned.1.call-done), kind=kOutput, calls=%fused_computation.13 | convolution fusion | flops 1174405120 | bytes 5832704 | tf_op jit(solution)/shard_map/dot_general | solution.py:50
  138.4 2.5 multiply_convert_fusion.2
  143.6 2.0 pad_maximum_fusion
  146.7 4.4 %fusion.12 = bf16[512,896]{1,0:T(8,128)(2,1)} fusion(bf16[896,1920]{1,0:T(8,128)(2,1)} %all-gather.6.cloned.1.call-done, bf16[512,640]{1,0:T(8,128)(2,1)} %copy-done.31, bf16[512,640]{1,0:T(8,128)(2,1)S(1)} %copy-done.30), kind=kOutput, calls=%fused_computation.22 | convolution fusion | flops 1177485312 | bytes 4521984 | tf_op jit(solution)/shard_map/dot_general | solution.py:50
  151.1 3.5 %all-to-all-start.2 = ((bf16[4,128,896]{2,1,0:T(8,128)(2,1)}), bf16[4,128,896]{2,1,0:T(8,128)(2,1)S(1)}, u32[]{:S(2)}, u32[]{:S(2)}) async-start(bf16[4,128,896]{2,1,0:T(8,128)(2,1)} %bitcast.22), calls=%async_computation.2 | async-start | bytes 1835008 | tf_op jit(solution)/shard_map/all_to_all | solution.py:73
  154.6 3.1 %convolution_convert_fusion.3 = bf16[512,896]{1,0:T(8,128)(2,1)} fusion(bf16[512,640]{1,0:T(8,128)(2,1)S(1)} %copy-done.28, bf16[896,1920]{1,0:T(8,128)(2,1)} %all-gather.6.cloned.1.call-done), kind=kOutput, calls=%fused_computation.21 | convolution fusion | flops 587661312 | bytes 2719744 | tf_op jit(solution)/shard_map/dot_general | solution.py:50
  157.8 9.9 %all-to-all-done.2 = bf16[4,128,896]{2,1,0:T(8,128)(2,1)S(1)} async-done(((bf16[4,128,896]{2,1,0:T(8,128)(2,1)}), bf16[4,128,896]{2,1,0:T(8,128)(2,1)S(1)}, u32[]{:S(2)}, u32[]{:S(2)}) %all-to-all-start.2) | async-done | bytes 917536 | tf_op jit(solution)/shard_map/all_to_all | solution.py:73
  167.7 3.7 %all-to-all-start.1 = ((bf16[4,128,896]{2,1,0:T(8,128)(2,1)}), bf16[4,128,896]{2,1,0:T(8,128)(2,1)S(1)}, u32[]{:S(2)}, u32[]{:S(2)}) async-start(bf16[4,128,896]{2,1,0:T(8,128)(2,1)} %bitcast.122), calls=%async_computation.1 | async-start | bytes 1835008 | tf_op jit(solution)/shard_map/all_to_all | solution.py:73
  171.6 1.5 collective-permute-start.5
  173.1 11.1 %all-to-all-done.1 = bf16[4,128,896]{2,1,0:T(8,128)(2,1)S(1)} async-done(((bf16[4,128,896]{2,1,0:T(8,128)(2,1)}), bf16[4,128,896]{2,1,0:T(8,128)(2,1)S(1)}, u32[]{:S(2)}, u32[]{:S(2)}) %all-to-all-start.1) | async-done | bytes 917536 | tf_op jit(solution)/shard_map/all_to_all | solution.py:73
  184.3 1.5 collective-permute-start.4
  186.6 5.0 %collective-permute-done.4 = bf16[128,896]{1,0:T(8,128)(2,1)S(1)} collective-permute-done((bf16[128,896]{1,0:T(8,128)(2,1)S(1)}, bf16[128,896]{1,0:T(8,128)(2,1)S(1)}, u32[]{:S(2)}, u32[]{:S(2)}) %collective-permute-start.4) | collective-permute-done | bytes 229408 | tf_op jit(solution)/shard_map/ppermute | solution.py:89
  191.7 2.0 subtract_add_fusion
  193.7 2.2 convolution_convert_fusion.7
  196.3 3.1 %fusion.17 = bf16[2,1024,64]{1,2,0:T(8,128)(2,1)S(1)} fusion(bf16[2,448,64]{2,1,0:T(8,128)(2,1)S(1)} %reshape.350, f32[2,448,1024]{2,1,0:T(8,128)} %copy-done.1, f32[2,448]{1,0:T(2,128)S(1)} %copy-done.21, s32[2,448]{1,0:T(2,128)S(1)} %copy-done.17, s32[2,1024]{1,0:T(2,128)S(1)} %broadcast_add_fusion), kind=kOutput, calls=%fused_computation.33 | convolution fusion | flops 122159104 | bytes 4062208 | tf_op jit(solution)/shard_map/aqk,aqd->akd/dot_general | solution.py:283
  201.1 3.0 multiply_convert_fusion
  205.7 2.3 copy.158
  208.0 1.5 maximum_bitcast_fusion.2
  210.9 3.1 %collective-permute-start.6 = (bf16[4,128,128]{2,1,0:T(8,128)(2,1)S(1)}, bf16[4,128,128]{2,1,0:T(8,128)(2,1)S(1)}, u32[]{:S(2)}, u32[]{:S(2)}) collective-permute-start(bf16[4,128,128]{2,1,0:T(8,128)(2,1)S(1)} %bitcast.136), channel_id=1, source_target_pairs={{0,8},{2,10},{4,12},{6,14},{8,0},{10,2},{12,4},{14,6},{16,24},{18,... | collective-permute-start | bytes 393224 | tf_op jit(solution)/shard_map/ppermute | solution.py:84
  214.7 3.2 %collective-permute-done.8 = bf16[4,128,128]{2,1,0:T(8,128)(2,1)S(1)} collective-permute-done((bf16[4,128,128]{2,1,0:T(8,128)(2,1)S(1)}, bf16[4,128,128]{2,1,0:T(8,128)(2,1)S(1)}, u32[]{:S(2)}, u32[]{:S(2)}) %collective-permute-start.8) | collective-permute-done | bytes 131104 | tf_op jit(solution)/shard_map/ppermute | solution.py:84
  217.9 3.5 %collective-permute-done.7 = bf16[4,128,128]{2,1,0:T(8,128)(2,1)S(1)} collective-permute-done((bf16[4,128,128]{2,1,0:T(8,128)(2,1)S(1)}, bf16[4,128,128]{2,1,0:T(8,128)(2,1)S(1)}, u32[]{:S(2)}, u32[]{:S(2)}) %collective-permute-start.7) | collective-permute-done | bytes 131104 | tf_op jit(solution)/shard_map/ppermute | solution.py:84
  222.1 3.3 %all-to-all-start.3 = ((bf16[4,128,128]{2,1,0:T(8,128)(2,1)}), bf16[4,128,128]{2,1,0:T(8,128)(2,1)S(1)}, u32[]{:S(2)}, u32[]{:S(2)}) async-start(bf16[4,128,128]{2,1,0:T(8,128)(2,1)} %fusion.56), calls=%async_computation.3 | async-start | bytes 262144 | tf_op jit(solution)/shard_map/all_to_all | solution.py:73
  226.4 3.6 %all-to-all-done.3 = bf16[4,128,128]{2,1,0:T(8,128)(2,1)S(1)} async-done(((bf16[4,128,128]{2,1,0:T(8,128)(2,1)}), bf16[4,128,128]{2,1,0:T(8,128)(2,1)S(1)}, u32[]{:S(2)}, u32[]{:S(2)}) %all-to-all-start.3) | async-done | bytes 131104 | tf_op jit(solution)/shard_map/all_to_all | solution.py:73
  231.1 2.6 copy.177
  233.6 1.8 convolution_convert_fusion.5
  235.4 1.5 collective-permute-start.9
  238.3 4.1 %collective-permute-done.9 = bf16[128,896]{1,0:T(8,128)(2,1)S(1)} collective-permute-done((bf16[128,896]{1,0:T(8,128)(2,1)S(1)}, bf16[128,896]{1,0:T(8,128)(2,1)S(1)}, u32[]{:S(2)}, u32[]{:S(2)}) %collective-permute-start.9) | collective-permute-done | bytes 229408 | tf_op jit(solution)/shard_map/ppermute | solution.py:89
  242.9 10.5 %all-reduce.4 = f32[9472]{0:T(1024)S(1)} all-reduce(f32[9472]{0:T(1024)S(1)} %maximum_dynamic-update-slice_fusion), channel_id=2, replica_groups={{0,2,4,6},{8,10,12,14},{16,18,20,22},{24,26,28,30},{1,3,5,7},{9,11,13,1..., use_global_device_ids=true, to_apply=%add.4 | all-reduce | flops 9472 | bytes 75776
  253.5 1.9 collective-permute-start.12
  255.4 2.5 collective-permute-start.10
  261.2 3.5 %all-to-all-start.4 = ((bf16[4,56,1920]{2,1,0:T(8,128)(2,1)}), bf16[4,56,1920]{2,1,0:T(8,128)(2,1)S(1)}, u32[]{:S(2)}, u32[]{:S(2)}) async-start(bf16[4,56,1920]{2,1,0:T(8,128)(2,1)} %bitcast.124), calls=%async_computation.5 | async-start | bytes 1720320 | tf_op jit(solution)/shard_map/all_to_all | solution.py:73
  265.3 27.7 %reduce-scatter.7.cloned.1.call-done = bf16[56,1024]{1,0:T(8,128)(2,1)} async-done(((bf16[896,1024]{1,0:T(8,128)(2,1)}), bf16[56,1024]{1,0:T(8,128)(2,1)}) %reduce-scatter.7.cloned.1.call-update) | async-done | bytes 114704
  (215 shorter events, 39.0 us)
Async XLA Ops:
  7.2 4.7 %copy-start.13 = (bf16[56,2432]{1,0:T(8,128)(2,1)S(1)}, bf16[56,2432]{1,0:T(8,128)(2,1)}, u32[]{:S(2)}) copy-start(bf16[56,2432]{1,0:T(8,128)(2,1)} %param.27) | copy-start | bytes 817156
  7.2 48.8 %all-gather.4.cloned.1.call-start = ((), (), s32[]{:S(2)}) async-start(), calls=%async_computation.7 | async-start | bytes 2193408 | tf_op jit(solution)/shard_map/all_gather | solution.py:127
  12.0 5.7 %copy-start.22 = (s32[2,32]{1,0:T(2,128)S(1)}, s32[2,32]{1,0:T(2,128)}, u32[]{:S(2)}) copy-start(s32[2,32]{1,0:T(2,128)} %param.17) | copy-start | bytes 772
  12.0 6.9 %copy-start = (bf16[2,64,896]{2,1,0:T(8,128)(2,1)S(1)}, bf16[2,64,896]{2,1,0:T(8,128)(2,1)}, u32[]{:S(2)}) copy-start(bf16[2,64,896]{2,1,0:T(8,128)(2,1)} %param.15) | copy-start | bytes 688132
  12.4 7.5 %copy-start.23 = (bf16[448]{0:T(512)(128)(2,1)S(1)}, bf16[448]{0:T(512)(128)(2,1)}, u32[]{:S(2)}) copy-start(bf16[448]{0:T(512)(128)(2,1)} %param.23) | copy-start | bytes 2692
  12.4 7.5 %copy-start.24 = (bf16[64]{0:T(256)(128)(2,1)S(1)}, bf16[64]{0:T(256)(128)(2,1)}, u32[]{:S(2)}) copy-start(bf16[64]{0:T(256)(128)(2,1)} %param.25) | copy-start | bytes 388
  12.4 7.5 %copy-start.25 = (bf16[64]{0:T(256)(128)(2,1)S(1)}, bf16[64]{0:T(256)(128)(2,1)}, u32[]{:S(2)}) copy-start(bf16[64]{0:T(256)(128)(2,1)} %param.24) | copy-start | bytes 388
  13.4 18.1 %all-to-all-start = ((bf16[4,56,1920]{2,1,0:T(8,128)(2,1)}), bf16[4,56,1920]{2,1,0:T(8,128)(2,1)S(1)}, u32[]{:S(2)}, u32[]{:S(2)}) async-start(bf16[4,56,1920]{2,1,0:T(8,128)(2,1)} %copy.150), calls=%async_computation | async-start | bytes 1720320 | tf_op jit(solution)/shard_map/all_to_all | solution.py:73
  17.7 117.5 %all-gather.6.cloned.1.call-start = ((), (), s32[]{:S(2)}) async-start(), calls=%async_computation.8 | async-start | bytes 4300800 | tf_op jit(solution)/shard_map/all_gather | solution.py:70
  19.4 78.2 %copy-start.16 = (s32[2,448]{1,0:T(2,128)}, s32[2,448]{1,0:T(2,128)S(1)}, u32[]{:S(2)}) copy-start(s32[2,448]{1,0:T(2,128)S(1)} %le.9) | copy-start | bytes 10756
  19.8 39.8 %copy-start.18 = (f32[128]{0:T(128)}, f32[128]{0:T(128)S(1)}, u32[]{:S(2)}) copy-start(f32[128]{0:T(128)S(1)} %rsqrt.20) | copy-start | bytes 1540
  20.1 74.3 %copy-start.11 = (f32[128,64]{0,1:T(8,128)}, f32[128,64]{0,1:T(8,128)S(1)}, u32[]{:S(2)}) copy-start(f32[128,64]{0,1:T(8,128)S(1)} %get-tuple-element.110) | copy-start | bytes 98308
  32.4 228.8 %reduce-scatter.5.cloned.1.call-start = ((), (), s32[]{:S(2)}) async-start(), calls=%async_computation.9 | async-start | bytes 4300800 | tf_op jit(solution)/shard_map/reduce_scatter | solution.py:247
  65.1 10.7 %collective-permute-start.2 = (bf16[512,128]{0,1:T(8,128)(2,1)S(1)}, bf16[512,128]{0,1:T(8,128)(2,1)S(1)}, u32[]{:S(2)}, u32[]{:S(2)}) collective-permute-start(bf16[512,128]{0,1:T(8,128)(2,1)S(1)} %all_gather.19), channel_id=1, source_target_pairs={{0,24},{2,26},{4,28},{6,30},{8,16},{10,18},{12,20},{14,22},{16,8},... | collective-permute-start | bytes 393224 | tf_op jit(solution)/shard_map/ppermute | solution.py:78
  67.2 27.0 %collective-permute-start.1 = (bf16[512,128]{0,1:T(8,128)(2,1)S(1)}, bf16[512,128]{0,1:T(8,128)(2,1)S(1)}, u32[]{:S(2)}, u32[]{:S(2)}) collective-permute-start(bf16[512,128]{0,1:T(8,128)(2,1)S(1)} %all_gather.19), channel_id=1, source_target_pairs={{0,16},{2,18},{4,20},{6,22},{8,24},{10,26},{12,28},{14,30},{16,0},... | collective-permute-start | bytes 393224 | tf_op jit(solution)/shard_map/ppermute | solution.py:78
  67.2 27.1 %collective-permute-start = (bf16[512,128]{0,1:T(8,128)(2,1)S(1)}, bf16[512,128]{0,1:T(8,128)(2,1)S(1)}, u32[]{:S(2)}, u32[]{:S(2)}) collective-permute-start(bf16[512,128]{0,1:T(8,128)(2,1)S(1)} %all_gather.19), channel_id=1, source_target_pairs={{0,8},{2,10},{4,12},{6,14},{8,0},{10,2},{12,4},{14,6},{16,24},{18,... | collective-permute-start | bytes 393224 | tf_op jit(solution)/shard_map/ppermute | solution.py:78
  70.0 25.6 %copy-start.4 = (bf16[2,448,64]{2,1,0:T(8,128)(2,1)}, bf16[2,448,64]{2,1,0:T(8,128)(2,1)S(1)}, u32[]{:S(2)}) copy-start(bf16[2,448,64]{2,1,0:T(8,128)(2,1)S(1)} %reshape.339) | copy-start | bytes 344068
  95.6 4.0 %copy-start.1 = (f32[2,448,1024]{2,1,0:T(8,128)}, f32[2,448,1024]{2,1,0:T(8,128)S(1)}, u32[]{:S(2)}) copy-start(f32[2,448,1024]{2,1,0:T(8,128)S(1)} %get-tuple-element.120) | copy-start | bytes 11010052
  97.5 5.8 %copy-start.8 = (bf16[2,64,896]{2,1,0:T(8,128)(2,1)S(1)}, bf16[2,64,896]{2,1,0:T(8,128)(2,1)}, u32[]{:S(2)}) copy-start(bf16[2,64,896]{2,1,0:T(8,128)(2,1)} %param.16) | copy-start | bytes 688132
  100.0 10.9 %copy-start.9 = (bf16[128,448]{1,0:T(8,128)(2,1)}, bf16[128,448]{1,0:T(8,128)(2,1)S(1)}, u32[]{:S(2)}) copy-start(bf16[128,448]{1,0:T(8,128)(2,1)S(1)} %reshape.341) | copy-start | bytes 344068
  101.8 9.1 %collective-permute-start.3 = (bf16[128,896]{1,0:T(8,128)(2,1)S(1)}, bf16[128,896]{1,0:T(8,128)(2,1)S(1)}, u32[]{:S(2)}, u32[]{:S(2)}) collective-permute-start(bf16[128,896]{1,0:T(8,128)(2,1)S(1)} %convolution_convert_fusion.6), channel_id=1, source_target_pairs={{0,1},{1,0},{2,3},{3,2},{4,5},{5,4},{6,7},{7,6},{8,9},{9,8},{10,11... | collective-permute-start | bytes 688136 | tf_op jit(solution)/shard_map/ppermute | solution.py:89
  111.1 74.8 %copy-start.20 = (f32[128]{0:T(128)}, f32[128]{0:T(128)S(1)}, u32[]{:S(2)}) copy-start(f32[128]{0:T(128)S(1)} %add_rsqrt_fusion.1) | copy-start | bytes 1540
  146.7 8.0 %copy-start.28 = (bf16[512,640]{1,0:T(8,128)(2,1)S(1)}, bf16[512,640]{1,0:T(8,128)(2,1)}, u32[]{:S(2)}) copy-start(bf16[512,640]{1,0:T(8,128)(2,1)} %copy-done.27) | copy-start | bytes 1966084
  151.1 16.5 %all-to-all-start.2 = ((bf16[4,128,896]{2,1,0:T(8,128)(2,1)}), bf16[4,128,896]{2,1,0:T(8,128)(2,1)S(1)}, u32[]{:S(2)}, u32[]{:S(2)}) async-start(bf16[4,128,896]{2,1,0:T(8,128)(2,1)} %bitcast.22), calls=%async_computation.2 | async-start | bytes 1835008 | tf_op jit(solution)/shard_map/all_to_all | solution.py:73
  167.7 16.5 %all-to-all-start.1 = ((bf16[4,128,896]{2,1,0:T(8,128)(2,1)}), bf16[4,128,896]{2,1,0:T(8,128)(2,1)S(1)}, u32[]{:S(2)}, u32[]{:S(2)}) async-start(bf16[4,128,896]{2,1,0:T(8,128)(2,1)} %bitcast.122), calls=%async_computation.1 | async-start | bytes 1835008 | tf_op jit(solution)/shard_map/all_to_all | solution.py:73
  171.5 15.1 %copy-start.3 = (bf16[128,896]{1,0:T(8,128)(2,1)}, bf16[128,896]{1,0:T(8,128)(2,1)S(1)}, u32[]{:S(2)}) copy-start(bf16[128,896]{1,0:T(8,128)(2,1)S(1)} %reduce_sum.140) | copy-start | bytes 688132
  171.6 14.3 %collective-permute-start.5 = (bf16[128,896]{1,0:T(8,128)(2,1)S(1)}, bf16[128,896]{1,0:T(8,128)(2,1)S(1)}, u32[]{:S(2)}, u32[]{:S(2)}) collective-permute-start(bf16[128,896]{1,0:T(8,128)(2,1)S(1)} %reduce_sum.140), channel_id=1, source_target_pairs={{0,1},{1,0},{2,3},{3,2},{4,5},{5,4},{6,7},{7,6},{8,9},{9,8},{10,11... | collective-permute-start | bytes 688136 | tf_op jit(solution)/shard_map/ppermute | solution.py:89
  184.3 7.3 %collective-permute-start.4 = (bf16[128,896]{1,0:T(8,128)(2,1)S(1)}, bf16[128,896]{1,0:T(8,128)(2,1)S(1)}, u32[]{:S(2)}, u32[]{:S(2)}) collective-permute-start(bf16[128,896]{1,0:T(8,128)(2,1)S(1)} %reduce_sum.139), channel_id=1, source_target_pairs={{0,1},{1,0},{2,3},{3,2},{4,5},{5,4},{6,7},{7,6},{8,9},{9,8},{10,11... | collective-permute-start | bytes 688136 | tf_op jit(solution)/shard_map/ppermute | solution.py:89
  186.6 9.7 %copy-start.17 = (s32[2,448]{1,0:T(2,128)S(1)}, s32[2,448]{1,0:T(2,128)}, u32[]{:S(2)}) copy-start(s32[2,448]{1,0:T(2,128)} %copy-done.16) | copy-start | bytes 10756
  186.6 9.7 %copy-start.21 = (f32[2,448]{1,0:T(2,128)S(1)}, f32[2,448]{1,0:T(2,128)}, u32[]{:S(2)}) copy-start(f32[2,448]{1,0:T(2,128)} %get-tuple-element.116) | copy-start | bytes 10756
  196.3 4.7 %copy-start.14 = (f32[2,448,64]{1,2,0:T(8,128)S(1)}, f32[2,448,64]{1,2,0:T(8,128)}, u32[]{:S(2)}) copy-start(f32[2,448,64]{1,2,0:T(8,128)} %get-tuple-element.122) | copy-start | bytes 688132
  201.1 3.0 copy-start.5
  209.5 16.0 %copy-start.10 = (bf16[128,448]{1,0:T(8,128)(2,1)S(1)}, bf16[128,448]{1,0:T(8,128)(2,1)}, u32[]{:S(2)}) copy-start(bf16[128,448]{1,0:T(8,128)(2,1)} %copy-done.9) | copy-start | bytes 344068
  209.6 8.4 %collective-permute-start.8 = (bf16[4,128,128]{2,1,0:T(8,128)(2,1)S(1)}, bf16[4,128,128]{2,1,0:T(8,128)(2,1)S(1)}, u32[]{:S(2)}, u32[]{:S(2)}) collective-permute-start(bf16[4,128,128]{2,1,0:T(8,128)(2,1)S(1)} %bitcast.138), channel_id=1, source_target_pairs={{0,24},{2,26},{4,28},{6,30},{8,16},{10,18},{12,20},{14,22},{16,8},... | collective-permute-start | bytes 393224 | tf_op jit(solution)/shard_map/ppermute | solution.py:84
  210.9 10.5 %collective-permute-start.7 = (bf16[4,128,128]{2,1,0:T(8,128)(2,1)S(1)}, bf16[4,128,128]{2,1,0:T(8,128)(2,1)S(1)}, u32[]{:S(2)}, u32[]{:S(2)}) collective-permute-start(bf16[4,128,128]{2,1,0:T(8,128)(2,1)S(1)} %bitcast.137), channel_id=1, source_target_pairs={{0,16},{2,18},{4,20},{6,22},{8,24},{10,26},{12,28},{14,30},{16,0},... | collective-permute-start | bytes 393224 | tf_op jit(solution)/shard_map/ppermute | solution.py:84
  210.9 10.5 %collective-permute-start.6 = (bf16[4,128,128]{2,1,0:T(8,128)(2,1)S(1)}, bf16[4,128,128]{2,1,0:T(8,128)(2,1)S(1)}, u32[]{:S(2)}, u32[]{:S(2)}) collective-permute-start(bf16[4,128,128]{2,1,0:T(8,128)(2,1)S(1)} %bitcast.136), channel_id=1, source_target_pairs={{0,8},{2,10},{4,12},{6,14},{8,0},{10,2},{12,4},{14,6},{16,24},{18,... | collective-permute-start | bytes 393224 | tf_op jit(solution)/shard_map/ppermute | solution.py:84
  222.1 7.9 %all-to-all-start.3 = ((bf16[4,128,128]{2,1,0:T(8,128)(2,1)}), bf16[4,128,128]{2,1,0:T(8,128)(2,1)S(1)}, u32[]{:S(2)}, u32[]{:S(2)}) async-start(bf16[4,128,128]{2,1,0:T(8,128)(2,1)} %fusion.56), calls=%async_computation.3 | async-start | bytes 262144 | tf_op jit(solution)/shard_map/all_to_all | solution.py:73
  225.5 67.5 %reduce-scatter.7.cloned.1.call-start = ((), (), s32[]{:S(2)}) async-start(), calls=%async_computation.10 | async-start | bytes 1949696
  226.0 4.5 %copy-start.12 = (f32[128,64]{0,1:T(8,128)S(1)}, f32[128,64]{0,1:T(8,128)}, u32[]{:S(2)}) copy-start(f32[128,64]{0,1:T(8,128)} %copy-done.11) | copy-start | bytes 98308
  226.0 4.5 %copy-start.7 = (bf16[128,896]{1,0:T(8,128)(2,1)S(1)}, bf16[128,896]{1,0:T(8,128)(2,1)}, u32[]{:S(2)}) copy-start(bf16[128,896]{1,0:T(8,128)(2,1)} %copy-done.6) | copy-start | bytes 688132
  233.6 3.3 %copy-start.26 = (u32[32]{0:T(128)S(1)}, u32[32]{0:T(128)}, u32[]{:S(2)}) copy-start(u32[32]{0:T(128)} %constant.94) | copy-start | bytes 388
  233.6 8.8 %copy-start.19 = (f32[128]{0:T(128)S(1)}, f32[128]{0:T(128)}, u32[]{:S(2)}) copy-start(f32[128]{0:T(128)} %copy-done.18) | copy-start | bytes 1540
  233.6 9.1 %copy-start.15 = (f32[896]{0:T(1024)S(1)}, f32[896]{0:T(1024)}, u32[]{:S(2)}) copy-start(f32[896]{0:T(1024)} %get-tuple-element.84) | copy-start | bytes 10756
  235.4 7.0 %collective-permute-start.9 = (bf16[128,896]{1,0:T(8,128)(2,1)S(1)}, bf16[128,896]{1,0:T(8,128)(2,1)S(1)}, u32[]{:S(2)}, u32[]{:S(2)}) collective-permute-start(bf16[128,896]{1,0:T(8,128)(2,1)S(1)} %convolution_convert_fusion.5), channel_id=1, source_target_pairs={{0,1},{1,0},{2,3},{3,2},{4,5},{5,4},{6,7},{7,6},{8,9},{9,8},{10,11... | collective-permute-start | bytes 688136 | tf_op jit(solution)/shard_map/ppermute | solution.py:89
  253.5 5.6 %collective-permute-start.12 = (f32[2368]{0:T(1024)S(1)}, f32[2368]{0:T(1024)S(1)}, u32[]{:S(2)}, u32[]{:S(2)}) collective-permute-start(f32[2368]{0:T(1024)S(1)} %reduce_sum.148), channel_id=1, source_target_pairs={{0,24},{2,26},{4,28},{6,30},{8,16},{10,18},{12,20},{14,22},{16,8},... | collective-permute-start | bytes 28424 | tf_op jit(solution)/shard_map/ppermute | solution.py:78
  255.4 4.6 %collective-permute-start.11 = (f32[2368]{0:T(1024)S(1)}, f32[2368]{0:T(1024)S(1)}, u32[]{:S(2)}, u32[]{:S(2)}) collective-permute-start(f32[2368]{0:T(1024)S(1)} %reduce_sum.148), channel_id=1, source_target_pairs={{0,16},{2,18},{4,20},{6,22},{8,24},{10,26},{12,28},{14,30},{16,0},... | collective-permute-start | bytes 28424 | tf_op jit(solution)/shard_map/ppermute | solution.py:78
  255.4 4.6 %collective-permute-start.10 = (f32[2368]{0:T(1024)S(1)}, f32[2368]{0:T(1024)S(1)}, u32[]{:S(2)}, u32[]{:S(2)}) collective-permute-start(f32[2368]{0:T(1024)S(1)} %reduce_sum.148), channel_id=1, source_target_pairs={{0,8},{2,10},{4,12},{6,14},{8,0},{10,2},{12,4},{14,6},{16,24},{18,... | collective-permute-start | bytes 28424 | tf_op jit(solution)/shard_map/ppermute | solution.py:78
  261.2 35.8 %all-to-all-start.4 = ((bf16[4,56,1920]{2,1,0:T(8,128)(2,1)}), bf16[4,56,1920]{2,1,0:T(8,128)(2,1)S(1)}, u32[]{:S(2)}, u32[]{:S(2)}) async-start(bf16[4,56,1920]{2,1,0:T(8,128)(2,1)} %bitcast.124), calls=%async_computation.5 | async-start | bytes 1720320 | tf_op jit(solution)/shard_map/all_to_all | solution.py:73
  (6 other events, 7.4 us)
Sparse Core Ops, SparseCore 0:
  10.8 45.1 all-gather.3
  57.6 77.5 all-gather.5
  145.7 63.0 reduce-scatter.4
  233.8 59.1 reduce-scatter.6

commit v2 on v1

v2 whole, which is shorter than its diff:
```python
import functools

import jax
import jax.numpy as jnp
from jax import lax
from jax.experimental import pallas as pl
from jax.experimental.pallas import tpu as pltpu
from jax.sharding import PartitionSpec as P

HEAD = 64


EPSILON = 1e-06
ROPE_BASE = 1000000.0
MASKED = -1e30
LOWEST = -1e29
VMEM_LIMIT = 48 * 1024 * 1024


def rope_tables(positions, head_dim):
    halfway = head_dim // 2
    inverse = ROPE_BASE ** (-(jnp.arange(halfway, dtype=jnp.float32) * 2.0 / head_dim))
    angles = positions.astype(jnp.float32)[..., None] * inverse
    angles = jnp.concatenate([angles, angles], axis=-1)
    return (jnp.cos(angles), jnp.sin(angles))


def unrotate(grads, cosine, sine):
    halfway = grads.shape[-1] // 2
    moved = grads * sine
    back = jnp.concatenate([moved[..., halfway:], -moved[..., :halfway]], axis=-1)
    return grads * cosine + back


def norm_apply(values):
    factor = lax.rsqrt(jnp.mean(values * values, axis=-1, keepdims=True) + EPSILON)
    return values * factor, factor


def norm_back(values, factor, weighted):
    inner = jnp.mean(weighted * values, axis=-1, keepdims=True)
    return factor * weighted - values * factor * factor * factor * inner


def dot(left, right, left_dim, right_dim):
    return lax.dot_general(
        left, right, (((left_dim,), (right_dim,)), ((), ())), preferred_element_type=jnp.float32
    )


def sum_tp(values):
    other = lax.ppermute(values, "tp", [(0, 1), (1, 0)])
    return values.astype(jnp.float32) + other.astype(jnp.float32)


def together(*values):
    return lax.optimization_barrier(values)


class Groups:
    def __init__(self, count):
        self.count = count
        self.low = min(4, count)
        self.high = count // self.low
        self.near = [[h * self.low + k for k in range(self.low)] for h in range(self.high)]
        self.far = [list(group) for group in zip(*self.near)]

    def flip(self, values, bit):
        return lax.ppermute(values, "ctx", [(i, i ^ bit) for i in range(self.count)])

    def swap_near(self, values):
        return lax.all_to_all(values, "ctx", 0, 0, tiled=True, axis_index_groups=self.near)

    def gather_near(self, values):
        first = jnp.concatenate([values, self.flip(values, 2)], axis=0)
        return first, self.flip(first, 1)

    def sum_near(self, parts):
        kept = parts[0].astype(jnp.float32) + self.flip(parts[1], 1).astype(jnp.float32)
        kept = kept.astype(jnp.bfloat16)
        rows = kept.shape[0] // 2
        sent = self.flip(kept[rows:], 2)
        return (kept[:rows].astype(jnp.float32) + sent.astype(jnp.float32)).astype(jnp.bfloat16)

    def far_flips(self, values):
        return [values] + [self.flip(values, self.low * m) for m in range(1, self.high)]

    def gather_far(self, values, place):
        if self.high != 4:
            return lax.all_gather(values, "ctx", axis=0, axis_index_groups=self.far)
        group = place // self.low
        far = jnp.stack(self.far_flips(values)).reshape((2, 2) + values.shape)
        far = jnp.where(group // 2 % 2 == 1, far[::-1], far)
        far = jnp.where(group % 2 == 1, far[:, ::-1], far)
        return far.reshape((4,) + values.shape)

    def spread_near(self, values):
        whole = lax.all_gather(values, "ctx", axis=0, axis_index_groups=self.near)
        whole = jnp.swapaxes(whole, 0, 1)
        return whole.reshape((self.count * values.shape[1],) + values.shape[2:])

    def gather_xor(self, values):
        far = jnp.stack(self.far_flips(values))
        both = jnp.stack([far, self.flip(far, 2)])
        return jnp.stack([both, self.flip(both, 1)])

    def sum_xor(self, pieces):
        kept = pieces[0].astype(jnp.float32) + self.flip(pieces[1], 1).astype(jnp.float32)
        low = kept.astype(jnp.bfloat16)
        kept = kept[0] + self.flip(low[1], 2).astype(jnp.float32)
        low = kept.astype(jnp.bfloat16)
        total = kept[0]
        for m in range(1, self.high):
            total = total + self.flip(low[m], self.low * m).astype(jnp.float32)
        return total

    def near_owner(self, pieces, place):
        pieces = pieces.reshape((self.high, 2, 2) + pieces.shape[1:])
        return halve(self, halve(self, pieces, 1, place, 2), 2, place, 1)

    def far_owner(self, pieces, place):
        if self.high > 4:
            shape = pieces.shape
            pieces = pieces.reshape((shape[0] * shape[1],) + shape[2:])
            return lax.psum_scatter(
                pieces, "ctx", scatter_dimension=0, tiled=True, axis_index_groups=self.far
            ).astype(jnp.float32)
        group = place // self.low
        total = lax.dynamic_index_in_dim(pieces, group, 0, False).astype(jnp.float32)
        for m in range(1, self.high):
            sent = lax.dynamic_index_in_dim(pieces, group ^ m, 0, False)
            total = total + self.flip(sent, self.low * m).astype(jnp.float32)
        return total


def halve(groups, pieces, bit, place, axis):
    mine = place // bit % 2
    kept = lax.dynamic_index_in_dim(pieces, mine, axis, False).astype(jnp.float32)
    sent = groups.flip(lax.dynamic_index_in_dim(pieces, 1 - mine, axis, False), bit)
    return (kept + sent.astype(jnp.float32)).astype(jnp.bfloat16)


def stack_heads(flat, heads, upper):
    tall = jnp.concatenate([flat[:, h * HEAD : (h + 1) * HEAD] for h in range(heads)], axis=0)
    blank = jnp.zeros_like(tall)
    return jnp.concatenate([blank, tall] if upper else [tall, blank], axis=1)


def flat_heads(tall, heads):
    rows = tall.shape[0] // heads
    return jnp.concatenate([tall[h * rows : (h + 1) * rows] for h in range(heads)], axis=1)


def masked_scores(pair, wide, key_pos, query_pos):
    return jnp.where(key_pos <= query_pos, dot(pair, wide, 1, 1), MASKED)


def first_half(shape):
    return lax.broadcasted_iota(jnp.int32, shape, 1) % HEAD < HEAD // 2


def turn(values):
    width = values.shape[1]
    return jnp.where(
        first_half(values.shape),
        pltpu.roll(values, width - HEAD // 2, 1),
        pltpu.roll(values, HEAD // 2, 1),
    )


def widen(table, width):
    return jnp.concatenate([table] * (width // table.shape[1]), axis=1)


def project_kernel(
    heads, token_ref, w_ref, bias_ref, cosine_ref, sine_ref, normed_ref, query_ref, pair_ref
):
    normed, _ = norm_apply(token_ref[...].astype(jnp.float32))
    normed = normed.astype(jnp.bfloat16)
    normed_ref[...] = normed
    lin = dot(normed, w_ref[...], 1, 0) + bias_ref[...]
    width = (heads + 1) * HEAD
    some = lin[:, :width]
    turned = turn(some)
    turned = jnp.where(first_half(some.shape), -turned, turned)
    rotated = some * widen(cosine_ref[...], width) + turned * widen(sine_ref[...], width)
    rotated = rotated.astype(jnp.bfloat16)
    query_ref[...] = rotated[:, : heads * HEAD] * jnp.bfloat16(HEAD ** (-0.5))
    pair_ref[...] = jnp.concatenate(
        [rotated[:, heads * HEAD :], lin[:, width:].astype(jnp.bfloat16)], axis=1
    )


def load_pair(pair_ref):
    return pair_ref[...].reshape(-1, 2 * HEAD)


def forward_kernel(
    heads,
    query_ref,
    pair_ref,
    key_pos_ref,
    query_pos_ref,
    w_out_ref,
    flat_ref,
    part_ref,
    out_ref,
    log_ref,
    best_ref,
    total_ref,
    sum_ref,
):
    step = pl.program_id(1)

    @pl.when(step == 0)
    def _():
        best_ref[...] = jnp.full_like(best_ref, LOWEST)
        total_ref[...] = jnp.zeros_like(total_ref)
        sum_ref[...] = jnp.zeros_like(sum_ref)

    pair = load_pair(pair_ref)
    wide = stack_heads(query_ref[0], heads, False)
    scores = masked_scores(pair, wide, key_pos_ref[0], query_pos_ref[0])
    best = best_ref[...]
    newest = jnp.maximum(best, jnp.max(scores, axis=0, keepdims=True))
    raised = jnp.exp(scores - newest)
    fading = jnp.exp(best - newest)
    best_ref[...] = newest
    total_ref[...] = total_ref[...] * fading + jnp.sum(raised, axis=0, keepdims=True)
    sum_ref[...] = sum_ref[...] * fading + dot(pair, raised.astype(jnp.bfloat16), 0, 0)

    @pl.when(step == pl.num_programs(1) - 1)
    def _():
        out = sum_ref[HEAD:, :] / total_ref[...]
        out_ref[0] = out
        log_ref[0] = best_ref[...] + jnp.log(total_ref[...])
        flat = flat_heads(out.T, heads).astype(jnp.bfloat16)
        flat_ref[0] = flat
        part_ref[0] = dot(flat, w_out_ref[...], 1, 1).astype(jnp.bfloat16)


def backward_kernel(
    heads,
    query_ref,
    pair_ref,
    key_pos_ref,
    query_pos_ref,
    out_ref,
    log_ref,
    w_out_ref,
    own_ref,
    other_ref,
    hidden_ref,
    cotangent_ref,
    cosine_ref,
    sine_ref,
    d_hidden_ref,
    d_low_ref,
    d_query_ref,
    d_pair_ref,
    d_out_ref,
    dots_ref,
    sum_ref,
):
    step = pl.program_id(1)

    @pl.when(step == 0)
    def _():
        sum_ref[...] = jnp.zeros_like(sum_ref)
        hidden = hidden_ref[0]
        weighted = own_ref[0].astype(jnp.float32) + other_ref[0].astype(jnp.float32)
        _, scale = norm_apply(hidden)
        d_hidden = cotangent_ref[0].astype(jnp.float32) + norm_back(hidden, scale, weighted)
        d_hidden_ref[0] = d_hidden
        low = d_hidden.astype(jnp.bfloat16)
        d_low_ref[0] = low
        flat = dot(low, w_out_ref[...], 1, 0).astype(jnp.bfloat16)
        d_out = stack_heads(flat, heads, True)
        d_out_ref[...] = d_out
        dots_ref[...] = jnp.sum(
            d_out[:, HEAD:].astype(jnp.float32).T * out_ref[0], axis=0, keepdims=True
        )

    pair = load_pair(pair_ref)
    wide = stack_heads(query_ref[0], heads, False)
    d_out = d_out_ref[...]
    scores = masked_scores(pair, wide, key_pos_ref[0], query_pos_ref[0])
    chances = jnp.exp(scores - log_ref[0])
    d_scores = (chances * (dot(pair, d_out, 1, 1) - dots_ref[...])).astype(jnp.bfloat16)
    d_pair = dot(d_scores, wide, 1, 0) + dot(chances.astype(jnp.bfloat16), d_out, 1, 0)
    d_pair_ref[...] = d_pair.astype(jnp.bfloat16).reshape(d_pair_ref.shape)
    sum_ref[...] += dot(pair, d_scores, 0, 0)

    @pl.when(step == pl.num_programs(1) - 1)
    def _():
        flat = flat_heads(sum_ref[:HEAD, :].T, heads) * (HEAD ** (-0.5))
        width = (heads + 1) * HEAD
        flat = jnp.concatenate([flat, jnp.zeros((flat.shape[0], HEAD), jnp.float32)], axis=1)
        turned = turn(flat * widen(sine_ref[0], width))
        turned = jnp.where(first_half(flat.shape), turned, -turned)
        back = flat * widen(cosine_ref[0], width) + turned
        d_query_ref[0] = back[:, : heads * HEAD].astype(jnp.bfloat16)


def attention_call(kernel, name, heads, rows, ctx, seqs, width, inputs, kinds, outs, scratch):
    group = min(ctx, 1024 // rows)
    span = group * rows
    tall = heads * rows
    wide = heads * HEAD
    shapes = {
        "flat": ((seqs, rows, wide), (1, rows, wide), lambda s, k: (s, 0, 0)),
        "model": ((seqs, rows, width), (1, rows, width), lambda s, k: (s, 0, 0)),
        "table": ((seqs, rows, 2 * HEAD), (1, rows, 2 * HEAD), lambda s, k: (s, 0, 0)),
        "pair": (
            (ctx, seqs, rows, 2 * HEAD),
            (group, 1, rows, 2 * HEAD),
            lambda s, k: (k, s, 0, 0),
        ),
        "key": ((seqs, ctx * rows, 1), (1, span, 1), lambda s, k: (s, k, 0)),
        "row": ((seqs, 1, tall), (1, 1, tall), lambda s, k: (s, 0, 0)),
        "out": ((seqs, HEAD, tall), (1, HEAD, tall), lambda s, k: (s, 0, 0)),
        "weight": ((width, wide), (width, wide), lambda s, k: (0, 0)),
    }
    spec = lambda kind: pl.BlockSpec(shapes[kind][1], shapes[kind][2])
    flops = 2 * seqs * tall * ctx * rows * 2 * HEAD * (2 if name == "forward" else 5)
    return pl.pallas_call(
        functools.partial(kernel, heads),
        grid=(seqs, ctx // group),
        in_specs=[spec(kind) for kind in kinds],
        out_specs=[spec(kind) for kind, _ in outs],
        out_shape=[jax.ShapeDtypeStruct(shapes[kind][0], dtype) for kind, dtype in outs],
        scratch_shapes=scratch,
        compiler_params=pltpu.CompilerParams(
            dimension_semantics=("arbitrary", "arbitrary"), vmem_limit_bytes=VMEM_LIMIT
        ),
        cost_estimate=pl.CostEstimate(
            flops=flops,
            bytes_accessed=4 * seqs * ctx * rows * 2 * HEAD,
            transcendentals=seqs * tall * ctx * rows,
        ),
        name=name,
    )(*inputs)


def ffn_kernel(
    part,
    normed_one,
    normed_two,
    grad_one,
    grad_two,
    w_ref,
    near_ref,
    mixed_ref,
    active_ref,
    d_gate_up_ref,
):
    step = pl.program_id(0)

    def run(normed_ref, grad_ref):
        gate_up = dot(normed_ref[...], w_ref[:, : 2 * part], 1, 0)
        gate, up_values = gate_up[:, :part], gate_up[:, part:]
        sigma = 1.0 / (1.0 + jnp.exp(-gate))
        silu = gate * sigma
        active = (silu * up_values).astype(jnp.bfloat16)
        active_ref[...] = active
        d_active = dot(grad_ref[...], w_ref[:, 2 * part :], 1, 0)
        d_gate = d_active * up_values * sigma * (1.0 + gate * (1.0 - sigma))
        d_gate_up = jnp.concatenate([d_gate, d_active * silu], axis=1).astype(jnp.bfloat16)
        d_gate_up_ref[...] = d_gate_up
        near_ref[0] = dot(d_gate_up, w_ref[:, : 2 * part], 1, 1).astype(jnp.bfloat16)
        mixed_ref[0] = dot(active, w_ref[:, 2 * part :], 1, 1).astype(jnp.bfloat16)

    pl.when(step == 0)(functools.partial(run, normed_one, grad_one))
    pl.when(step == 1)(functools.partial(run, normed_two, grad_two))


def ffn_call(part, normed, grads, w_ffn):
    block, width = normed[0].shape
    fixed = lambda shape: pl.BlockSpec(shape, lambda i: (0, 0))
    model = pl.BlockSpec((1, block, width), lambda i: (i, 0, 0))
    units = lambda count: pl.BlockSpec((block, count * part), lambda i: (i, 0))
    return pl.pallas_call(
        functools.partial(ffn_kernel, part),
        grid=(2,),
        in_specs=[fixed((block, width))] * 4 + [fixed(w_ffn.shape)],
        out_specs=[model, model, units(1), units(2)],
        out_shape=[
            jax.ShapeDtypeStruct((2, block, width), jnp.bfloat16),
            jax.ShapeDtypeStruct((2, block, width), jnp.bfloat16),
            jax.ShapeDtypeStruct((2 * block, part), jnp.bfloat16),
            jax.ShapeDtypeStruct((2 * block, 2 * part), jnp.bfloat16),
        ],
        compiler_params=pltpu.CompilerParams(
            dimension_semantics=("arbitrary",), vmem_limit_bytes=VMEM_LIMIT
        ),
        cost_estimate=pl.CostEstimate(
            flops=4 * block * width * part * 6,
            bytes_accessed=2 * width * (8 * block + 3 * part),
            transcendentals=2 * block * part,
        ),
        name="ffn",
    )(*normed, *grads, w_ffn)


def ffn_grad_kernel(
    normed_one, normed_two, grad_one, grad_two, active_ref, d_gate_up_ref, out_ref
):
    step = pl.program_id(0)

    def run(one_ref, two_ref, right_ref):
        half = one_ref.shape[0]
        total = dot(one_ref[...], right_ref[:half], 0, 0) + dot(two_ref[...], right_ref[half:], 0, 0)
        out_ref[...] = total.astype(jnp.bfloat16)

    pl.when(step < 2)(functools.partial(run, normed_one, normed_two, d_gate_up_ref))
    pl.when(step == 2)(functools.partial(run, grad_one, grad_two, active_ref))


def ffn_grad_call(part, normed, grads, active, d_gate_up):
    block, width = normed[0].shape
    fixed = lambda shape: pl.BlockSpec(shape, lambda j: (0, 0))
    return pl.pallas_call(
        ffn_grad_kernel,
        grid=(3,),
        in_specs=[fixed((block, width))] * 4
        + [
            fixed((2 * block, part)),
            pl.BlockSpec((2 * block, part), lambda j: (0, jnp.minimum(j, 1))),
        ],
        out_specs=pl.BlockSpec((width, part), lambda j: (0, j)),
        out_shape=jax.ShapeDtypeStruct((width, 3 * part), jnp.bfloat16),
        compiler_params=pltpu.CompilerParams(
            dimension_semantics=("arbitrary",), vmem_limit_bytes=VMEM_LIMIT
        ),
        cost_estimate=pl.CostEstimate(
            flops=4 * block * width * part * 3,
            bytes_accessed=2 * width * (8 * block + 3 * part),
            transcendentals=0,
        ),
        name="ffn_grad",
    )(*normed, *grads, active, d_gate_up)


def local(
    tokens,
    cotangent,
    block_of,
    norm_gain,
    ffn_gain,
    w_query,
    w_key,
    w_value,
    b_query,
    b_key,
    b_value,
    w_out,
    w_gate,
    w_up,
    w_down,
):
    seqs, rows, width = tokens.shape
    count = seqs * rows
    block_len = rows // 2
    ctx = lax.axis_size("ctx")
    groups = Groups(ctx)
    low = groups.low
    device = lax.axis_index("ctx")
    heads = w_query.shape[1] // HEAD
    share = width // ctx
    units = w_gate.shape[1]
    part = -(-units // (low * 128)) * 128
    query_width = heads * HEAD
    own_gain_one = norm_gain.astype(jnp.float32)[:, None]
    own_gain_two = ffn_gain.astype(jnp.float32)[:, None]

    def scaled(matrix, gain):
        return (matrix.astype(jnp.float32) * gain).astype(jnp.bfloat16)

    def pieces(matrix):
        return jnp.pad(matrix, ((0, 0), (0, low * part - units))).reshape(share, low, part)

    w_ffn = jnp.concatenate(
        [
            pieces(scaled(w_gate, own_gain_two)),
            pieces(scaled(w_up, own_gain_two)),
            pieces(w_down.T),
        ],
        axis=2,
    )
    w_ffn = groups.swap_near(w_ffn.transpose(1, 0, 2)).reshape(low * share, 3 * part)
    w_attn = jnp.concatenate(
        [scaled(jnp.concatenate([w_query, w_key, w_value], axis=1), own_gain_one), w_out.T], axis=1
    )
    w_attn = groups.gather_far(w_attn, device)

    offsets = jnp.arange(block_len, dtype=jnp.int32)
    own_blocks = lax.dynamic_slice_in_dim(block_of, device * 2, 2, 1)
    row_pos = (own_blocks[:, :, None] * block_len + offsets).reshape(seqs, rows)
    query_pos = jnp.tile(row_pos, (1, heads))[:, None, :]
    flips = jnp.arange(ctx, dtype=jnp.int32)
    high = groups.high
    flips = flips // (2 * high) + flips // high % 2 * 2 + flips % high * low
    key_blocks = block_of.reshape(seqs, ctx, 2)[:, device ^ flips]
    key_pos = (key_blocks[..., None] * block_len + offsets).reshape(seqs, ctx * rows, 1)
    cosine, sine = rope_tables(row_pos.reshape(count), HEAD)
    cosine, sine = jnp.tile(cosine, (1, 2)), jnp.tile(sine, (1, 2))

    w_ffn, w_attn, key_pos, query_pos, cosine, sine = together(
        w_ffn, w_attn, key_pos, query_pos, cosine, sine
    )
    w_ffn = lax.all_gather(w_ffn, "ctx", axis=0, tiled=True, axis_index_groups=groups.far)
    qkv_width = query_width + 2 * HEAD
    w_qkv = groups.spread_near(w_attn[:, :, :qkv_width])
    grads_in = cotangent.reshape(count, width)

    bias = jnp.concatenate([b_query, b_key, b_value]).astype(jnp.float32)[None]
    normed_low, queries, pair = pl.pallas_call(
        functools.partial(project_kernel, heads),
        out_shape=[
            jax.ShapeDtypeStruct((count, width), jnp.bfloat16),
            jax.ShapeDtypeStruct((count, query_width), jnp.bfloat16),
            jax.ShapeDtypeStruct((count, 2 * HEAD), jnp.bfloat16),
        ],
        compiler_params=pltpu.CompilerParams(vmem_limit_bytes=VMEM_LIMIT),
        cost_estimate=pl.CostEstimate(
            flops=2 * count * width * (query_width + 2 * HEAD),
            bytes_accessed=2 * width * (count + query_width),
            transcendentals=0,
        ),
        name="project",
    )(tokens.reshape(count, width), w_qkv, bias, cosine, sine)
    queries = queries.reshape(seqs, rows, query_width)
    pairs = groups.gather_xor(pair).reshape(ctx, seqs, rows, 2 * HEAD)
    w_out_t = groups.spread_near(w_attn[:, :, qkv_width:])
    pairs, w_out_t = together(pairs, w_out_t)
    attend = functools.partial(
        attention_call, heads=heads, rows=rows, ctx=ctx, seqs=seqs, width=width
    )
    tall = heads * rows
    out_flat, attention, out_tall, log_total = attend(
        forward_kernel,
        "forward",
        inputs=(queries, pairs, key_pos, query_pos, w_out_t),
        kinds=("flat", "pair", "key", "row", "weight"),
        outs=(
            ("flat", jnp.bfloat16),
            ("model", jnp.bfloat16),
            ("out", jnp.float32),
            ("row", jnp.float32),
        ),
        scratch=[
            pltpu.VMEM((1, tall), jnp.float32),
            pltpu.VMEM((1, tall), jnp.float32),
            pltpu.VMEM((2 * HEAD, tall), jnp.float32),
        ],
    )
    out_flat = out_flat.reshape(count, query_width)
    inputs = tokens.astype(jnp.float32).reshape(count, width)
    hidden = inputs + sum_tp(attention.reshape(count, width))

    grads_near = groups.gather_near(grads_in)
    hidden, *grads_near = together(hidden, *grads_near)
    normed_two, _ = norm_apply(hidden)
    near_two = groups.gather_near(normed_two.astype(jnp.bfloat16))
    d_near, mixed_near, active, d_gate_up = ffn_call(part, near_two, grads_near, w_ffn)
    d_w_ffn = ffn_grad_call(part, near_two, grads_near, active, d_gate_up)
    d_own = groups.sum_near(d_near)
    d_own, _ = together(d_own, d_w_ffn)
    d_other = lax.ppermute(d_own, "tp", [(0, 1), (1, 0)])
    d_w_ffn = lax.psum_scatter(
        d_w_ffn, "ctx", scatter_dimension=0, tiled=True, axis_index_groups=groups.far
    )

    by_seq = lambda values: values.reshape((seqs, rows) + values.shape[1:])
    d_hidden, d_hidden_low, d_query_low, d_pairs = attend(
        backward_kernel,
        "backward",
        inputs=(
            queries,
            pairs,
            key_pos,
            query_pos,
            out_tall,
            log_total,
            w_out_t,
            by_seq(d_own),
            by_seq(d_other),
            by_seq(hidden),
            cotangent,
            by_seq(cosine),
            by_seq(sine),
        ),
        kinds=(
            ("flat", "pair", "key", "row", "out", "row", "weight")
            + ("model", "model", "model", "model", "table", "table")
        ),
        outs=(
            ("model", jnp.float32),
            ("model", jnp.bfloat16),
            ("flat", jnp.bfloat16),
            ("pair", jnp.bfloat16),
        ),
        scratch=[
            pltpu.VMEM((tall, 2 * HEAD), jnp.bfloat16),
            pltpu.VMEM((1, tall), jnp.float32),
            pltpu.VMEM((2 * HEAD, tall), jnp.float32),
        ],
    )
    d_hidden = d_hidden.reshape(count, width)
    d_hidden_low = d_hidden_low.reshape(count, width)
    d_query_low = d_query_low.reshape(count, query_width)
    mixed_near, d_query_low = together(mixed_near, d_query_low)
    mixed_own = groups.sum_near(mixed_near)
    pair_grads = groups.sum_xor(d_pairs.reshape(2, 2, high, count, 2 * HEAD))
    d_w_wide = jnp.concatenate(
        [dot(normed_low, d_query_low, 0, 0), dot(d_hidden_low, out_flat, 0, 0)], axis=1
    ).astype(jnp.bfloat16)
    d_w_wide = groups.near_owner(d_w_wide.reshape(ctx, share, 2 * query_width), device)
    pair_grads, mixed_own, d_w_wide = together(pair_grads, mixed_own, d_w_wide)
    d_w_wide = groups.far_owner(d_w_wide, device)
    mixed = (hidden + sum_tp(mixed_own)).astype(jnp.bfloat16)

    d_key = pair_grads[:, :HEAD]
    d_pair_low = jnp.concatenate(
        [unrotate(d_key, cosine[:, :HEAD], sine[:, :HEAD]), pair_grads[:, HEAD:]], axis=1
    ).astype(jnp.bfloat16)
    d_weighted_part = dot(d_query_low, w_qkv[:, :query_width], 1, 1) + dot(
        d_pair_low, w_qkv[:, query_width:], 1, 1
    )
    d_weighted = sum_tp(d_weighted_part.astype(jnp.bfloat16))
    normed, scale_one = norm_apply(inputs)
    tokens_grad = (d_hidden + norm_back(inputs, scale_one, d_weighted)).astype(jnp.bfloat16)

    d_weighted_two = d_own.astype(jnp.float32) + d_other.astype(jnp.float32)
    ones = jnp.zeros((2, count, 128), jnp.float32)
    ones = ones.at[0, :, 0].set(1.0).at[1, :, 1].set(1.0).reshape(2 * count, 128)
    gain_columns = lax.dot_general(
        jnp.concatenate([d_weighted_part * normed, d_weighted_two * normed_two], axis=0),
        ones,
        (((0,), (0,)), ((), ())),
        precision=lax.Precision.HIGHEST,
    )
    narrow = jnp.concatenate([dot(normed_low, d_pair_low, 0, 0), gain_columns], axis=1)
    bias = jnp.concatenate(
        [
            jnp.sum(d_query_low.astype(jnp.float32), axis=0),
            jnp.sum(d_pair_low.astype(jnp.float32), axis=0),
        ]
    )
    bias = jnp.pad(bias, (0, 8 * 256 - bias.shape[0])).reshape(1, 8, 256)
    narrow = jnp.concatenate(
        [narrow.reshape(ctx, share, 256), jnp.broadcast_to(bias, (ctx, 8, 256))], axis=1
    ).astype(jnp.bfloat16)
    narrow = groups.far_owner(groups.near_owner(narrow, device), device)
    d_w_ffn = groups.swap_near(d_w_ffn.reshape(low, share, 3 * part))
    d_w_ffn = d_w_ffn.transpose(1, 0, 2).astype(jnp.float32)

    def whole(index):
        some = d_w_ffn[:, :, index * part : (index + 1) * part]
        return some.reshape(share, low * part)[:, :units]

    g_gate, g_up, g_down = whole(0) * own_gain_two, whole(1) * own_gain_two, whole(2).T

    g_bias = narrow[share:].reshape(8 * 256)
    g_pair = narrow[:share, : 2 * HEAD] * own_gain_one
    g_two = narrow[:share, 2 * HEAD + 1] / own_gain_two[:, 0]
    g_one = narrow[:share, 2 * HEAD] / own_gain_one[:, 0]
    g_one = g_one + lax.ppermute(g_one, "tp", [(0, 1), (1, 0)])
    return (
        mixed.reshape(tokens.shape),
        tokens_grad.reshape(tokens.shape),
        g_one,
        g_two,
        d_w_wide[:, :query_width] * own_gain_one,
        g_pair[:, :HEAD],
        g_pair[:, HEAD:],
        g_bias[:query_width],
        g_bias[query_width : query_width + HEAD],
        g_bias[query_width + HEAD : query_width + 2 * HEAD],
        d_w_wide[:, query_width:].T,
        g_gate,
        g_up,
        g_down,
    )


def solution(mesh):
    placed = (
        P(None, "ctx", None),
        P(None, "ctx", None),
        P(),
        P("ctx"),
        P("ctx"),
        P("ctx", "tp"),
        P("ctx", "tp"),
        P("ctx", "tp"),
        P("tp"),
        P("tp"),
        P("tp"),
        P("tp", "ctx"),
        P("ctx", "tp"),
        P("ctx", "tp"),
        P("tp", "ctx"),
    )
    return jax.shard_map(
        local,
        mesh=mesh,
        in_specs=placed,
        out_specs=(
            P(None, "ctx", None),
            P(None, "ctx", None),
            P("ctx"),
            P("ctx"),
            P("ctx", "tp"),
            P("ctx", "tp"),
            P("ctx", "tp"),
            P("tp"),
            P("tp"),
            P("tp"),
            P("tp", "ctx"),
            P("ctx", "tp"),
            P("ctx", "tp"),
            P("tp", "ctx"),
        ),
        check_vma=False,
    )
```

time: 308 us -> 250 us (0.81)
  waiting for transfers between devices: 142 us -> 89.5 us
  matrix products: 34.5 us -> 4.87 us
  Pallas kernels: 0 us -> 20.2 us
  blocking collectives: 33.8 us -> 19.5 us
  starting transfers between devices: 37.9 us -> 50.6 us
  other arithmetic: 14.3 us -> 20.2 us
    unnamed x5 -> x2, waiting for transfers between devices: 27.7 us -> 0.03 us
    all_gather x2 -> x1, waiting for transfers between devices: 37.2 us -> 10.8 us  [local(): lax.all_gather(w_ffn, 'ctx', axis=0, tiled=True, axis_index_groups=groups...]
    ppermute x9 -> x33, starting transfers between devices: 13.3 us -> 38.9 us  [the longest x31 35.9 us: flip(): lax.ppermute(values, 'ctx', [(i, i ^ bit) for i in range(self.count)])]
    ppermute x9 -> x33, waiting for transfers between devices: 31.9 us -> 54.2 us  [the longest x31 49.4 us: flip(): lax.ppermute(values, 'ctx', [(i, i ^ bit) for i in range(self.count)])]
    dot_general x12 -> x5, matrix products: 24.1 us -> 2.59 us  [dot(): lax.dot_general(left, right, (((left_dim,), (right_dim,)), ((), ())), pre...]
    pallas_call x0 -> x5, Pallas kernels: none -> 20.2 us  [the longest x2 8.65 us: attention_call(): pl.pallas_call(functools.partial(kernel, heads), grid=(seqs, ctx // group...]
    all_to_all x5 -> x2, waiting for transfers between devices: 36 us -> 18.4 us  [swap_near(): lax.all_to_all(values, 'ctx', 0, 0, tiled=True, axis_index_groups=self.near)]
    all_to_all x5 -> x2, starting transfers between devices: 18.3 us -> 7 us  [swap_near(): lax.all_to_all(values, 'ctx', 0, 0, tiled=True, axis_index_groups=self.near)]
  transfers between devices with their start and end apart: 22 -> 40, of which waited for: 15 -> 22; matrix products, arithmetic and copies ran while one was open for 19% -> 12% of each run, Pallas kernels for 0% -> 5%
where the time goes in v2:
time: 250 us; the launch traced here: 249 us
  waiting for transfers between devices  89.5 us (36%)
  starting transfers between devices  50.6 us (20%)
  local copies, waits for them, and re-layouts  29 us (12%)
  other arithmetic  20.2 us (8%)
  Pallas kernels  20.2 us (8%)
  blocking collectives  19.5 us (8%)
  between operations  15.4 us (6%)
  matrix products  4.87 us (2%)
    ppermute x31, waiting for transfers between devices, flip(): lax.ppermute(values, 'ctx', [(i, i ^ bit) for i in range(self.count)])  49.4 us
    ppermute x31, starting transfers between devices, flip(): lax.ppermute(values, 'ctx', [(i, i ^ bit) for i in range(self.count)])  35.9 us
    all_gather x2, blocking collectives, spread_near(): whole = lax.all_gather(values, 'ctx', axis=0, axis_index_groups=self.near)  19.5 us
    all_to_all x2, waiting for transfers between devices, swap_near(): lax.all_to_all(values, 'ctx', 0, 0, tiled=True, axis_index_groups=self.near)  18.4 us
    unnamed x113, local copies, waits for them, and re-layouts  16.3 us
    all_gather x1, waiting for transfers between devices, local(): lax.all_gather(w_ffn, 'ctx', axis=0, tiled=True, axis_index_groups=groups...  10.8 us
    pallas_call x2, Pallas kernels, attention_call(): pl.pallas_call(functools.partial(kernel, heads), grid=(seqs, ctx // group...  8.65 us
    all_to_all x2, starting transfers between devices, swap_near(): lax.all_to_all(values, 'ctx', 0, 0, tiled=True, axis_index_groups=self.near)  7 us
  transfers between devices with their start and end apart: 40, of which 22 were waited for; matrix products, arithmetic and copies ran while one was open for 12% of the time, Pallas kernels for 5%

profile of v2, /device:TPU:0, one launch (start us, length us, event | category | flops | bytes accessed | tf_op | source)
XLA Modules:
  0.0 249.3 jit_solution(9463473585958895698)
XLA Ops:
  8.8 1.6 pad_maximum_fusion.7
  10.4 3.0 %collective-permute-start = (bf16[56,1024]{1,0:T(8,128)(2,1)}, bf16[56,1024]{1,0:T(8,128)(2,1)S(1)}, u32[]{:S(2)}, u32[]{:S(2)}) collective-permute-start(bf16[56,1024]{1,0:T(8,128)(2,1)} %pad_maximum_fusion.7), channel_id=1, source_target_pairs={{0,8},{2,10},{4,12},{6,14},{8,0},{10,2},{12,4},{14,6},{16,24},{18,... | collective-permute-start | bytes 344072 | tf_op jit(solution)/shard_map/ppermute | solution.py:69
  13.4 2.6 %collective-permute-start.1 = (bf16[56,1024]{1,0:T(8,128)(2,1)}, bf16[56,1024]{1,0:T(8,128)(2,1)S(1)}, u32[]{:S(2)}, u32[]{:S(2)}) collective-permute-start(bf16[56,1024]{1,0:T(8,128)(2,1)} %pad_maximum_fusion.7), channel_id=1, source_target_pairs={{0,16},{2,18},{4,20},{6,22},{8,24},{10,26},{12,28},{14,30},{16,0},... | collective-permute-start | bytes 344072 | tf_op jit(solution)/shard_map/ppermute | solution.py:69
  19.1 3.5 %all-to-all-start = ((bf16[4,56,1920]{2,1,0:T(8,128)(2,1)}), bf16[4,56,1920]{2,1,0:T(8,128)(2,1)S(1)}, u32[]{:S(2)}, u32[]{:S(2)}) async-start(bf16[4,56,1920]{2,1,0:T(8,128)(2,1)} %maximum_bitcast_fusion), calls=%async_computation | async-start | bytes 1720320 | tf_op jit(solution)/shard_map/all_to_all | solution.py:72
  26.1 8.9 %all-to-all-done = bf16[4,56,1920]{2,1,0:T(8,128)(2,1)S(1)} async-done(((bf16[4,56,1920]{2,1,0:T(8,128)(2,1)}), bf16[4,56,1920]{2,1,0:T(8,128)(2,1)S(1)}, u32[]{:S(2)}, u32[]{:S(2)}) %all-to-all-start) | async-done | bytes 860192 | tf_op jit(solution)/shard_map/all_to_all | solution.py:72
  36.2 10.0 %all-gather = bf16[16,56,576]{2,1,0:T(8,128)(2,1)S(1)} all-gather(bf16[4,56,576]{2,1,0:T(8,128)(2,1)S(1)} %slice.173), channel_id=2, replica_groups={{0,2,4,6},{8,10,12,14},{16,18,20,22},{24,26,28,30},{1,3,5,7},{9,11,13,1..., dimensions={0}, use_global_device_ids=true | all-gather | bytes 1290240 | tf_op jit(solution)/shard_map/all_gather | solution.py:98
  48.7 3.5 %collective-permute-start.4 = (bf16[128,128]{1,0:T(8,128)(2,1)S(1)}, bf16[128,128]{1,0:T(8,128)(2,1)S(1)}, u32[]{:S(2)}, u32[]{:S(2)}) collective-permute-start(bf16[128,128]{1,0:T(8,128)(2,1)S(1)} %get-tuple-element.74), channel_id=1, source_target_pairs={{0,16},{2,18},{4,20},{6,22},{8,24},{10,26},{12,28},{14,30},{16,0},... | collective-permute-start | bytes 98312 | tf_op jit(solution)/shard_map/ppermute | solution.py:69
  52.2 3.1 %collective-permute-done.3 = bf16[128,128]{1,0:T(8,128)(2,1)S(1)} collective-permute-done((bf16[128,128]{1,0:T(8,128)(2,1)S(1)}, bf16[128,128]{1,0:T(8,128)(2,1)S(1)}, u32[]{:S(2)}, u32[]{:S(2)}) %collective-permute-start.3) | collective-permute-done | bytes 32800 | tf_op jit(solution)/shard_map/ppermute | solution.py:69
  55.3 3.5 %collective-permute-done.4 = bf16[128,128]{1,0:T(8,128)(2,1)S(1)} collective-permute-done((bf16[128,128]{1,0:T(8,128)(2,1)S(1)}, bf16[128,128]{1,0:T(8,128)(2,1)S(1)}, u32[]{:S(2)}, u32[]{:S(2)}) %collective-permute-start.4) | collective-permute-done | bytes 32800 | tf_op jit(solution)/shard_map/ppermute | solution.py:69
  61.0 4.1 %collective-permute-done.6 = bf16[4,128,128]{2,1,0:T(8,128)(2,1)S(1)} collective-permute-done((bf16[4,128,128]{2,1,0:T(8,128)(2,1)S(1)}, bf16[4,128,128]{2,1,0:T(8,128)(2,1)S(1)}, u32[]{:S(2)}, u32[]{:S(2)}) %collective-permute-start.6) | collective-permute-done | bytes 131104 | tf_op jit(solution)/shard_map/ppermute | solution.py:69
  65.3 9.6 %all-gather.1 = bf16[16,56,448]{2,1,0:T(8,128)(2,1)S(1)} all-gather(bf16[4,56,448]{2,1,0:T(8,128)(2,1)S(1)} %slice.174), channel_id=3, replica_groups={{0,2,4,6},{8,10,12,14},{16,18,20,22},{24,26,28,30},{1,3,5,7},{9,11,13,1..., dimensions={0}, use_global_device_ids=true | all-gather | bytes 1003520 | tf_op jit(solution)/shard_map/all_gather | solution.py:98
  75.1 3.6 %forward.1 = (bf16[2,64,448]{2,1,0:T(8,128)(2,1)S(1)}, bf16[2,64,896]{2,1,0:T(8,128)(2,1)S(1)}, f32[2,64,448]{2,1,0:T(8,128)S(1)}, f32[2,1,448]{2,1,0:T(1,128)S(1)}) custom-call(bf16[2,64,448]{2,1,0:T(8,128)(2,1)S(1)} %bitcast.210, bf16[16,2,64,128]{3,2,1,0:T(8,128)(2,1)S(1)} %bitcast.200, s32[2,1024,1]{2,1,0:T(8,128)S(1)} %broadcast_add_fusion.key_pos_ref, ...), custom_call_target="tpu_custom_call" | custom-call | flops 469762048 | bytes 1048576 | tf_op jit(solution)/shard_map/forward/pallas_call | solution.py:326
  78.7 1.6 collective-permute-start.8
  80.5 6.2 %collective-permute-done.8 = bf16[128,896]{1,0:T(8,128)(2,1)S(1)} collective-permute-done((bf16[128,896]{1,0:T(8,128)(2,1)S(1)}, bf16[128,896]{1,0:T(8,128)(2,1)S(1)}, u32[]{:S(2)}, u32[]{:S(2)}) %collective-permute-start.8) | collective-permute-done | bytes 229408 | tf_op jit(solution)/shard_map/ppermute | solution.py:52
  88.3 6.0 %collective-permute-done.11 = bf16[128,896]{1,0:T(8,128)(2,1)S(1)} collective-permute-done((bf16[128,896]{1,0:T(8,128)(2,1)S(1)}, bf16[128,896]{1,0:T(8,128)(2,1)S(1)}, u32[]{:S(2)}, u32[]{:S(2)}) %collective-permute-start.11) | collective-permute-done | bytes 229408 | tf_op jit(solution)/shard_map/ppermute | solution.py:69
  97.0 10.8 %all-gather.4.cloned.1.call-done.w_ref = bf16[896,1920]{1,0:T(8,128)(2,1)} async-done(((bf16[224,1920]{1,0:T(8,128)(2,1)}), bf16[896,1920]{1,0:T(8,128)(2,1)}) %all-gather.4.cloned.1.call-update) | async-done | bytes 3440656 | tf_op jit(solution)/shard_map/all_gather | solution.py:511
  111.8 6.9 %ffn.1 = (bf16[2,256,896]{2,1,0:T(8,128)(2,1)S(1)}, bf16[2,256,896]{2,1,0:T(8,128)(2,1)S(1)}, bf16[512,640]{1,0:T(8,128)(2,1)S(1)}, bf16[512,1280]{1,0:T(8,128)(2,1)S(1)}) custom-call(bf16[256,896]{1,0:T(8,128)(2,1)S(1)} %copy-done.6, bf16[256,896]{1,0:T(8,128)(2,1)S(1)} %copy-done.16, bf16[256,896]{1,0:T(8,128)(2,1)S(1)} %copy-done.4, ...), custom_call_target="tpu_custom_call" | custom-call | flops 3523215360 | bytes 7110656 | tf_op jit(solution)/shard_map/ffn/pallas_call | solution.py:382
  119.8 1.8 collective-permute-done.13
  123.2 1.5 collective-permute-start.14
  124.7 4.1 %ffn_grad.1 = bf16[896,1920]{1,0:T(8,128)(2,1)} custom-call(bf16[256,896]{1,0:T(8,128)(2,1)S(1)} %copy-done.6, bf16[256,896]{1,0:T(8,128)(2,1)S(1)} %copy-done.16, bf16[256,896]{1,0:T(8,128)(2,1)S(1)} %copy-done.4, bf16[256,896]{1,0:T(8,128)(2,1)S(1)} %copy-done.14, bf16[512,640]{1,0:T(8,128)(2,1)S(1)} %get-tuple-element.87.active_ref, ...), custom_call_target="tpu_custom_call" | custom-call | flops 1761607680 | bytes 7110656 | tf_op jit(solution)/shard_map/ffn_grad/pallas_call | solution.py:422
  128.7 2.4 collective-permute-done.14
  131.1 1.8 add_convert_fusion.2
  132.9 1.5 collective-permute-start.15
  135.2 4.8 %collective-permute-done.15 = bf16[128,896]{1,0:T(8,128)(2,1)} collective-permute-done((bf16[128,896]{1,0:T(8,128)(2,1)}, bf16[128,896]{1,0:T(8,128)(2,1)}, u32[]{:S(2)}, u32[]{:S(2)}) %collective-permute-start.15) | collective-permute-done | bytes 229408 | tf_op jit(solution)/shard_map/ppermute | solution.py:569
  145.7 5.0 %backward.1 = (f32[2,64,896]{2,1,0:T(8,128)S(1)}, bf16[2,64,896]{2,1,0:T(8,128)(2,1)S(1)}, bf16[2,64,448]{2,1,0:T(8,128)(2,1)S(1)}, bf16[16,2,64,128]{3,2,1,0:T(8,128)(2,1)S(1)}) custom-call(bf16[2,64,448]{2,1,0:T(8,128)(2,1)S(1)} %bitcast.211, bf16[16,2,64,128]{3,2,1,0:T(8,128)(2,1)S(1)} %bitcast.201, s32[2,1024,1]{2,1,0:T(8,128)S(1)} %broadcast_add_fusion.key_pos_ref, ...), custom_call_target="tpu_custom_call" | custom-call | flops 1174405120 | bytes 1048576 | tf_op jit(solution)/shard_map/backward/pallas_call | solution.py:326
  152.7 1.6 copy.77
  154.7 1.5 copy.76
  156.3 2.4 fusion.7
  161.6 1.5 collective-permute-start.17
  163.3 4.0 %collective-permute-done.17 = bf16[4,128,128]{1,2,0:T(8,128)(2,1)S(1)} collective-permute-done((bf16[4,128,128]{1,2,0:T(8,128)(2,1)S(1)}, bf16[4,128,128]{1,2,0:T(8,128)(2,1)S(1)}, u32[]{:S(2)}, u32[]{:S(2)}) %collective-permute-start.17) | collective-permute-done | bytes 131104 | tf_op jit(solution)/shard_map/ppermute | solution.py:69
  168.7 3.1 %collective-permute-start.20 = (bf16[128,128]{0,1:T(8,128)(2,1)S(1)}, bf16[128,128]{0,1:T(8,128)(2,1)S(1)}, u32[]{:S(2)}, u32[]{:S(2)}) collective-permute-start(bf16[128,128]{0,1:T(8,128)(2,1)S(1)} %get-tuple-element.124), channel_id=1, source_target_pairs={{0,24},{2,26},{4,28},{6,30},{8,16},{10,18},{12,20},{14,22},{16,8},... | collective-permute-start | bytes 98312 | tf_op jit(solution)/shard_map/ppermute | solution.py:69
  172.0 1.5 collective-permute-start.22
  173.5 1.5 fusion
  176.5 3.9 %collective-permute-done.22 = bf16[128,896]{1,0:T(8,128)(2,1)S(1)} collective-permute-done((bf16[128,896]{1,0:T(8,128)(2,1)S(1)}, bf16[128,896]{1,0:T(8,128)(2,1)S(1)}, u32[]{:S(2)}, u32[]{:S(2)}) %collective-permute-start.22) | collective-permute-done | bytes 229408 | tf_op jit(solution)/shard_map/ppermute | solution.py:69
  180.5 6.4 %collective-permute-done.24 = bf16[4,56,896]{2,1,0:T(8,128)(2,1)S(1)} collective-permute-done((bf16[4,56,896]{2,1,0:T(8,128)(2,1)S(1)}, bf16[4,56,896]{2,1,0:T(8,128)(2,1)S(1)}, u32[]{:S(2)}, u32[]{:S(2)}) %collective-permute-start.24) | collective-permute-done | bytes 401440 | tf_op jit(solution)/shard_map/ppermute | solution.py:69
  189.0 3.1 %collective-permute-start.35 = (bf16[56,896]{1,0:T(8,128)(2,1)}, bf16[56,896]{1,0:T(8,128)(2,1)}, u32[]{:S(2)}, u32[]{:S(2)}) collective-permute-start(bf16[56,896]{1,0:T(8,128)(2,1)} %get-tuple-element.114), channel_id=1, source_target_pairs={{0,24},{2,26},{4,28},{6,30},{8,16},{10,18},{12,20},{14,22},{16,8},... | collective-permute-start | bytes 301064 | tf_op jit(solution)/shard_map/ppermute | solution.py:69
  193.6 1.7 fusion.1
  195.7 1.6 collective-permute-start.26
  197.3 2.8 %collective-permute-done.33 = bf16[56,896]{1,0:T(8,128)(2,1)} collective-permute-done((bf16[56,896]{1,0:T(8,128)(2,1)}, bf16[56,896]{1,0:T(8,128)(2,1)}, u32[]{:S(2)}, u32[]{:S(2)}) %collective-permute-start.33) | collective-permute-done | bytes 100384 | tf_op jit(solution)/shard_map/ppermute | solution.py:69
  200.1 1.5 collective-permute-start.25
  201.5 4.2 %collective-permute-done.34 = bf16[56,896]{1,0:T(8,128)(2,1)} collective-permute-done((bf16[56,896]{1,0:T(8,128)(2,1)}, bf16[56,896]{1,0:T(8,128)(2,1)}, u32[]{:S(2)}, u32[]{:S(2)}) %collective-permute-start.34) | collective-permute-done | bytes 100384 | tf_op jit(solution)/shard_map/ppermute | solution.py:69
  210.1 2.7 %collective-permute-done.28 = bf16[4,64,256]{2,1,0:T(8,128)(2,1)S(1)} collective-permute-done((bf16[4,64,256]{2,1,0:T(8,128)(2,1)S(1)}, bf16[4,64,256]{2,1,0:T(8,128)(2,1)S(1)}, u32[]{:S(2)}, u32[]{:S(2)}) %collective-permute-start.28) | collective-permute-done | bytes 131104 | tf_op jit(solution)/shard_map/ppermute | solution.py:69
  212.9 3.6 %collective-permute-start.29 = (bf16[64,256]{1,0:T(8,128)(2,1)S(1)}, bf16[64,256]{1,0:T(8,128)(2,1)S(1)}, u32[]{:S(2)}, u32[]{:S(2)}) collective-permute-start(bf16[64,256]{1,0:T(8,128)(2,1)S(1)} %get-tuple-element.120), channel_id=1, source_target_pairs={{0,8},{2,10},{4,12},{6,14},{8,0},{10,2},{12,4},{14,6},{16,24},{18,... | collective-permute-start | bytes 98312 | tf_op jit(solution)/shard_map/ppermute | solution.py:69
  216.6 2.4 collective-permute-start.31
  219.8 1.6 collective-permute-done.30
  222.6 1.5 collective-permute-start.32
  224.2 3.5 %all-to-all-start.1 = ((bf16[4,56,1920]{2,1,0:T(8,128)(2,1)}), bf16[4,56,1920]{2,1,0:T(8,128)(2,1)S(1)}, u32[]{:S(2)}, u32[]{:S(2)}) async-start(bf16[4,56,1920]{2,1,0:T(8,128)(2,1)} %bitcast.234), calls=%async_computation.2 | async-start | bytes 1720320 | tf_op jit(solution)/shard_map/all_to_all | solution.py:72
  230.6 9.5 %all-to-all-done.1 = bf16[4,56,1920]{2,1,0:T(8,128)(2,1)S(1)} async-done(((bf16[4,56,1920]{2,1,0:T(8,128)(2,1)}), bf16[4,56,1920]{2,1,0:T(8,128)(2,1)S(1)}, u32[]{:S(2)}, u32[]{:S(2)}) %all-to-all-start.1) | async-done | bytes 860192 | tf_op jit(solution)/shard_map/all_to_all | solution.py:72
  (284 shorter events, 55.7 us)
Async XLA Ops:
  10.4 15.4 %collective-permute-start = (bf16[56,1024]{1,0:T(8,128)(2,1)}, bf16[56,1024]{1,0:T(8,128)(2,1)S(1)}, u32[]{:S(2)}, u32[]{:S(2)}) collective-permute-start(bf16[56,1024]{1,0:T(8,128)(2,1)} %pad_maximum_fusion.7), channel_id=1, source_target_pairs={{0,8},{2,10},{4,12},{6,14},{8,0},{10,2},{12,4},{14,6},{16,24},{18,... | collective-permute-start | bytes 344072 | tf_op jit(solution)/shard_map/ppermute | solution.py:69
  13.4 12.4 %collective-permute-start.1 = (bf16[56,1024]{1,0:T(8,128)(2,1)}, bf16[56,1024]{1,0:T(8,128)(2,1)S(1)}, u32[]{:S(2)}, u32[]{:S(2)}) collective-permute-start(bf16[56,1024]{1,0:T(8,128)(2,1)} %pad_maximum_fusion.7), channel_id=1, source_target_pairs={{0,16},{2,18},{4,20},{6,22},{8,24},{10,26},{12,28},{14,30},{16,0},... | collective-permute-start | bytes 344072 | tf_op jit(solution)/shard_map/ppermute | solution.py:69
  16.0 9.8 %collective-permute-start.2 = (bf16[56,1024]{1,0:T(8,128)(2,1)}, bf16[56,1024]{1,0:T(8,128)(2,1)S(1)}, u32[]{:S(2)}, u32[]{:S(2)}) collective-permute-start(bf16[56,1024]{1,0:T(8,128)(2,1)} %pad_maximum_fusion.7), channel_id=1, source_target_pairs={{0,24},{2,26},{4,28},{6,30},{8,16},{10,18},{12,20},{14,22},{16,8},... | collective-permute-start | bytes 344072 | tf_op jit(solution)/shard_map/ppermute | solution.py:69
  19.1 15.9 %all-to-all-start = ((bf16[4,56,1920]{2,1,0:T(8,128)(2,1)}), bf16[4,56,1920]{2,1,0:T(8,128)(2,1)S(1)}, u32[]{:S(2)}, u32[]{:S(2)}) async-start(bf16[4,56,1920]{2,1,0:T(8,128)(2,1)} %maximum_bitcast_fusion), calls=%async_computation | async-start | bytes 1720320 | tf_op jit(solution)/shard_map/all_to_all | solution.py:72
  22.6 85.1 %all-gather.4.cloned.1.call-start = ((), (), s32[]{:S(2)}) async-start(), calls=%async_computation.3 | async-start | bytes 4300800 | tf_op jit(solution)/shard_map/all_gather | solution.py:511
  26.1 20.0 %copy-start.34 = (bf16[2,2,56,1024]{3,2,1,0:T(8,128)(2,1)}, bf16[2,2,56,1024]{3,2,1,0:T(8,128)(2,1)S(1)}, u32[]{:S(2)}) copy-start(bf16[2,2,56,1024]{3,2,1,0:T(8,128)(2,1)S(1)} %reverse_select_fusion) | copy-start | bytes 1376260
  36.0 188.2 %reduce-scatter.2.cloned.1.call-start = ((), (), s32[]{:S(2)}) async-start(), calls=%async_computation.4 | async-start | bytes 4300800 | tf_op jit(solution)/shard_map/reduce_scatter | solution.py:570
  46.4 18.8 %copy-start.19 = (f32[128,128]{1,0:T(8,128)}, f32[128,128]{1,0:T(8,128)S(1)}, u32[]{:S(2)}) copy-start(f32[128,128]{1,0:T(8,128)S(1)} %copy.67.cosine_ref) | copy-start | bytes 196612
  46.5 28.4 %copy-start.21 = (f32[128,128]{1,0:T(8,128)}, f32[128,128]{1,0:T(8,128)S(1)}, u32[]{:S(2)}) copy-start(f32[128,128]{1,0:T(8,128)S(1)} %copy.68.sine_ref) | copy-start | bytes 196612
  47.7 27.2 %copy-start.9 = (bf16[128,896]{1,0:T(8,128)(2,1)}, bf16[128,896]{1,0:T(8,128)(2,1)S(1)}, u32[]{:S(2)}) copy-start(bf16[128,896]{1,0:T(8,128)(2,1)S(1)} %get-tuple-element.94) | copy-start | bytes 688132
  47.7 27.4 %copy-start.25 = (bf16[128,448]{1,0:T(8,128)(2,1)}, bf16[128,448]{1,0:T(8,128)(2,1)S(1)}, u32[]{:S(2)}) copy-start(bf16[128,448]{1,0:T(8,128)(2,1)S(1)} %get-tuple-element.73) | copy-start | bytes 344068
  47.7 7.6 %collective-permute-start.3 = (bf16[128,128]{1,0:T(8,128)(2,1)S(1)}, bf16[128,128]{1,0:T(8,128)(2,1)S(1)}, u32[]{:S(2)}, u32[]{:S(2)}) collective-permute-start(bf16[128,128]{1,0:T(8,128)(2,1)S(1)} %get-tuple-element.74), channel_id=1, source_target_pairs={{0,8},{2,10},{4,12},{6,14},{8,0},{10,2},{12,4},{14,6},{16,24},{18,... | collective-permute-start | bytes 98312 | tf_op jit(solution)/shard_map/ppermute | solution.py:69
  48.7 10.1 %collective-permute-start.4 = (bf16[128,128]{1,0:T(8,128)(2,1)S(1)}, bf16[128,128]{1,0:T(8,128)(2,1)S(1)}, u32[]{:S(2)}, u32[]{:S(2)}) collective-permute-start(bf16[128,128]{1,0:T(8,128)(2,1)S(1)} %get-tuple-element.74), channel_id=1, source_target_pairs={{0,16},{2,18},{4,20},{6,22},{8,24},{10,26},{12,28},{14,30},{16,0},... | collective-permute-start | bytes 98312 | tf_op jit(solution)/shard_map/ppermute | solution.py:69
  52.1 6.6 %collective-permute-start.5 = (bf16[128,128]{1,0:T(8,128)(2,1)S(1)}, bf16[128,128]{1,0:T(8,128)(2,1)S(1)}, u32[]{:S(2)}, u32[]{:S(2)}) collective-permute-start(bf16[128,128]{1,0:T(8,128)(2,1)S(1)} %get-tuple-element.74), channel_id=1, source_target_pairs={{0,24},{2,26},{4,28},{6,30},{8,16},{10,18},{12,20},{14,22},{16,8},... | collective-permute-start | bytes 98312 | tf_op jit(solution)/shard_map/ppermute | solution.py:69
  58.8 6.4 %collective-permute-start.6 = (bf16[4,128,128]{2,1,0:T(8,128)(2,1)S(1)}, bf16[4,128,128]{2,1,0:T(8,128)(2,1)S(1)}, u32[]{:S(2)}, u32[]{:S(2)}) collective-permute-start(bf16[4,128,128]{2,1,0:T(8,128)(2,1)S(1)} %get-tuple-element.127), channel_id=1, source_target_pairs={{0,4},{2,6},{4,0},{6,2},{8,12},{10,14},{12,8},{14,10},{16,20},{18,... | collective-permute-start | bytes 393224 | tf_op jit(solution)/shard_map/ppermute | solution.py:69
  59.9 20.4 %collective-permute-start.9 = (bf16[128,896]{1,0:T(8,128)(2,1)S(1)}, bf16[128,896]{1,0:T(8,128)(2,1)S(1)}, u32[]{:S(2)}, u32[]{:S(2)}) collective-permute-start(bf16[128,896]{1,0:T(8,128)(2,1)S(1)} %bitcast.207), channel_id=1, source_target_pairs={{0,4},{2,6},{4,0},{6,2},{8,12},{10,14},{12,8},{14,10},{16,20},{18,... | collective-permute-start | bytes 688136 | tf_op jit(solution)/shard_map/ppermute | solution.py:69
  65.2 9.8 %collective-permute-start.7 = (bf16[2,4,128,128]{3,2,1,0:T(8,128)(2,1)S(1)}, bf16[2,4,128,128]{3,2,1,0:T(8,128)(2,1)S(1)}, u32[]{:S(2)}, u32[]{:S(2)}) collective-permute-start(bf16[2,4,128,128]{3,2,1,0:T(8,128)(2,1)S(1)} %get-tuple-element.117), channel_id=1, source_target_pairs={{0,2},{2,0},{4,6},{6,4},{8,10},{10,8},{12,14},{14,12},{16,18},{18,... | collective-permute-start | bytes 786440 | tf_op jit(solution)/shard_map/ppermute | solution.py:69
  78.7 7.9 %collective-permute-start.8 = (bf16[128,896]{1,0:T(8,128)(2,1)S(1)}, bf16[128,896]{1,0:T(8,128)(2,1)S(1)}, u32[]{:S(2)}, u32[]{:S(2)}) collective-permute-start(bf16[128,896]{1,0:T(8,128)(2,1)S(1)} %bitcast.209), channel_id=1, source_target_pairs={{0,1},{1,0},{2,3},{3,2},{4,5},{5,4},{6,7},{7,6},{8,9},{9,8},{10,11... | collective-permute-start | bytes 688136 | tf_op jit(solution)/shard_map/ppermute | solution.py:52
  80.4 6.4 %collective-permute-start.10 = (bf16[256,896]{1,0:T(8,128)(2,1)S(1)}, bf16[256,896]{1,0:T(8,128)(2,1)S(1)}, u32[]{:S(2)}, u32[]{:S(2)}) collective-permute-start(bf16[256,896]{1,0:T(8,128)(2,1)S(1)} %pad_maximum_fusion.2.grad_one), channel_id=1, source_target_pairs={{0,2},{2,0},{4,6},{6,4},{8,10},{10,8},{12,14},{14,12},{16,18},{18,... | collective-permute-start | bytes 1376264 | tf_op jit(solution)/shard_map/ppermute | solution.py:69
  86.9 31.8 %copy-start.47 = (f32[128]{0:T(128)}, f32[128]{0:T(128)S(1)}, u32[]{:S(2)}) copy-start(f32[128]{0:T(128)S(1)} %add_rsqrt_fusion.1) | copy-start | bytes 1540
  87.0 7.2 %collective-permute-start.11 = (bf16[128,896]{1,0:T(8,128)(2,1)S(1)}, bf16[128,896]{1,0:T(8,128)(2,1)S(1)}, u32[]{:S(2)}, u32[]{:S(2)}) collective-permute-start(bf16[128,896]{1,0:T(8,128)(2,1)S(1)} %multiply_convert_fusion.2), channel_id=1, source_target_pairs={{0,4},{2,6},{4,0},{6,2},{8,12},{10,14},{12,8},{14,10},{16,20},{18,... | collective-permute-start | bytes 688136 | tf_op jit(solution)/shard_map/ppermute | solution.py:69
  94.3 1.9 collective-permute-start.12
  119.7 1.9 collective-permute-start.13
  123.2 8.0 %collective-permute-start.14 = (bf16[128,896]{1,0:T(8,128)(2,1)}, bf16[128,896]{1,0:T(8,128)(2,1)}, u32[]{:S(2)}, u32[]{:S(2)}) collective-permute-start(bf16[128,896]{1,0:T(8,128)(2,1)} %slice.219), channel_id=1, source_target_pairs={{0,4},{2,6},{4,0},{6,2},{8,12},{10,14},{12,8},{14,10},{16,20},{18,... | collective-permute-start | bytes 688136 | tf_op jit(solution)/shard_map/ppermute | solution.py:69
  132.9 7.1 %collective-permute-start.15 = (bf16[128,896]{1,0:T(8,128)(2,1)}, bf16[128,896]{1,0:T(8,128)(2,1)}, u32[]{:S(2)}, u32[]{:S(2)}) collective-permute-start(bf16[128,896]{1,0:T(8,128)(2,1)} %add_convert_fusion.2), channel_id=1, source_target_pairs={{0,1},{1,0},{2,3},{3,2},{4,5},{5,4},{6,7},{7,6},{8,9},{9,8},{10,11... | collective-permute-start | bytes 688136 | tf_op jit(solution)/shard_map/ppermute | solution.py:569
  158.6 14.9 %collective-permute-start.23 = (bf16[4,2,56,896]{3,2,1,0:T(8,128)(2,1)}, bf16[4,2,56,896]{3,2,1,0:T(8,128)(2,1)}, u32[]{:S(2)}, u32[]{:S(2)}) collective-permute-start(bf16[4,2,56,896]{3,2,1,0:T(8,128)(2,1)} %fusion.7), channel_id=1, source_target_pairs={{0,2},{2,0},{4,6},{6,4},{8,10},{10,8},{12,14},{14,12},{16,18},{18,... | collective-permute-start | bytes 2408456 | tf_op jit(solution)/shard_map/ppermute | solution.py:69
  159.5 2.0 collective-permute-start.16
  161.6 5.7 %collective-permute-start.17 = (bf16[4,128,128]{1,2,0:T(8,128)(2,1)S(1)}, bf16[4,128,128]{1,2,0:T(8,128)(2,1)S(1)}, u32[]{:S(2)}, u32[]{:S(2)}) collective-permute-start(bf16[4,128,128]{1,2,0:T(8,128)(2,1)S(1)} %fusion.35), channel_id=1, source_target_pairs={{0,4},{2,6},{4,0},{6,2},{8,12},{10,14},{12,8},{14,10},{16,20},{18,... | collective-permute-start | bytes 393224 | tf_op jit(solution)/shard_map/ppermute | solution.py:69
  163.2 8.6 %collective-permute-start.21 = (bf16[256,896]{1,0:T(8,128)(2,1)S(1)}, bf16[256,896]{1,0:T(8,128)(2,1)S(1)}, u32[]{:S(2)}, u32[]{:S(2)}) collective-permute-start(bf16[256,896]{1,0:T(8,128)(2,1)S(1)} %slice_bitcast_fusion.4), channel_id=1, source_target_pairs={{0,2},{2,0},{4,6},{6,4},{8,10},{10,8},{12,14},{14,12},{16,18},{18,... | collective-permute-start | bytes 1376264 | tf_op jit(solution)/shard_map/ppermute | solution.py:69
  167.4 8.3 %collective-permute-start.18 = (bf16[128,128]{0,1:T(8,128)(2,1)S(1)}, bf16[128,128]{0,1:T(8,128)(2,1)S(1)}, u32[]{:S(2)}, u32[]{:S(2)}) collective-permute-start(bf16[128,128]{0,1:T(8,128)(2,1)S(1)} %get-tuple-element.123), channel_id=1, source_target_pairs={{0,8},{2,10},{4,12},{6,14},{8,0},{10,2},{12,4},{14,6},{16,24},{18,... | collective-permute-start | bytes 98312 | tf_op jit(solution)/shard_map/ppermute | solution.py:69
  167.5 9.0 %collective-permute-start.19 = (bf16[128,128]{0,1:T(8,128)(2,1)S(1)}, bf16[128,128]{0,1:T(8,128)(2,1)S(1)}, u32[]{:S(2)}, u32[]{:S(2)}) collective-permute-start(bf16[128,128]{0,1:T(8,128)(2,1)S(1)} %get-tuple-element.125), channel_id=1, source_target_pairs={{0,16},{2,18},{4,20},{6,22},{8,24},{10,26},{12,28},{14,30},{16,0},... | collective-permute-start | bytes 98312 | tf_op jit(solution)/shard_map/ppermute | solution.py:69
  168.7 7.8 %collective-permute-start.20 = (bf16[128,128]{0,1:T(8,128)(2,1)S(1)}, bf16[128,128]{0,1:T(8,128)(2,1)S(1)}, u32[]{:S(2)}, u32[]{:S(2)}) collective-permute-start(bf16[128,128]{0,1:T(8,128)(2,1)S(1)} %get-tuple-element.124), channel_id=1, source_target_pairs={{0,24},{2,26},{4,28},{6,30},{8,16},{10,18},{12,20},{14,22},{16,8},... | collective-permute-start | bytes 98312 | tf_op jit(solution)/shard_map/ppermute | solution.py:69
  172.0 8.4 %collective-permute-start.22 = (bf16[128,896]{1,0:T(8,128)(2,1)S(1)}, bf16[128,896]{1,0:T(8,128)(2,1)S(1)}, u32[]{:S(2)}, u32[]{:S(2)}) collective-permute-start(bf16[128,896]{1,0:T(8,128)(2,1)S(1)} %slice.227), channel_id=1, source_target_pairs={{0,4},{2,6},{4,0},{6,2},{8,12},{10,14},{12,8},{14,10},{16,20},{18,... | collective-permute-start | bytes 688136 | tf_op jit(solution)/shard_map/ppermute | solution.py:69
  175.1 17.1 %copy-start.41 = (f32[128,2,64]{0,2,1:T(8,128)S(1)}, f32[128,2,64]{0,2,1:T(8,128)}, u32[]{:S(2)}) copy-start(f32[128,2,64]{0,2,1:T(8,128)} %copy-done.40) | copy-start | bytes 196612
  175.1 17.0 %copy-start.39 = (f32[128,2,64]{0,2,1:T(8,128)S(1)}, f32[128,2,64]{0,2,1:T(8,128)}, u32[]{:S(2)}) copy-start(f32[128,2,64]{0,2,1:T(8,128)} %copy-done.38) | copy-start | bytes 196612
  175.1 11.7 %collective-permute-start.24 = (bf16[4,56,896]{2,1,0:T(8,128)(2,1)S(1)}, bf16[4,56,896]{2,1,0:T(8,128)(2,1)S(1)}, u32[]{:S(2)}, u32[]{:S(2)}) collective-permute-start(bf16[4,56,896]{2,1,0:T(8,128)(2,1)S(1)} %dynamic-slice_bitcast_fusion), channel_id=1, source_target_pairs={{0,4},{2,6},{4,0},{6,2},{8,12},{10,14},{12,8},{14,10},{16,20},{18,... | collective-permute-start | bytes 1204232 | tf_op jit(solution)/shard_map/ppermute | solution.py:69
  187.7 12.3 %collective-permute-start.33 = (bf16[56,896]{1,0:T(8,128)(2,1)}, bf16[56,896]{1,0:T(8,128)(2,1)}, u32[]{:S(2)}, u32[]{:S(2)}) collective-permute-start(bf16[56,896]{1,0:T(8,128)(2,1)} %get-tuple-element.113), channel_id=1, source_target_pairs={{0,8},{2,10},{4,12},{6,14},{8,0},{10,2},{12,4},{14,6},{16,24},{18,... | collective-permute-start | bytes 301064 | tf_op jit(solution)/shard_map/ppermute | solution.py:69
  187.7 17.9 %collective-permute-start.34 = (bf16[56,896]{1,0:T(8,128)(2,1)}, bf16[56,896]{1,0:T(8,128)(2,1)}, u32[]{:S(2)}, u32[]{:S(2)}) collective-permute-start(bf16[56,896]{1,0:T(8,128)(2,1)} %get-tuple-element.115), channel_id=1, source_target_pairs={{0,16},{2,18},{4,20},{6,22},{8,24},{10,26},{12,28},{14,30},{16,0},... | collective-permute-start | bytes 301064 | tf_op jit(solution)/shard_map/ppermute | solution.py:69
  189.0 16.7 %collective-permute-start.35 = (bf16[56,896]{1,0:T(8,128)(2,1)}, bf16[56,896]{1,0:T(8,128)(2,1)}, u32[]{:S(2)}, u32[]{:S(2)}) collective-permute-start(bf16[56,896]{1,0:T(8,128)(2,1)} %get-tuple-element.114), channel_id=1, source_target_pairs={{0,24},{2,26},{4,28},{6,30},{8,16},{10,18},{12,20},{14,22},{16,8},... | collective-permute-start | bytes 301064 | tf_op jit(solution)/shard_map/ppermute | solution.py:69
  195.6 12.1 %collective-permute-start.27 = (bf16[4,2,64,256]{3,2,1,0:T(8,128)(2,1)S(1)}, bf16[4,2,64,256]{3,2,1,0:T(8,128)(2,1)S(1)}, u32[]{:S(2)}, u32[]{:S(2)}) collective-permute-start(bf16[4,2,64,256]{3,2,1,0:T(8,128)(2,1)S(1)} %fusion.26), channel_id=1, source_target_pairs={{0,2},{2,0},{4,6},{6,4},{8,10},{10,8},{12,14},{14,12},{16,18},{18,... | collective-permute-start | bytes 786440 | tf_op jit(solution)/shard_map/ppermute | solution.py:69
  195.7 11.8 %collective-permute-start.26 = (bf16[128,896]{1,0:T(8,128)(2,1)S(1)}, bf16[128,896]{1,0:T(8,128)(2,1)S(1)}, u32[]{:S(2)}, u32[]{:S(2)}) collective-permute-start(bf16[128,896]{1,0:T(8,128)(2,1)S(1)} %get-tuple-element.112), channel_id=1, source_target_pairs={{0,1},{1,0},{2,3},{3,2},{4,5},{5,4},{6,7},{7,6},{8,9},{9,8},{10,11... | collective-permute-start | bytes 688136 | tf_op jit(solution)/shard_map/ppermute | solution.py:52
  200.1 19.0 %collective-permute-start.25 = (bf16[128,896]{1,0:T(8,128)(2,1)S(1)}, bf16[128,896]{1,0:T(8,128)(2,1)S(1)}, u32[]{:S(2)}, u32[]{:S(2)}) collective-permute-start(bf16[128,896]{1,0:T(8,128)(2,1)S(1)} %add_convert_fusion.1), channel_id=1, source_target_pairs={{0,1},{1,0},{2,3},{3,2},{4,5},{5,4},{6,7},{7,6},{8,9},{9,8},{10,11... | collective-permute-start | bytes 688136 | tf_op jit(solution)/shard_map/ppermute | solution.py:52
  207.8 5.0 %collective-permute-start.28 = (bf16[4,64,256]{2,1,0:T(8,128)(2,1)S(1)}, bf16[4,64,256]{2,1,0:T(8,128)(2,1)S(1)}, u32[]{:S(2)}, u32[]{:S(2)}) collective-permute-start(bf16[4,64,256]{2,1,0:T(8,128)(2,1)S(1)} %dynamic-slice_bitcast_fusion.1), channel_id=1, source_target_pairs={{0,4},{2,6},{4,0},{6,2},{8,12},{10,14},{12,8},{14,10},{16,20},{18,... | collective-permute-start | bytes 393224 | tf_op jit(solution)/shard_map/ppermute | solution.py:69
  212.9 6.9 %collective-permute-start.29 = (bf16[64,256]{1,0:T(8,128)(2,1)S(1)}, bf16[64,256]{1,0:T(8,128)(2,1)S(1)}, u32[]{:S(2)}, u32[]{:S(2)}) collective-permute-start(bf16[64,256]{1,0:T(8,128)(2,1)S(1)} %get-tuple-element.120), channel_id=1, source_target_pairs={{0,8},{2,10},{4,12},{6,14},{8,0},{10,2},{12,4},{14,6},{16,24},{18,... | collective-permute-start | bytes 98312 | tf_op jit(solution)/shard_map/ppermute | solution.py:69
  216.6 4.8 %collective-permute-start.30 = (bf16[64,256]{1,0:T(8,128)(2,1)S(1)}, bf16[64,256]{1,0:T(8,128)(2,1)S(1)}, u32[]{:S(2)}, u32[]{:S(2)}) collective-permute-start(bf16[64,256]{1,0:T(8,128)(2,1)S(1)} %get-tuple-element.122), channel_id=1, source_target_pairs={{0,16},{2,18},{4,20},{6,22},{8,24},{10,26},{12,28},{14,30},{16,0},... | collective-permute-start | bytes 98312 | tf_op jit(solution)/shard_map/ppermute | solution.py:69
  216.6 5.7 %collective-permute-start.31 = (bf16[64,256]{1,0:T(8,128)(2,1)S(1)}, bf16[64,256]{1,0:T(8,128)(2,1)S(1)}, u32[]{:S(2)}, u32[]{:S(2)}) collective-permute-start(bf16[64,256]{1,0:T(8,128)(2,1)S(1)} %get-tuple-element.121), channel_id=1, source_target_pairs={{0,24},{2,26},{4,28},{6,30},{8,16},{10,18},{12,20},{14,22},{16,8},... | collective-permute-start | bytes 98312 | tf_op jit(solution)/shard_map/ppermute | solution.py:69
  222.6 7.5 %collective-permute-start.32 = (f32[56]{0:T(128)S(1)}, f32[56]{0:T(128)S(1)}, u32[]{:S(2)}, u32[]{:S(2)}) collective-permute-start(f32[56]{0:T(128)S(1)} %convert_divide_fusion), channel_id=1, source_target_pairs={{0,1},{1,0},{2,3},{3,2},{4,5},{5,4},{6,7},{7,6},{8,9},{9,8},{10,11... | collective-permute-start | bytes 680 | tf_op jit(solution)/shard_map/ppermute | solution.py:668
  224.2 15.9 %all-to-all-start.1 = ((bf16[4,56,1920]{2,1,0:T(8,128)(2,1)}), bf16[4,56,1920]{2,1,0:T(8,128)(2,1)S(1)}, u32[]{:S(2)}, u32[]{:S(2)}) async-start(bf16[4,56,1920]{2,1,0:T(8,128)(2,1)} %bitcast.234), calls=%async_computation.2 | async-start | bytes 1720320 | tf_op jit(solution)/shard_map/all_to_all | solution.py:72
  (47 other events, 268.3 us)
Sparse Core Ops, SparseCore 0:
  36.1 71.5 all-gather.3
  135.4 70.8 reduce-scatter.1

commit v3 on v2

v3 whole, which is shorter than its diff:
```python
import functools

import jax
import jax.numpy as jnp
from jax import lax
from jax.experimental import pallas as pl
from jax.experimental.pallas import tpu as pltpu
from jax.sharding import PartitionSpec as P

HEAD = 64


EPSILON = 1e-06
ROPE_BASE = 1000000.0
MASKED = -1e30
LOWEST = -1e29
BRIEF = pl.CostEstimate(flops=1, bytes_accessed=1, transcendentals=0)
VMEM_LIMIT = 48 * 1024 * 1024


def rope_tables(positions, head_dim):
    halfway = head_dim // 2
    inverse = ROPE_BASE ** (-(jnp.arange(halfway, dtype=jnp.float32) * 2.0 / head_dim))
    angles = positions.astype(jnp.float32)[..., None] * inverse
    angles = jnp.concatenate([angles, angles], axis=-1)
    return (jnp.cos(angles), jnp.sin(angles))


def norm_apply(values):
    factor = lax.rsqrt(jnp.mean(values * values, axis=-1, keepdims=True) + EPSILON)
    return values * factor, factor


def norm_back(values, factor, weighted):
    inner = jnp.mean(weighted * values, axis=-1, keepdims=True)
    return factor * weighted - values * factor * factor * factor * inner


def dot(left, right, left_dim, right_dim):
    return lax.dot_general(
        left, right, (((left_dim,), (right_dim,)), ((), ())), preferred_element_type=jnp.float32
    )


def sum_tp(values):
    other = lax.ppermute(values, "tp", [(0, 1), (1, 0)])
    return values.astype(jnp.float32) + other.astype(jnp.float32)


def together(*values):
    return lax.optimization_barrier(values)


class Groups:
    def __init__(self, count):
        self.count = count
        self.low = 4
        self.high = count // self.low
        self.near = [[base + here for here in range(4)] for base in range(0, count, 4)]
        self.far = [list(group) for group in zip(*self.near)]
        self.far_bits = list(range(0, count, 4))

    def flip(self, values, bit):
        return lax.ppermute(values, "ctx", [(i, i ^ bit) for i in range(self.count)])

    def swap_near(self, values):
        return lax.all_to_all(values, "ctx", 0, 0, tiled=True, axis_index_groups=self.near)

    def gather_near(self, values):
        first = jnp.concatenate([values, self.flip(values, 2)], axis=0)
        return first, self.flip(first, 1)

    def far_flips(self, values):
        return jnp.stack([values] + [self.flip(values, bits) for bits in self.far_bits[1:]])


    def gather_far(self, values, place):
        if self.high != 4:
            return lax.all_gather(values, "ctx", axis=0, axis_index_groups=self.far)
        far = self.far_flips(values).reshape((2, 2) + values.shape)
        far = jnp.where(place // 8 % 2 == 1, far[::-1], far)
        far = jnp.where(place // 4 % 2 == 1, far[:, ::-1], far)
        return far.reshape((4,) + values.shape)

    def spread_near(self, values):
        whole = lax.all_gather(values, "ctx", axis=0, axis_index_groups=self.near)
        whole = jnp.swapaxes(whole, 0, 1)
        return whole.reshape((self.count * values.shape[1],) + values.shape[2:])

    def flip_near(self, values, place):
        other = self.flip(values, 2)
        upper = place // 2 % 2 == 1
        both = jnp.stack([jnp.where(upper, other, values), jnp.where(upper, values, other)], axis=1)
        other = self.flip(both, 1)
        upper = place % 2 == 1
        whole = jnp.stack([jnp.where(upper, other, both), jnp.where(upper, both, other)], axis=2)
        return whole.reshape((self.count * values.shape[1],) + values.shape[2:])

    def far_owner(self, pieces, place):
        if self.high != 4:
            shape = pieces.shape
            pieces = pieces.reshape((shape[0] * shape[1],) + shape[2:])
            return lax.psum_scatter(
                pieces, "ctx", scatter_dimension=0, tiled=True, axis_index_groups=self.far
            ).astype(jnp.float32)
        group = place // self.low
        total = lax.dynamic_index_in_dim(pieces, group, 0, False).astype(jnp.float32)
        for m in range(1, self.high):
            sent = lax.dynamic_index_in_dim(pieces, group ^ m, 0, False)
            total = total + self.flip(sent, self.far_bits[m]).astype(jnp.float32)
        return total


def add(one, two):
    return (one.astype(jnp.float32) + two.astype(jnp.float32)).astype(jnp.bfloat16)


def halve(groups, pieces, bit, place, axis):
    mine = place // bit % 2
    kept = lax.dynamic_index_in_dim(pieces, mine, axis, False).astype(jnp.float32)
    sent = groups.flip(lax.dynamic_index_in_dim(pieces, 1 - mine, axis, False), bit)
    return (kept + sent.astype(jnp.float32)).astype(jnp.bfloat16)


def stack_heads(flat, heads, upper):
    tall = jnp.concatenate([flat[:, h * HEAD : (h + 1) * HEAD] for h in range(heads)], axis=0)
    blank = jnp.zeros_like(tall)
    return jnp.concatenate([blank, tall] if upper else [tall, blank], axis=1)


def flat_heads(tall, heads):
    rows = tall.shape[0] // heads
    return jnp.concatenate([tall[h * rows : (h + 1) * rows] for h in range(heads)], axis=1)


def masked_scores(pair, wide, key_pos, query_pos):
    return jnp.where(key_pos <= query_pos, dot(pair, wide, 1, 1), MASKED)


def first_half(shape):
    return lax.broadcasted_iota(jnp.int32, shape, 1) % HEAD < HEAD // 2


def turn(values):
    width = values.shape[1]
    return jnp.where(
        first_half(values.shape),
        pltpu.roll(values, width - HEAD // 2, 1),
        pltpu.roll(values, HEAD // 2, 1),
    )


def widen(table, width):
    return jnp.concatenate([table] * (width // table.shape[1]), axis=1)


def project_kernel(
    heads, token_ref, w_ref, bias_ref, cosine_ref, sine_ref, normed_ref, query_ref, pair_ref
):
    normed, _ = norm_apply(token_ref[...].astype(jnp.float32))
    normed = normed.astype(jnp.bfloat16)
    normed_ref[...] = normed
    lin = dot(normed, w_ref[...], 1, 0) + bias_ref[...]
    width = (heads + 1) * HEAD
    some = lin[:, :width]
    turned = turn(some)
    turned = jnp.where(first_half(some.shape), -turned, turned)
    rotated = some * widen(cosine_ref[...], width) + turned * widen(sine_ref[...], width)
    rotated = rotated.astype(jnp.bfloat16)
    query_ref[...] = rotated[:, : heads * HEAD] * jnp.bfloat16(HEAD ** (-0.5))
    pair_ref[...] = jnp.concatenate(
        [rotated[:, heads * HEAD :], lin[:, width:].astype(jnp.bfloat16)], axis=1
    )


def whole_call(kernel, name, inputs, out_shape, scratch=(), place=None):
    whole = pl.BlockSpec(memory_space=pltpu.VMEM)
    in_specs = [whole] * len(inputs)
    if place is not None:
        inputs = (place.astype(jnp.int32)[None], *inputs)
        in_specs = [pl.BlockSpec(memory_space=pltpu.SMEM)] + in_specs
    return pl.pallas_call(
        kernel,
        in_specs=in_specs,
        out_specs=[whole] * len(out_shape),
        out_shape=out_shape,
        scratch_shapes=list(scratch),
        compiler_params=pltpu.CompilerParams(vmem_limit_bytes=VMEM_LIMIT),
        cost_estimate=BRIEF,
        name=name,
    )(*inputs)


def when(flag):
    if isinstance(flag, bool):
        return lambda body: body() if flag else None
    return pl.when(flag)


def forward_kernel(
    heads,
    steps,
    query_ref,
    pair_ref,
    key_pos_ref,
    query_pos_ref,
    w_out_ref,
    flat_ref,
    part_ref,
    out_ref,
    log_ref,
    best_ref,
    total_ref,
    sum_ref,
):
    step = 0 if steps == 1 else pl.program_id(1)
    for s in range(query_ref.shape[0]):

        @when(step == 0)
        def _():
            best_ref[s] = jnp.full(best_ref.shape[1:], LOWEST, jnp.float32)
            total_ref[s] = jnp.zeros(total_ref.shape[1:], jnp.float32)
            sum_ref[s] = jnp.zeros(sum_ref.shape[1:], jnp.float32)

        pair = pair_ref[:, s].reshape(-1, 2 * HEAD)
        wide = stack_heads(query_ref[s], heads, False)
        scores = masked_scores(pair, wide, key_pos_ref[s], query_pos_ref[s])
        best = best_ref[s]
        newest = jnp.maximum(best, jnp.max(scores, axis=0, keepdims=True))
        raised = jnp.exp(scores - newest)
        fading = jnp.exp(best - newest)
        best_ref[s] = newest
        total_ref[s] = total_ref[s] * fading + jnp.sum(raised, axis=0, keepdims=True)
        sum_ref[s] = sum_ref[s] * fading + dot(pair, raised.astype(jnp.bfloat16), 0, 0)

        @when(step == steps - 1)
        def _():
            out = sum_ref[s, HEAD:, :] / total_ref[s]
            if steps > 1:
                out_ref[s] = out
            log_ref[s] = best_ref[s] + jnp.log(total_ref[s])
            flat = flat_heads(out.T, heads).astype(jnp.bfloat16)
            flat_ref[s] = flat
            part_ref[s] = dot(flat, w_out_ref[...], 1, 1).astype(jnp.bfloat16)


def backward_kernel(
    heads,
    steps,
    query_ref,
    pair_ref,
    key_pos_ref,
    query_pos_ref,
    out_ref,
    log_ref,
    w_out_ref,
    own_ref,
    other_ref,
    hidden_ref,
    cotangent_ref,
    cosine_ref,
    sine_ref,
    d_hidden_ref,
    d_low_ref,
    d_query_ref,
    d_pair_ref,
    d_out_ref,
    dots_ref,
    sum_ref,
):
    step = 0 if steps == 1 else pl.program_id(1)
    for s in range(query_ref.shape[0]):

        @when(step == 0)
        def _():
            sum_ref[s] = jnp.zeros(sum_ref.shape[1:], jnp.float32)
            hidden = hidden_ref[s]
            weighted = own_ref[s].astype(jnp.float32) + other_ref[s].astype(jnp.float32)
            _, scale = norm_apply(hidden)
            d_hidden = cotangent_ref[s].astype(jnp.float32) + norm_back(hidden, scale, weighted)
            d_hidden_ref[s] = d_hidden
            low = d_hidden.astype(jnp.bfloat16)
            d_low_ref[s] = low
            flat = dot(low, w_out_ref[...], 1, 0).astype(jnp.bfloat16)
            d_out = stack_heads(flat, heads, True)
            d_out_ref[s] = d_out
            if steps > 1:
                dots_ref[s] = jnp.sum(
                    d_out[:, HEAD:].astype(jnp.float32).T * out_ref[s], axis=0, keepdims=True
                )

        pair = pair_ref[:, s].reshape(-1, 2 * HEAD)
        wide = stack_heads(query_ref[s], heads, False)
        d_out = d_out_ref[s]
        scores = masked_scores(pair, wide, key_pos_ref[s], query_pos_ref[s])
        chances = jnp.exp(scores - log_ref[s])
        d_chances = dot(pair, d_out, 1, 1)
        if steps > 1:
            dots = dots_ref[s]
        else:
            dots = jnp.sum(chances * d_chances, axis=0, keepdims=True)
        d_scores = (chances * (d_chances - dots)).astype(jnp.bfloat16)
        d_pair = dot(d_scores, wide, 1, 0) + dot(chances.astype(jnp.bfloat16), d_out, 1, 0)
        d_pair = d_pair.astype(jnp.bfloat16)
        d_pair_ref[:, s] = d_pair.reshape(d_pair_ref.shape[:1] + d_pair_ref.shape[2:])
        sum_ref[s] += dot(pair, d_scores, 0, 0)

        @when(step == steps - 1)
        def _():
            flat = flat_heads(sum_ref[s, :HEAD, :].T, heads) * (HEAD ** (-0.5))
            d_query_ref[s] = turn_back(flat, cosine_ref[s], sine_ref[s]).astype(jnp.bfloat16)


def turn_back(flat, cosine, sine):
    wide = -(-flat.shape[1] // 128) * 128
    blank = jnp.zeros((flat.shape[0], wide - flat.shape[1]), jnp.float32)
    padded = jnp.concatenate([flat, blank], axis=1) if wide > flat.shape[1] else flat
    turned = turn(padded * widen(sine, wide))
    turned = jnp.where(first_half(padded.shape), turned, -turned)
    return (padded * widen(cosine, wide) + turned)[:, : flat.shape[1]]


def attention_call(kernel, name, heads, rows, ctx, seqs, width, inputs, kinds, outs, scratch):
    group = min(ctx, 1024 // rows)
    steps = ctx // group
    span = group * rows
    tall = heads * rows
    wide = heads * HEAD
    shapes = {
        "flat": ((seqs, rows, wide), (1, rows, wide), lambda s, k: (s, 0, 0)),
        "model": ((seqs, rows, width), (1, rows, width), lambda s, k: (s, 0, 0)),
        "table": ((seqs, rows, 2 * HEAD), (1, rows, 2 * HEAD), lambda s, k: (s, 0, 0)),
        "pair": (
            (ctx, seqs, rows, 2 * HEAD),
            (group, 1, rows, 2 * HEAD),
            lambda s, k: (k, s, 0, 0),
        ),
        "key": ((seqs, ctx * rows, 1), (1, span, 1), lambda s, k: (s, k, 0)),
        "row": ((seqs, 1, tall), (1, 1, tall), lambda s, k: (s, 0, 0)),
        "out": ((seqs, HEAD, tall), (1, HEAD, tall), lambda s, k: (s, 0, 0)),
        "none": ((1, 8, 128), (1, 8, 128), lambda s, k: (0, 0, 0)),
        "weight": ((width, wide), (width, wide), lambda s, k: (0, 0)),
    }
    out_shape = [jax.ShapeDtypeStruct(shapes[kind][0], dtype) for kind, dtype in outs]
    here = seqs if steps == 1 else 1
    scratch = [pltpu.VMEM((here,) + shape, dtype) for shape, dtype in scratch]
    kernel = functools.partial(kernel, heads, steps)
    if steps == 1:
        return whole_call(kernel, name, inputs, out_shape, scratch)
    spec = lambda kind: pl.BlockSpec(shapes[kind][1], shapes[kind][2])
    return pl.pallas_call(
        kernel,
        grid=(seqs, steps),
        in_specs=[spec(kind) for kind in kinds],
        out_specs=[spec(kind) for kind, _ in outs],
        out_shape=out_shape,
        scratch_shapes=scratch,
        compiler_params=pltpu.CompilerParams(vmem_limit_bytes=VMEM_LIMIT),
        cost_estimate=BRIEF,
        name=name,
    )(*inputs)


def ffn_kernel(part, token_ref, w_ref, *refs):
    near_refs, mixed_refs, active_ref, d_gate_up_ref = refs[:2], refs[2:4], *refs[4:]
    block = token_ref.shape[0] // 4
    for half in (1, 0):
        rows = pl.ds(half * block, block)
        gate_up = dot(token_ref[rows, :], w_ref[:, : 2 * part], 1, 0)
        gate, up_values = gate_up[:, :part], gate_up[:, part:]
        sigma = 1.0 / (1.0 + jnp.exp(-gate))
        silu = gate * sigma
        active = (silu * up_values).astype(jnp.bfloat16)
        active_ref[rows, :] = active
        d_active = dot(token_ref[pl.ds((2 + half) * block, block), :], w_ref[:, 2 * part :], 1, 0)
        d_gate = d_active * up_values * sigma * (1.0 + gate * (1.0 - sigma))
        d_gate_up = jnp.concatenate([d_gate, d_active * silu], axis=1).astype(jnp.bfloat16)
        d_gate_up_ref[rows, :] = d_gate_up
        near_refs[half][...] = dot(d_gate_up, w_ref[:, : 2 * part], 1, 1).astype(jnp.bfloat16)
        mixed_refs[half][...] = dot(active, w_ref[:, 2 * part :], 1, 1).astype(jnp.bfloat16)


def ffn_call(part, tokens, w_ffn):
    block, width = tokens.shape[0] // 4, tokens.shape[1]
    model = jax.ShapeDtypeStruct((block, width), jnp.bfloat16)
    units = lambda count: jax.ShapeDtypeStruct((2 * block, count * part), jnp.bfloat16)
    return whole_call(
        functools.partial(ffn_kernel, part),
        "ffn",
        (tokens, w_ffn),
        [model, model, model, model, units(1), units(2)],
    )


def ffn_grad_kernel(part, token_ref, active_ref, d_gate_up_ref, out_ref):
    half = token_ref.shape[0] // 2
    for index in range(3):
        columns = slice(index * part, (index + 1) * part)
        left = token_ref[:half, :] if index < 2 else token_ref[half:, :]
        right = d_gate_up_ref[:, columns] if index < 2 else active_ref[...]
        out_ref[:, columns] = dot(left, right, 0, 0).astype(jnp.bfloat16)


def ffn_grad_call(part, tokens, active, d_gate_up):
    return whole_call(
        functools.partial(ffn_grad_kernel, part),
        "ffn_grad",
        (tokens, active, d_gate_up),
        [jax.ShapeDtypeStruct((tokens.shape[1], 3 * part), jnp.bfloat16)],
    )[0]


def split_rows(total, place_ref, share, kept_ref, sent_ref):
    odd = place_ref[0] % 2 == 1
    for index in range(total.shape[0] // (2 * share)):
        even_rows = total[2 * index * share : (2 * index + 1) * share]
        odd_rows = total[(2 * index + 1) * share : (2 * index + 2) * share]
        kept_ref[index] = jnp.where(odd, odd_rows, even_rows).astype(jnp.bfloat16)
        sent_ref[index] = jnp.where(odd, even_rows, odd_rows).astype(jnp.bfloat16)


def wide_kernel(share, place_ref, normed_ref, d_query_ref, d_low_ref, flat_ref, kept_ref, sent_ref):
    d_query = dot(normed_ref[...], d_query_ref[...], 0, 0)
    d_w_out = dot(d_low_ref[...], flat_ref[...], 0, 0)
    split_rows(jnp.concatenate([d_query, d_w_out], axis=1), place_ref, share, kept_ref, sent_ref)


def finish_kernel(
    share,
    place_ref,
    pair_ref,
    cosine_ref,
    sine_ref,
    normed_ref,
    token_ref,
    w_ref,
    d_query_ref,
    own_ref,
    other_ref,
    hidden_ref,
    same_ref,
    column_ref,
    weighted_ref,
    kept_ref,
    sent_ref,
):
    pair = pair_ref[...]
    turned = turn_back(pair, cosine_ref[...], sine_ref[...])
    lane = lax.broadcasted_iota(jnp.int32, pair.shape, 1)
    d_pair = jnp.where(lane < HEAD, turned, pair).astype(jnp.bfloat16)
    d_lin = jnp.concatenate([d_query_ref[...], d_pair], axis=1)
    weighted = dot(d_lin, w_ref[...], 1, 1)
    weighted_ref[...] = weighted.astype(jnp.bfloat16)
    count = pair.shape[0]
    d_pair_w = dot(normed_ref[...], d_pair, 0, 0)
    normed, _ = norm_apply(token_ref[...].astype(jnp.float32))
    hidden, _ = norm_apply(hidden_ref[...])
    weighted_two = own_ref[...].astype(jnp.float32) + other_ref[...].astype(jnp.float32)

    def spot(column):
        return (lax.broadcasted_iota(jnp.int32, (count, 128), 1) == column).astype(jnp.bfloat16)

    gains = dot((weighted * normed).astype(jnp.bfloat16), spot(0), 0, 0)
    gains = gains + dot((weighted_two * hidden).astype(jnp.bfloat16), spot(1), 0, 0)
    ones = jnp.ones((count, 128), jnp.bfloat16)
    bias = dot(d_lin, ones, 0, 0)
    bias = jnp.where(column_ref[...] > 0, bias, 0.0).astype(jnp.bfloat16)
    bias = dot(same_ref[...], bias, 1, 0)
    total = jnp.concatenate([d_pair_w, gains + bias], axis=1)
    split_rows(total, place_ref, share, kept_ref, sent_ref)


def local(
    tokens,
    cotangent,
    block_of,
    norm_gain,
    ffn_gain,
    w_query,
    w_key,
    w_value,
    b_query,
    b_key,
    b_value,
    w_out,
    w_gate,
    w_up,
    w_down,
):
    seqs, rows, width = tokens.shape
    count = seqs * rows
    block_len = rows // 2
    ctx = lax.axis_size("ctx")
    groups = Groups(ctx)
    low = groups.low
    device = lax.axis_index("ctx")
    heads = w_query.shape[1] // HEAD
    share = width // ctx
    units = w_gate.shape[1]
    part = -(-units // (low * 128)) * 128
    query_width = heads * HEAD
    own_gain_one = norm_gain.astype(jnp.float32)[:, None]
    own_gain_two = ffn_gain.astype(jnp.float32)[:, None]

    def scaled(matrix, gain):
        return (matrix.astype(jnp.float32) * gain).astype(jnp.bfloat16)

    def pieces(matrix):
        return jnp.pad(matrix, ((0, 0), (0, low * part - units))).reshape(share, low, part)

    w_ffn = jnp.concatenate(
        [
            pieces(scaled(w_gate, own_gain_two)),
            pieces(scaled(w_up, own_gain_two)),
            pieces(w_down.T),
        ],
        axis=2,
    ).transpose(1, 0, 2)
    w_attn = jnp.concatenate(
        [scaled(jnp.concatenate([w_query, w_key, w_value], axis=1), own_gain_one), w_out.T], axis=1
    )
    w_ffn, w_attn = together(w_ffn, w_attn)
    w_ffn = groups.swap_near(w_ffn).reshape(low * share, 3 * part)
    w_attn = groups.gather_far(w_attn, device)

    offsets = jnp.arange(block_len, dtype=jnp.int32)
    own_blocks = lax.dynamic_slice_in_dim(block_of, device * 2, 2, 1)
    row_pos = (own_blocks[:, :, None] * block_len + offsets).reshape(seqs, rows)
    query_pos = jnp.tile(row_pos, (1, heads))[:, None, :]
    flips = jnp.array(
        [core + step + far for core in (0, 1) for step in (0, 2) for far in groups.far_bits],
        jnp.int32,
    )
    key_blocks = block_of.reshape(seqs, ctx, 2)[:, device ^ flips]
    key_pos = (key_blocks[..., None] * block_len + offsets).reshape(seqs, ctx * rows, 1)
    cosine, sine = rope_tables(row_pos.reshape(count), HEAD)
    cosine, sine = jnp.tile(cosine, (1, 2)), jnp.tile(sine, (1, 2))

    w_ffn, w_attn, key_pos, query_pos, cosine, sine = together(
        w_ffn, w_attn, key_pos, query_pos, cosine, sine
    )
    w_ffn = lax.all_gather(w_ffn, "ctx", axis=0, tiled=True, axis_index_groups=groups.far)
    qkv_width = query_width + 2 * HEAD
    w_qkv = groups.spread_near(w_attn[:, :, :qkv_width])
    grads_in = cotangent.reshape(count, width)

    bias = jnp.concatenate([b_query, b_key, b_value]).astype(jnp.float32)[None]
    normed_low, queries, pair = whole_call(
        functools.partial(project_kernel, heads),
        "project",
        (tokens.reshape(count, width), w_qkv, bias, cosine, sine),
        [
            jax.ShapeDtypeStruct((count, width), jnp.bfloat16),
            jax.ShapeDtypeStruct((count, query_width), jnp.bfloat16),
            jax.ShapeDtypeStruct((count, 2 * HEAD), jnp.bfloat16),
        ],
    )
    queries = queries.reshape(seqs, rows, query_width)
    pairs = groups.far_flips(pair)
    w_out_t = groups.flip_near(w_attn[:, :, qkv_width:], device)
    pairs = jnp.stack([pairs, groups.flip(pairs, 2)])
    pairs = jnp.stack([pairs, groups.flip(pairs, 1)]).reshape(ctx, seqs, rows, 2 * HEAD)
    pairs, w_out_t = together(pairs, w_out_t)
    attend = functools.partial(
        attention_call, heads=heads, rows=rows, ctx=ctx, seqs=seqs, width=width
    )
    tall = heads * rows
    tall_kind = "out" if ctx * rows > 1024 else "none"
    out_flat, attention, out_tall, log_total = attend(
        forward_kernel,
        "forward",
        inputs=(queries, pairs, key_pos, query_pos, w_out_t),
        kinds=("flat", "pair", "key", "row", "weight"),
        outs=(
            ("flat", jnp.bfloat16),
            ("model", jnp.bfloat16),
            (tall_kind, jnp.float32),
            ("row", jnp.float32),
        ),
        scratch=[
            ((1, tall), jnp.float32),
            ((1, tall), jnp.float32),
            ((2 * HEAD, tall), jnp.float32),
        ],
    )
    out_flat = out_flat.reshape(count, query_width)
    inputs = tokens.astype(jnp.float32).reshape(count, width)
    hidden = inputs + sum_tp(attention.reshape(count, width))

    grads_near = groups.gather_near(grads_in)
    hidden, *grads_near = together(hidden, *grads_near)
    normed_two, _ = norm_apply(hidden)
    near_two = groups.gather_near(normed_two.astype(jnp.bfloat16))
    token_parts = jnp.concatenate([*near_two, *grads_near], axis=0)
    near_kept, near_sent, mixed_kept, mixed_sent, active, d_gate_up = ffn_call(
        part, token_parts, w_ffn
    )
    d_w_ffn = ffn_grad_call(part, token_parts, active, d_gate_up)
    crossed = groups.flip(near_sent, 1)
    crossed, d_w_ffn = together(crossed, d_w_ffn)
    d_w_ffn = lax.psum_scatter(
        d_w_ffn, "ctx", scatter_dimension=0, tiled=True, axis_index_groups=groups.far
    )
    near_sent = groups.flip(add(near_kept[count:], crossed[count:]), 2)
    d_own = add(add(near_kept[:count], crossed[:count]), near_sent)
    mixed_sent = groups.flip(mixed_sent, 1)
    d_own, mixed_sent = together(d_own, mixed_sent)
    d_other = lax.ppermute(d_own, "tp", [(0, 1), (1, 0)])
    mixed_kept = add(mixed_kept, mixed_sent)
    d_other, mixed_kept = together(d_other, mixed_kept)
    mixed_own = add(mixed_kept[:count], groups.flip(mixed_kept[count:], 2))

    by_seq = lambda values: values.reshape((seqs, rows) + values.shape[1:])
    d_hidden, d_hidden_low, d_query_low, d_pairs = attend(
        backward_kernel,
        "backward",
        inputs=(
            queries,
            pairs,
            key_pos,
            query_pos,
            out_tall,
            log_total,
            w_out_t,
            by_seq(d_own),
            by_seq(d_other),
            by_seq(hidden),
            cotangent,
            by_seq(cosine),
            by_seq(sine),
        ),
        kinds=(
            ("flat", "pair", "key", "row", tall_kind, "row", "weight")
            + ("model", "model", "model", "model", "table", "table")
        ),
        outs=(
            ("model", jnp.float32),
            ("model", jnp.bfloat16),
            ("flat", jnp.bfloat16),
            ("pair", jnp.bfloat16),
        ),
        scratch=[
            ((tall, 2 * HEAD), jnp.bfloat16),
            ((1, tall), jnp.float32),
            ((2 * HEAD, tall), jnp.float32),
        ],
    )
    d_hidden = d_hidden.reshape(count, width)
    d_hidden_low = d_hidden_low.reshape(count, width)
    d_query_low = d_query_low.reshape(count, query_width)
    d_pairs, mixed_own = together(d_pairs, mixed_own)
    mixed_other = lax.ppermute(mixed_own, "tp", [(0, 1), (1, 0)])
    d_pairs = d_pairs.reshape(2, 2 * groups.high * count, 2 * HEAD)
    crossed = groups.flip(d_pairs[1], 1)
    crossed, d_query_low = together(crossed, d_query_low)
    halves = lambda columns: [jax.ShapeDtypeStruct((ctx // 2, share, columns), jnp.bfloat16)] * 2
    wide_kept, wide_sent = whole_call(
        functools.partial(wide_kernel, share),
        "wide",
        (normed_low, d_query_low, d_hidden_low, out_flat),
        halves(2 * query_width),
        place=device,
    )
    wide_crossed = groups.flip(wide_sent, 1)
    d_pairs = add(d_pairs[0], crossed).reshape(2, groups.high * count, 2 * HEAD)
    d_pairs = add(d_pairs[0], groups.flip(d_pairs[1], 2)).reshape(groups.high, count, 2 * HEAD)
    d_pairs, wide_crossed = together(d_pairs, wide_crossed)
    near_half = lambda kept, crossed: halve(
        groups, add(kept, crossed).reshape((groups.high, 2) + kept.shape[1:]), 2, device, 1
    )
    d_w_wide = near_half(wide_kept, wide_crossed)
    pair_grads = d_pairs[0].astype(jnp.float32)
    for m in range(1, groups.high):
        pair_grads = pair_grads + groups.flip(d_pairs[m], groups.far_bits[m]).astype(jnp.float32)
    pair_grads, d_w_wide = together(pair_grads, d_w_wide)
    mixed = hidden + mixed_own.astype(jnp.float32) + mixed_other.astype(jnp.float32)
    mixed = mixed.astype(jnp.bfloat16)

    row = jnp.arange(width)[:, None] % share
    unit = jnp.arange(qkv_width)[None, :]
    same = (row == unit % share).astype(jnp.bfloat16)
    column = (unit.T // share + 2 == jnp.arange(128)[None, :]).astype(jnp.float32)
    d_weighted_low, narrow_kept, narrow_sent = whole_call(
        functools.partial(finish_kernel, share),
        "finish",
        (
            pair_grads,
            cosine,
            sine,
            normed_low,
            tokens.reshape(count, width),
            w_qkv,
            d_query_low,
            d_own,
            d_other,
            hidden,
            same,
            column,
        ),
        [
            jax.ShapeDtypeStruct((count, width), jnp.bfloat16),
            *halves(256),
        ],
        place=device,
    )
    d_weighted = sum_tp(d_weighted_low)
    _, scale_one = norm_apply(inputs)
    tokens_grad = (d_hidden + norm_back(inputs, scale_one, d_weighted)).astype(jnp.bfloat16)
    narrow = near_half(narrow_kept, groups.flip(narrow_sent, 1))
    narrow, d_w_ffn = together(jnp.concatenate([d_w_wide, narrow], axis=2), d_w_ffn)
    d_w_ffn = groups.swap_near(d_w_ffn.reshape(low, share, 3 * part))
    narrow = groups.far_owner(narrow, device)
    d_w_wide, narrow = narrow[:, : 2 * query_width], narrow[:, 2 * query_width :]

    def whole(swapped, index):
        some = swapped[:, :, index * part : (index + 1) * part].transpose(1, 0, 2)
        return some.reshape(share, low * part)[:, :units].astype(jnp.float32)

    g_gate = whole(d_w_ffn, 0) * own_gain_two
    g_up = whole(d_w_ffn, 1) * own_gain_two
    g_down = whole(d_w_ffn, 2).T

    held = -(-qkv_width // share)
    g_bias = narrow[:, 2 * HEAD + 2 : 2 * HEAD + 2 + held].T.reshape(held * share)
    g_pair = narrow[:, : 2 * HEAD] * own_gain_one
    g_two = narrow[:, 2 * HEAD + 1] / own_gain_two[:, 0]
    g_one = narrow[:, 2 * HEAD] / own_gain_one[:, 0]
    g_one = g_one + lax.ppermute(g_one, "tp", [(0, 1), (1, 0)])
    return (
        mixed.reshape(tokens.shape),
        tokens_grad.reshape(tokens.shape),
        g_one,
        g_two,
        d_w_wide[:, :query_width] * own_gain_one,
        g_pair[:, :HEAD],
        g_pair[:, HEAD:],
        g_bias[:query_width],
        g_bias[query_width : query_width + HEAD],
        g_bias[query_width + HEAD : query_width + 2 * HEAD],
        d_w_wide[:, query_width:].T,
        g_gate,
        g_up,
        g_down,
    )


def solution(mesh):
    placed = (
        P(None, "ctx", None),
        P(None, "ctx", None),
        P(),
        P("ctx"),
        P("ctx"),
        P("ctx", "tp"),
        P("ctx", "tp"),
        P("ctx", "tp"),
        P("tp"),
        P("tp"),
        P("tp"),
        P("tp", "ctx"),
        P("ctx", "tp"),
        P("ctx", "tp"),
        P("tp", "ctx"),
    )
    return jax.shard_map(
        local,
        mesh=mesh,
        in_specs=placed,
        out_specs=(
            P(None, "ctx", None),
            P(None, "ctx", None),
            P("ctx"),
            P("ctx"),
            P("ctx", "tp"),
            P("ctx", "tp"),
            P("ctx", "tp"),
            P("tp"),
            P("tp"),
            P("tp"),
            P("tp", "ctx"),
            P("ctx", "tp"),
            P("ctx", "tp"),
            P("tp", "ctx"),
        ),
        check_vma=False,
    )
```

time: 250 us -> 217 us (0.87)
  waiting for transfers between devices: 89.5 us -> 75.3 us
  local copies, waits for them, and re-layouts: 29 us -> 18.5 us
  other arithmetic: 20.2 us -> 26.9 us
  starting transfers between devices: 50.6 us -> 44.8 us
  blocking collectives: 19.5 us -> 13.8 us
  matrix products: 4.87 us -> 0 us
    all_to_all x2, waiting for transfers between devices: 18.4 us -> 7.28 us  [swap_near(): lax.all_to_all(values, 'ctx', 0, 0, tiled=True, axis_index_groups=self.near)]
    ppermute x31 -> x30, waiting for transfers between devices: 49.4 us -> 41 us  [flip(): lax.ppermute(values, 'ctx', [(i, i ^ bit) for i in range(self.count)])]
    ppermute x31 -> x30, starting transfers between devices: 35.9 us -> 29.7 us  [flip(): lax.ppermute(values, 'ctx', [(i, i ^ bit) for i in range(self.count)])]
    convert_element_type x8 -> x11, other arithmetic: 3.08 us -> 9.17 us  [the longest x8 6.03 us: add(): (one.astype(jnp.float32) + two.astype(jnp.float32)).astype(jnp.bfloat16)]
    another operation x7 -> x8, other arithmetic: 0.35 us -> 6.05 us  [the longest x2 1.96 us: flip_near(): jnp.stack([jnp.where(upper, other, values), jnp.where(upper, values, othe...]
    all_gather x2 -> x1, blocking collectives: 19.5 us -> 13.8 us  [spread_near(): whole = lax.all_gather(values, 'ctx', axis=0, axis_index_groups=self.near)]
    dot_general x7 -> x0, matrix products: 4.87 us -> none  [the longest x5 2.59 us: dot(): lax.dot_general(left, right, (((left_dim,), (right_dim,)), ((), ())), pre...]
    unnamed x113 -> x98, local copies, waits for them, and re-layouts: 16.3 us -> 11.9 us
  transfers between devices with their start and end apart: 40 -> 39, of which waited for: 22 -> 23; matrix products, arithmetic and copies ran while one was open for 12% -> 13% of each run, Pallas kernels for 5% -> 7%
where the time goes in v3:
time: 217 us; the launch traced here: 216 us
  waiting for transfers between devices  75.3 us (35%)
  starting transfers between devices  44.8 us (21%)
  other arithmetic  26.9 us (12%)
  Pallas kernels  21.8 us (10%)
  local copies, waits for them, and re-layouts  18.5 us (9%)
  between operations  15.2 us (7%)
  blocking collectives  13.8 us (6%)
    ppermute x30, waiting for transfers between devices, flip(): lax.ppermute(values, 'ctx', [(i, i ^ bit) for i in range(self.count)])  41 us
    ppermute x30, starting transfers between devices, flip(): lax.ppermute(values, 'ctx', [(i, i ^ bit) for i in range(self.count)])  29.7 us
    pallas_call x7, Pallas kernels, whole_call(): pl.pallas_call(kernel, in_specs=in_specs, out_specs=[whole] * len(out_sha...  21.8 us
    all_gather x1, blocking collectives, spread_near(): whole = lax.all_gather(values, 'ctx', axis=0, axis_index_groups=self.near)  13.8 us
    unnamed x98, local copies, waits for them, and re-layouts  11.9 us
    ppermute x2, waiting for transfers between devices, sum_tp(): other = lax.ppermute(values, 'tp', [(0, 1), (1, 0)])  9.94 us
    all_gather x1, waiting for transfers between devices, local(): lax.all_gather(w_ffn, 'ctx', axis=0, tiled=True, axis_index_groups=groups...  9.79 us
    all_to_all x2, waiting for transfers between devices, swap_near(): lax.all_to_all(values, 'ctx', 0, 0, tiled=True, axis_index_groups=self.near)  7.28 us
  transfers between devices with their start and end apart: 39, of which 23 were waited for; matrix products, arithmetic and copies ran while one was open for 13% of the time, Pallas kernels for 7%

profile of v3, /device:TPU:0, one launch (start us, length us, event | category | flops | bytes accessed | tf_op | source)
XLA Modules:
  0.0 216.3 jit_solution(7828093884227192309)
XLA Ops:
  11.1 3.0 %collective-permute-start = (bf16[56,1024]{1,0:T(8,128)(2,1)S(1)}, bf16[56,1024]{1,0:T(8,128)(2,1)S(1)}, u32[]{:S(2)}, u32[]{:S(2)}) collective-permute-start(bf16[56,1024]{1,0:T(8,128)(2,1)S(1)} %pad_maximum_fusion.9), channel_id=1, source_target_pairs={{0,8},{2,10},{4,12},{6,14},{8,0},{10,2},{12,4},{14,6},{16,24},{18,... | collective-permute-start | bytes 344072 | tf_op jit(solution)/shard_map/ppermute | solution.py:64
  14.2 2.6 %collective-permute-start.1 = (bf16[56,1024]{1,0:T(8,128)(2,1)S(1)}, bf16[56,1024]{1,0:T(8,128)(2,1)S(1)}, u32[]{:S(2)}, u32[]{:S(2)}) collective-permute-start(bf16[56,1024]{1,0:T(8,128)(2,1)S(1)} %pad_maximum_fusion.9), channel_id=1, source_target_pairs={{0,16},{2,18},{4,20},{6,22},{8,24},{10,26},{12,28},{14,30},{16,0},... | collective-permute-start | bytes 344072 | tf_op jit(solution)/shard_map/ppermute | solution.py:64
  16.8 3.5 %all-to-all-start = ((bf16[4,56,1920]{2,1,0:T(8,128)(2,1)}), bf16[4,56,1920]{2,1,0:T(8,128)(2,1)S(1)}, u32[]{:S(2)}, u32[]{:S(2)}) async-start(bf16[4,56,1920]{2,1,0:T(8,128)(2,1)} %maximum_bitcast_fusion), calls=%async_computation | async-start | bytes 1720320 | tf_op jit(solution)/shard_map/all_to_all | solution.py:67
  23.4 2.5 %collective-permute-done.1 = bf16[56,1024]{1,0:T(8,128)(2,1)S(1)} collective-permute-done((bf16[56,1024]{1,0:T(8,128)(2,1)S(1)}, bf16[56,1024]{1,0:T(8,128)(2,1)S(1)}, u32[]{:S(2)}, u32[]{:S(2)}) %collective-permute-start.1) | collective-permute-done | bytes 114720 | tf_op jit(solution)/shard_map/ppermute | solution.py:64
  26.1 6.5 %all-to-all-done = bf16[4,56,1920]{2,1,0:T(8,128)(2,1)S(1)} async-done(((bf16[4,56,1920]{2,1,0:T(8,128)(2,1)}), bf16[4,56,1920]{2,1,0:T(8,128)(2,1)S(1)}, u32[]{:S(2)}, u32[]{:S(2)}) %all-to-all-start) | async-done | bytes 860192 | tf_op jit(solution)/shard_map/all_to_all | solution.py:67
  34.5 13.8 %all-gather = bf16[16,56,576]{2,1,0:T(8,128)(2,1)S(1)} all-gather(bf16[4,56,576]{2,1,0:T(8,128)(2,1)S(1)} %slice.114), channel_id=2, replica_groups={{0,2,4,6},{8,10,12,14},{16,18,20,22},{24,26,28,30},{1,3,5,7},{9,11,13,1..., dimensions={0}, use_global_device_ids=true | all-gather | bytes 1290240 | tf_op jit(solution)/shard_map/all_gather | solution.py:86
  51.5 3.5 %collective-permute-start.4 = (bf16[128,128]{1,0:T(8,128)(2,1)S(1)}, bf16[128,128]{1,0:T(8,128)(2,1)}, u32[]{:S(2)}, u32[]{:S(2)}) collective-permute-start(bf16[128,128]{1,0:T(8,128)(2,1)S(1)} %get-tuple-element.71), channel_id=1, source_target_pairs={{0,16},{2,18},{4,20},{6,22},{8,24},{10,26},{12,28},{14,30},{16,0},... | collective-permute-start | bytes 98312 | tf_op jit(solution)/shard_map/ppermute | solution.py:64
  55.0 3.2 %collective-permute-done.3 = bf16[128,128]{1,0:T(8,128)(2,1)S(1)} collective-permute-done((bf16[128,128]{1,0:T(8,128)(2,1)S(1)}, bf16[128,128]{1,0:T(8,128)(2,1)S(1)}, u32[]{:S(2)}, u32[]{:S(2)}) %collective-permute-start.3) | collective-permute-done | bytes 32800 | tf_op jit(solution)/shard_map/ppermute | solution.py:64
  58.2 3.4 %collective-permute-done.4 = bf16[128,128]{1,0:T(8,128)(2,1)} collective-permute-done((bf16[128,128]{1,0:T(8,128)(2,1)S(1)}, bf16[128,128]{1,0:T(8,128)(2,1)}, u32[]{:S(2)}, u32[]{:S(2)}) %collective-permute-start.4) | collective-permute-done | bytes 32800 | tf_op jit(solution)/shard_map/ppermute | solution.py:64
  65.0 2.5 %collective-permute-done.6 = bf16[4,128,128]{2,1,0:T(8,128)(2,1)S(1)} collective-permute-done((bf16[4,128,128]{2,1,0:T(8,128)(2,1)S(1)}, bf16[4,128,128]{2,1,0:T(8,128)(2,1)S(1)}, u32[]{:S(2)}, u32[]{:S(2)}) %collective-permute-start.6) | collective-permute-done | bytes 131104 | tf_op jit(solution)/shard_map/ppermute | solution.py:64
  71.6 1.3 select_bitcast_fusion.1
  73.8 3.4 %forward.1 = (bf16[2,64,448]{2,1,0:T(8,128)(2,1)S(1)}, bf16[2,64,896]{2,1,0:T(8,128)(2,1)S(1)}, f32[1,8,128]{2,1,0:T(8,128)S(1)}, f32[2,1,448]{2,1,0:T(1,128)S(1)}) custom-call(bf16[2,64,448]{2,1,0:T(8,128)(2,1)S(1)} %bitcast.161, bf16[16,2,64,128]{3,2,1,0:T(8,128)(2,1)S(1)} %bitcast.153, s32[2,1024,1]{2,1,0:T(8,128)S(1)} %broadcast_add_fusion.key_pos_ref, ...), custom_call_target="tpu_custom_call" | custom-call | flops 1 | bytes 1 | tf_op jit(solution)/shard_map/forward/pallas_call | solution.py:182
  77.2 1.5 collective-permute-start.10
  79.8 5.1 %collective-permute-done.10 = bf16[128,896]{1,0:T(8,128)(2,1)S(1)} collective-permute-done((bf16[128,896]{1,0:T(8,128)(2,1)S(1)}, bf16[128,896]{1,0:T(8,128)(2,1)S(1)}, u32[]{:S(2)}, u32[]{:S(2)}) %collective-permute-start.10) | collective-permute-done | bytes 229408 | tf_op jit(solution)/shard_map/ppermute | solution.py:46
  86.0 6.2 %collective-permute-done.13 = bf16[128,896]{1,0:T(8,128)(2,1)S(1)} collective-permute-done((bf16[128,896]{1,0:T(8,128)(2,1)S(1)}, bf16[128,896]{1,0:T(8,128)(2,1)S(1)}, u32[]{:S(2)}, u32[]{:S(2)}) %collective-permute-start.13) | collective-permute-done | bytes 229408 | tf_op jit(solution)/shard_map/ppermute | solution.py:64
  92.4 1.8 collective-permute-done.14
  94.3 1.3 copy-done
  95.6 9.8 %all-gather.3.cloned.1.call-done.w_ref = bf16[896,1920]{1,0:T(8,128)(2,1)} async-done(((bf16[224,1920]{1,0:T(8,128)(2,1)}), bf16[896,1920]{1,0:T(8,128)(2,1)}) %all-gather.3.cloned.1.call-update) | async-done | bytes 3440656 | tf_op jit(solution)/shard_map/all_gather | solution.py:542
  105.4 1.5 copy-done.1
  106.9 6.8 %ffn.1 = (bf16[256,896]{1,0:T(8,128)(2,1)S(1)}, bf16[256,896]{1,0:T(8,128)(2,1)}, bf16[256,896]{1,0:T(8,128)(2,1)S(1)}, bf16[256,896]{1,0:T(8,128)(2,1)S(1)}, bf...) custom-call(bf16[1024,896]{1,0:T(8,128)(2,1)S(1)} %copy-done.1, ...), custom_call_target="tpu_custom_call" | custom-call | flops 1 | bytes 1 | tf_op jit(solution)/shard_map/ffn/pallas_call | solution.py:182
  116.0 4.1 %ffn_grad.1 = bf16[896,1920]{1,0:T(8,128)(2,1)} custom-call(bf16[1024,896]{1,0:T(8,128)(2,1)S(1)} %copy-done.1, bf16[512,640]{1,0:T(8,128)(2,1)S(1)} %get-tuple-element.85.active_ref, bf16[512,1280]{1,0:T(8,128)(2,1)S(1)} %get-tuple-element.86.d_gate_up_ref), custom_call_target="tpu_custom_call" | custom-call | flops 1 | bytes 1 | tf_op jit(solution)/shard_map/ffn_grad/pallas_call | solution.py:182
  121.4 1.6 collective-permute-start.16
  123.2 6.3 %collective-permute-done.16 = bf16[128,896]{1,0:T(8,128)(2,1)S(1)} collective-permute-done((bf16[128,896]{1,0:T(8,128)(2,1)S(1)}, bf16[128,896]{1,0:T(8,128)(2,1)S(1)}, u32[]{:S(2)}, u32[]{:S(2)}) %collective-permute-start.16) | collective-permute-done | bytes 229408 | tf_op jit(solution)/shard_map/ppermute | solution.py:64
  130.6 1.8 collective-permute-start.18
  133.6 4.7 %collective-permute-done.18.other_ref = bf16[128,896]{1,0:T(8,128)(2,1)S(1)} collective-permute-done((bf16[128,896]{1,0:T(8,128)(2,1)S(1)}, bf16[128,896]{1,0:T(8,128)(2,1)S(1)}, u32[]{:S(2)}, u32[]{:S(2)}) %collective-permute-start.18) | collective-permute-done | bytes 229408 | tf_op jit(solution)/shard_map/ppermute | solution.py:608
  138.3 1.6 collective-permute-start.19
  139.9 4.2 %backward.1 = (f32[2,64,896]{2,1,0:T(8,128)S(1)}, bf16[2,64,896]{2,1,0:T(8,128)(2,1)S(1)}, bf16[2,64,448]{2,1,0:T(8,128)(2,1)S(1)}, bf16[16,2,64,128]{3,2,1,0:T(8,128)(2,1)S(1)}) custom-call(bf16[2,64,448]{2,1,0:T(8,128)(2,1)S(1)} %bitcast.162, bf16[16,2,64,128]{3,2,1,0:T(8,128)(2,1)S(1)} %bitcast.154, s32[2,1024,1]{2,1,0:T(8,128)S(1)} %broadcast_add_fusion.key_pos_ref, ...), custom_call_target="tpu_custom_call" | custom-call | flops 1 | bytes 1 | tf_op jit(solution)/shard_map/backward/pallas_call | solution.py:182
  145.8 1.3 compare_convert_fusion.same_ref
  147.3 1.7 wide.1
  149.4 1.6 collective-permute-start.22
  151.3 3.8 %collective-permute-done.22 = bf16[512,128]{1,0:T(8,128)(2,1)S(1)} collective-permute-done((bf16[512,128]{1,0:T(8,128)(2,1)S(1)}, bf16[512,128]{1,0:T(8,128)(2,1)S(1)}, u32[]{:S(2)}, u32[]{:S(2)}) %collective-permute-start.22) | collective-permute-done | bytes 131104 | tf_op jit(solution)/shard_map/ppermute | solution.py:64
  155.2 1.6 add_convert_fusion
  158.5 1.5 collective-permute-start.27
  160.1 1.3 collective-permute-start.25
  161.4 3.0 %collective-permute-start.26 = (bf16[128,128]{1,0:T(8,128)(2,1)S(1)}, bf16[128,128]{1,0:T(8,128)(2,1)S(1)}, u32[]{:S(2)}, u32[]{:S(2)}) collective-permute-start(bf16[128,128]{1,0:T(8,128)(2,1)S(1)} %get-tuple-element.137), channel_id=1, source_target_pairs={{0,24},{2,26},{4,28},{6,30},{8,16},{10,18},{12,20},{14,22},{16,8},... | collective-permute-start | bytes 98312 | tf_op jit(solution)/shard_map/ppermute | solution.py:64
  164.6 1.5 collective-permute-start.20
  166.8 1.6 collective-permute-done.26
  170.8 1.2 copy-done.5
  173.2 1.7 add_convert_fusion.3
  175.0 1.5 collective-permute-start.28
  176.6 1.5 collective-permute-start.30
  178.1 4.9 %collective-permute-done.28 = bf16[128,896]{1,0:T(8,128)(2,1)S(1)} collective-permute-done((bf16[128,896]{1,0:T(8,128)(2,1)S(1)}, bf16[128,896]{1,0:T(8,128)(2,1)S(1)}, u32[]{:S(2)}, u32[]{:S(2)}) %collective-permute-start.28) | collective-permute-done | bytes 229408 | tf_op jit(solution)/shard_map/ppermute | solution.py:46
  183.2 2.6 %reduce-scatter.2.cloned.1.call-done = bf16[224,1920]{1,0:T(8,128)(2,1)} async-done(((bf16[896,1920]{1,0:T(8,128)(2,1)}), bf16[224,1920]{1,0:T(8,128)(2,1)}) %reduce-scatter.2.cloned.1.call-update) | async-done | bytes 860176 | tf_op jit(solution)/shard_map/reduce_scatter | solution.py:601
  185.9 2.0 collective-permute-start.31
  188.9 1.5 collective-permute-start.33
  191.3 3.6 %all-to-all-start.1 = ((bf16[4,56,1920]{2,1,0:T(8,128)(2,1)}), bf16[4,56,1920]{2,1,0:T(8,128)(2,1)S(1)}, u32[]{:S(2)}, u32[]{:S(2)}) async-start(bf16[4,56,1920]{2,1,0:T(8,128)(2,1)} %bitcast.68), calls=%async_computation.2 | async-start | bytes 1720320 | tf_op jit(solution)/shard_map/all_to_all | solution.py:67
  194.9 5.7 %collective-permute-done.32 = bf16[56,1152]{1,0:T(8,128)(2,1)S(1)} collective-permute-done((bf16[56,1152]{1,0:T(8,128)(2,1)S(1)}, bf16[56,1152]{1,0:T(8,128)(2,1)S(1)}, u32[]{:S(2)}, u32[]{:S(2)}) %collective-permute-start.32) | collective-permute-done | bytes 129056 | tf_op jit(solution)/shard_map/ppermute | solution.py:64
  201.9 1.5 collective-permute-start.34
  (251 shorter events, 46.8 us)
Async XLA Ops:
  11.1 12.2 %collective-permute-start = (bf16[56,1024]{1,0:T(8,128)(2,1)S(1)}, bf16[56,1024]{1,0:T(8,128)(2,1)S(1)}, u32[]{:S(2)}, u32[]{:S(2)}) collective-permute-start(bf16[56,1024]{1,0:T(8,128)(2,1)S(1)} %pad_maximum_fusion.9), channel_id=1, source_target_pairs={{0,8},{2,10},{4,12},{6,14},{8,0},{10,2},{12,4},{14,6},{16,24},{18,... | collective-permute-start | bytes 344072 | tf_op jit(solution)/shard_map/ppermute | solution.py:64
  14.2 11.7 %collective-permute-start.1 = (bf16[56,1024]{1,0:T(8,128)(2,1)S(1)}, bf16[56,1024]{1,0:T(8,128)(2,1)S(1)}, u32[]{:S(2)}, u32[]{:S(2)}) collective-permute-start(bf16[56,1024]{1,0:T(8,128)(2,1)S(1)} %pad_maximum_fusion.9), channel_id=1, source_target_pairs={{0,16},{2,18},{4,20},{6,22},{8,24},{10,26},{12,28},{14,30},{16,0},... | collective-permute-start | bytes 344072 | tf_op jit(solution)/shard_map/ppermute | solution.py:64
  16.7 9.1 %collective-permute-start.2 = (bf16[56,1024]{1,0:T(8,128)(2,1)S(1)}, bf16[56,1024]{1,0:T(8,128)(2,1)S(1)}, u32[]{:S(2)}, u32[]{:S(2)}) collective-permute-start(bf16[56,1024]{1,0:T(8,128)(2,1)S(1)} %pad_maximum_fusion.9), channel_id=1, source_target_pairs={{0,24},{2,26},{4,28},{6,30},{8,16},{10,18},{12,20},{14,22},{16,8},... | collective-permute-start | bytes 344072 | tf_op jit(solution)/shard_map/ppermute | solution.py:64
  16.8 15.9 %all-to-all-start = ((bf16[4,56,1920]{2,1,0:T(8,128)(2,1)}), bf16[4,56,1920]{2,1,0:T(8,128)(2,1)S(1)}, u32[]{:S(2)}, u32[]{:S(2)}) async-start(bf16[4,56,1920]{2,1,0:T(8,128)(2,1)} %maximum_bitcast_fusion), calls=%async_computation | async-start | bytes 1720320 | tf_op jit(solution)/shard_map/all_to_all | solution.py:67
  20.3 85.1 %all-gather.3.cloned.1.call-start = ((), (), s32[]{:S(2)}) async-start(), calls=%async_computation.3 | async-start | bytes 4300800 | tf_op jit(solution)/shard_map/all_gather | solution.py:542
  33.7 152.2 %reduce-scatter.2.cloned.1.call-start = ((), (), s32[]{:S(2)}) async-start(), calls=%async_computation.4 | async-start | bytes 4300800 | tf_op jit(solution)/shard_map/reduce_scatter | solution.py:601
  34.0 14.6 %copy-start.4 = (bf16[2,64,896]{2,1,0:T(8,128)(2,1)S(1)}, bf16[2,64,896]{2,1,0:T(8,128)(2,1)}, u32[]{:S(2)}) copy-start(bf16[2,64,896]{2,1,0:T(8,128)(2,1)} %param.16) | copy-start | bytes 688132
  34.0 28.9 %collective-permute-start.8 = (bf16[4,56,448]{2,1,0:T(8,128)(2,1)S(1)}, bf16[4,56,448]{2,1,0:T(8,128)(2,1)}, u32[]{:S(2)}, u32[]{:S(2)}) collective-permute-start(bf16[4,56,448]{2,1,0:T(8,128)(2,1)S(1)} %slice.115), channel_id=1, source_target_pairs={{0,4},{2,6},{4,0},{6,2},{8,12},{10,14},{12,8},{14,10},{16,20},{18,... | collective-permute-start | bytes 602120 | tf_op jit(solution)/shard_map/ppermute | solution.py:64
  50.6 17.7 %copy-start.8 = (bf16[2,64,896]{2,1,0:T(8,128)(2,1)S(1)}, bf16[2,64,896]{2,1,0:T(8,128)(2,1)}, u32[]{:S(2)}) copy-start(bf16[2,64,896]{2,1,0:T(8,128)(2,1)} %cotangent_ref.1) | copy-start | bytes 688132
  50.6 7.6 %collective-permute-start.3 = (bf16[128,128]{1,0:T(8,128)(2,1)S(1)}, bf16[128,128]{1,0:T(8,128)(2,1)S(1)}, u32[]{:S(2)}, u32[]{:S(2)}) collective-permute-start(bf16[128,128]{1,0:T(8,128)(2,1)S(1)} %get-tuple-element.71), channel_id=1, source_target_pairs={{0,8},{2,10},{4,12},{6,14},{8,0},{10,2},{12,4},{14,6},{16,24},{18,... | collective-permute-start | bytes 98312 | tf_op jit(solution)/shard_map/ppermute | solution.py:64
  51.5 10.2 %collective-permute-start.4 = (bf16[128,128]{1,0:T(8,128)(2,1)S(1)}, bf16[128,128]{1,0:T(8,128)(2,1)}, u32[]{:S(2)}, u32[]{:S(2)}) collective-permute-start(bf16[128,128]{1,0:T(8,128)(2,1)S(1)} %get-tuple-element.71), channel_id=1, source_target_pairs={{0,16},{2,18},{4,20},{6,22},{8,24},{10,26},{12,28},{14,30},{16,0},... | collective-permute-start | bytes 98312 | tf_op jit(solution)/shard_map/ppermute | solution.py:64
  54.9 6.7 %collective-permute-start.5 = (bf16[128,128]{1,0:T(8,128)(2,1)S(1)}, bf16[128,128]{1,0:T(8,128)(2,1)}, u32[]{:S(2)}, u32[]{:S(2)}) collective-permute-start(bf16[128,128]{1,0:T(8,128)(2,1)S(1)} %get-tuple-element.71), channel_id=1, source_target_pairs={{0,24},{2,26},{4,28},{6,30},{8,16},{10,18},{12,20},{14,22},{16,8},... | collective-permute-start | bytes 98312 | tf_op jit(solution)/shard_map/ppermute | solution.py:64
  62.4 5.0 %collective-permute-start.6 = (bf16[4,128,128]{2,1,0:T(8,128)(2,1)S(1)}, bf16[4,128,128]{2,1,0:T(8,128)(2,1)S(1)}, u32[]{:S(2)}, u32[]{:S(2)}) collective-permute-start(bf16[4,128,128]{2,1,0:T(8,128)(2,1)S(1)} %get-tuple-element.140), channel_id=1, source_target_pairs={{0,4},{2,6},{4,0},{6,2},{8,12},{10,14},{12,8},{14,10},{16,20},{18,... | collective-permute-start | bytes 393224 | tf_op jit(solution)/shard_map/ppermute | solution.py:64
  65.0 6.6 %collective-permute-start.9 = (bf16[4,2,56,448]{3,2,0,1:T(8,128)(2,1)}, bf16[4,2,56,448]{3,2,0,1:T(8,128)(2,1)}, u32[]{:S(2)}, u32[]{:S(2)}) collective-permute-start(bf16[4,2,56,448]{3,2,0,1:T(8,128)(2,1)} %pad_maximum_fusion.4), channel_id=1, source_target_pairs={{0,2},{2,0},{4,6},{6,4},{8,10},{10,8},{12,14},{14,12},{16,18},{18,... | collective-permute-start | bytes 1204232 | tf_op jit(solution)/shard_map/ppermute | solution.py:64
  68.2 1.5 collective-permute-start.7
  68.2 10.5 %collective-permute-start.11 = (bf16[128,896]{1,0:T(8,128)(2,1)S(1)}, bf16[128,896]{1,0:T(8,128)(2,1)}, u32[]{:S(2)}, u32[]{:S(2)}) collective-permute-start(bf16[128,896]{1,0:T(8,128)(2,1)S(1)} %bitcast.158), channel_id=1, source_target_pairs={{0,4},{2,6},{4,0},{6,2},{8,12},{10,14},{12,8},{14,10},{16,20},{18,... | collective-permute-start | bytes 688136 | tf_op jit(solution)/shard_map/ppermute | solution.py:64
  77.2 15.1 %copy-start.24 = (bf16[2,64,448]{2,1,0:T(8,128)(2,1)}, bf16[2,64,448]{2,1,0:T(8,128)(2,1)S(1)}, u32[]{:S(2)}) copy-start(bf16[2,64,448]{2,1,0:T(8,128)(2,1)S(1)} %get-tuple-element.103) | copy-start | bytes 344068
  77.2 7.7 %collective-permute-start.10 = (bf16[128,896]{1,0:T(8,128)(2,1)S(1)}, bf16[128,896]{1,0:T(8,128)(2,1)S(1)}, u32[]{:S(2)}, u32[]{:S(2)}) collective-permute-start(bf16[128,896]{1,0:T(8,128)(2,1)S(1)} %bitcast.166), channel_id=1, source_target_pairs={{0,1},{1,0},{2,3},{3,2},{4,5},{5,4},{6,7},{7,6},{8,9},{9,8},{10,11... | collective-permute-start | bytes 688136 | tf_op jit(solution)/shard_map/ppermute | solution.py:46
  79.7 5.3 %collective-permute-start.12 = (bf16[256,896]{1,0:T(8,128)(2,1)S(1)}, bf16[256,896]{1,0:T(8,128)(2,1)S(1)}, u32[]{:S(2)}, u32[]{:S(2)}) collective-permute-start(bf16[256,896]{1,0:T(8,128)(2,1)S(1)} %pad_maximum_fusion.5), channel_id=1, source_target_pairs={{0,2},{2,0},{4,6},{6,4},{8,10},{10,8},{12,14},{14,12},{16,18},{18,... | collective-permute-start | bytes 1376264 | tf_op jit(solution)/shard_map/ppermute | solution.py:64
  85.2 7.0 %collective-permute-start.13 = (bf16[128,896]{1,0:T(8,128)(2,1)S(1)}, bf16[128,896]{1,0:T(8,128)(2,1)S(1)}, u32[]{:S(2)}, u32[]{:S(2)}) collective-permute-start(bf16[128,896]{1,0:T(8,128)(2,1)S(1)} %get-tuple-element.119), channel_id=1, source_target_pairs={{0,4},{2,6},{4,0},{6,2},{8,12},{10,14},{12,8},{14,10},{16,20},{18,... | collective-permute-start | bytes 688136 | tf_op jit(solution)/shard_map/ppermute | solution.py:64
  92.2 1.9 collective-permute-start.14
  116.0 4.1 %collective-permute-start.15 = (bf16[256,896]{1,0:T(8,128)(2,1)}, bf16[256,896]{1,0:T(8,128)(2,1)}, u32[]{:S(2)}, u32[]{:S(2)}) collective-permute-start(bf16[256,896]{1,0:T(8,128)(2,1)} %get-tuple-element.84), channel_id=1, source_target_pairs={{0,2},{2,0},{4,6},{6,4},{8,10},{10,8},{12,14},{14,12},{16,18},{18,... | collective-permute-start | bytes 1376264 | tf_op jit(solution)/shard_map/ppermute | solution.py:64
  120.1 19.7 %copy-start.3 = (bf16[4,2,2,56,448]{4,3,2,1,0:T(8,128)(2,1)S(1)}, bf16[4,2,2,56,448]{4,3,2,1,0:T(8,128)(2,1)}, u32[]{:S(2)}) copy-start(bf16[4,2,2,56,448]{4,3,2,1,0:T(8,128)(2,1)} %copy-done.2) | copy-start | bytes 2408452
  120.2 19.7 %copy-start.9 = (bf16[2,64,896]{2,1,0:T(8,128)(2,1)S(1)}, bf16[2,64,896]{2,1,0:T(8,128)(2,1)}, u32[]{:S(2)}) copy-start(bf16[2,64,896]{2,1,0:T(8,128)(2,1)} %cotangent_ref.1) | copy-start | bytes 688132
  120.2 19.7 %copy-start.17 = (bf16[128,448]{1,0:T(8,128)(2,1)S(1)}, bf16[128,448]{1,0:T(8,128)(2,1)}, u32[]{:S(2)}) copy-start(bf16[128,448]{1,0:T(8,128)(2,1)} %copy-done.15) | copy-start | bytes 344068
  121.4 8.1 %collective-permute-start.16 = (bf16[128,896]{1,0:T(8,128)(2,1)S(1)}, bf16[128,896]{1,0:T(8,128)(2,1)S(1)}, u32[]{:S(2)}, u32[]{:S(2)}) collective-permute-start(bf16[128,896]{1,0:T(8,128)(2,1)S(1)} %add_convert_fusion.6), channel_id=1, source_target_pairs={{0,4},{2,6},{4,0},{6,2},{8,12},{10,14},{12,8},{14,10},{16,20},{18,... | collective-permute-start | bytes 688136 | tf_op jit(solution)/shard_map/ppermute | solution.py:64
  123.0 7.7 %collective-permute-start.17 = (bf16[256,896]{1,0:T(8,128)(2,1)}, bf16[256,896]{1,0:T(8,128)(2,1)S(1)}, u32[]{:S(2)}, u32[]{:S(2)}) collective-permute-start(bf16[256,896]{1,0:T(8,128)(2,1)} %copy-done.26), channel_id=1, source_target_pairs={{0,2},{2,0},{4,6},{6,4},{8,10},{10,8},{12,14},{14,12},{16,18},{18,... | collective-permute-start | bytes 1376264 | tf_op jit(solution)/shard_map/ppermute | solution.py:64
  130.6 7.6 %collective-permute-start.18 = (bf16[128,896]{1,0:T(8,128)(2,1)S(1)}, bf16[128,896]{1,0:T(8,128)(2,1)S(1)}, u32[]{:S(2)}, u32[]{:S(2)}) collective-permute-start(bf16[128,896]{1,0:T(8,128)(2,1)S(1)} %add_convert_fusion.5.own_ref), channel_id=1, source_target_pairs={{0,1},{1,0},{2,3},{3,2},{4,5},{5,4},{6,7},{7,6},{8,9},{9,8},{10,11... | collective-permute-start | bytes 688136 | tf_op jit(solution)/shard_map/ppermute | solution.py:608
  138.3 6.6 %collective-permute-start.19 = (bf16[128,896]{1,0:T(8,128)(2,1)S(1)}, bf16[128,896]{1,0:T(8,128)(2,1)S(1)}, u32[]{:S(2)}, u32[]{:S(2)}) collective-permute-start(bf16[128,896]{1,0:T(8,128)(2,1)S(1)} %slice.121), channel_id=1, source_target_pairs={{0,4},{2,6},{4,0},{6,2},{8,12},{10,14},{12,8},{14,10},{16,20},{18,... | collective-permute-start | bytes 688136 | tf_op jit(solution)/shard_map/ppermute | solution.py:64
  145.7 1.6 collective-permute-start.21
  149.0 6.2 %collective-permute-start.23 = (bf16[8,56,896]{2,1,0:T(8,128)(2,1)}, bf16[8,56,896]{2,1,0:T(8,128)(2,1)}, u32[]{:S(2)}, u32[]{:S(2)}) collective-permute-start(bf16[8,56,896]{2,1,0:T(8,128)(2,1)} %get-tuple-element.104), channel_id=1, source_target_pairs={{0,2},{2,0},{4,6},{6,4},{8,10},{10,8},{12,14},{14,12},{16,18},{18,... | collective-permute-start | bytes 2408456 | tf_op jit(solution)/shard_map/ppermute | solution.py:64
  149.4 5.7 %collective-permute-start.22 = (bf16[512,128]{1,0:T(8,128)(2,1)S(1)}, bf16[512,128]{1,0:T(8,128)(2,1)S(1)}, u32[]{:S(2)}, u32[]{:S(2)}) collective-permute-start(bf16[512,128]{1,0:T(8,128)(2,1)S(1)} %slice.151), channel_id=1, source_target_pairs={{0,4},{2,6},{4,0},{6,2},{8,12},{10,14},{12,8},{14,10},{16,20},{18,... | collective-permute-start | bytes 393224 | tf_op jit(solution)/shard_map/ppermute | solution.py:64
  155.1 15.6 %copy-start.7 = (bf16[128,896]{1,0:T(8,128)(2,1)S(1)}, bf16[128,896]{1,0:T(8,128)(2,1)}, u32[]{:S(2)}) copy-start(bf16[128,896]{1,0:T(8,128)(2,1)} %copy-done.6) | copy-start | bytes 688132
  155.2 15.6 %copy-start.13 = (bf16[128,896]{1,0:T(8,128)(2,1)S(1)}, bf16[128,896]{1,0:T(8,128)(2,1)}, u32[]{:S(2)}) copy-start(bf16[128,896]{1,0:T(8,128)(2,1)} %copy-done.12) | copy-start | bytes 688132
  155.2 15.6 %copy-start.19 = (bf16[2,64,448]{2,1,0:T(8,128)(2,1)S(1)}, bf16[2,64,448]{2,1,0:T(8,128)(2,1)}, u32[]{:S(2)}) copy-start(bf16[2,64,448]{2,1,0:T(8,128)(2,1)} %copy-done.18) | copy-start | bytes 344068
  158.5 11.0 %collective-permute-start.27 = (bf16[4,56,896]{2,1,0:T(8,128)(2,1)}, bf16[4,56,896]{2,1,0:T(8,128)(2,1)}, u32[]{:S(2)}, u32[]{:S(2)}) collective-permute-start(bf16[4,56,896]{2,1,0:T(8,128)(2,1)} %dynamic-slice_bitcast_fusion), channel_id=1, source_target_pairs={{0,4},{2,6},{4,0},{6,2},{8,12},{10,14},{12,8},{14,10},{16,20},{18,... | collective-permute-start | bytes 1204232 | tf_op jit(solution)/shard_map/ppermute | solution.py:64
  160.0 6.4 %collective-permute-start.24 = (bf16[128,128]{1,0:T(8,128)(2,1)S(1)}, bf16[128,128]{1,0:T(8,128)(2,1)S(1)}, u32[]{:S(2)}, u32[]{:S(2)}) collective-permute-start(bf16[128,128]{1,0:T(8,128)(2,1)S(1)} %get-tuple-element.136), channel_id=1, source_target_pairs={{0,8},{2,10},{4,12},{6,14},{8,0},{10,2},{12,4},{14,6},{16,24},{18,... | collective-permute-start | bytes 98312 | tf_op jit(solution)/shard_map/ppermute | solution.py:64
  160.1 6.7 %collective-permute-start.25 = (bf16[128,128]{1,0:T(8,128)(2,1)S(1)}, bf16[128,128]{1,0:T(8,128)(2,1)S(1)}, u32[]{:S(2)}, u32[]{:S(2)}) collective-permute-start(bf16[128,128]{1,0:T(8,128)(2,1)S(1)} %get-tuple-element.138), channel_id=1, source_target_pairs={{0,16},{2,18},{4,20},{6,22},{8,24},{10,26},{12,28},{14,30},{16,0},... | collective-permute-start | bytes 98312 | tf_op jit(solution)/shard_map/ppermute | solution.py:64
  161.4 6.9 %collective-permute-start.26 = (bf16[128,128]{1,0:T(8,128)(2,1)S(1)}, bf16[128,128]{1,0:T(8,128)(2,1)S(1)}, u32[]{:S(2)}, u32[]{:S(2)}) collective-permute-start(bf16[128,128]{1,0:T(8,128)(2,1)S(1)} %get-tuple-element.137), channel_id=1, source_target_pairs={{0,24},{2,26},{4,28},{6,30},{8,16},{10,18},{12,20},{14,22},{16,8},... | collective-permute-start | bytes 98312 | tf_op jit(solution)/shard_map/ppermute | solution.py:64
  164.6 8.7 %collective-permute-start.20 = (bf16[128,896]{1,0:T(8,128)(2,1)}, bf16[128,896]{1,0:T(8,128)(2,1)S(1)}, u32[]{:S(2)}, u32[]{:S(2)}) collective-permute-start(bf16[128,896]{1,0:T(8,128)(2,1)} %add_convert_fusion.4), channel_id=1, source_target_pairs={{0,1},{1,0},{2,3},{3,2},{4,5},{5,4},{6,7},{7,6},{8,9},{9,8},{10,11... | collective-permute-start | bytes 688136 | tf_op jit(solution)/shard_map/ppermute | solution.py:652
  173.1 3.3 %collective-permute-start.29 = (bf16[8,56,256]{2,1,0:T(8,128)(2,1)S(1)}, bf16[8,56,256]{2,1,0:T(8,128)(2,1)S(1)}, u32[]{:S(2)}, u32[]{:S(2)}) collective-permute-start(bf16[8,56,256]{2,1,0:T(8,128)(2,1)S(1)} %get-tuple-element.112), channel_id=1, source_target_pairs={{0,2},{2,0},{4,6},{6,4},{8,10},{10,8},{12,14},{14,12},{16,18},{18,... | collective-permute-start | bytes 688136 | tf_op jit(solution)/shard_map/ppermute | solution.py:64
  175.0 8.0 %collective-permute-start.28 = (bf16[128,896]{1,0:T(8,128)(2,1)S(1)}, bf16[128,896]{1,0:T(8,128)(2,1)S(1)}, u32[]{:S(2)}, u32[]{:S(2)}) collective-permute-start(bf16[128,896]{1,0:T(8,128)(2,1)S(1)} %get-tuple-element.109), channel_id=1, source_target_pairs={{0,1},{1,0},{2,3},{3,2},{4,5},{5,4},{6,7},{7,6},{8,9},{9,8},{10,11... | collective-permute-start | bytes 688136 | tf_op jit(solution)/shard_map/ppermute | solution.py:46
  176.6 6.6 %collective-permute-start.30 = (bf16[4,56,256]{2,1,0:T(8,128)(2,1)S(1)}, bf16[4,56,256]{2,1,0:T(8,128)(2,1)S(1)}, u32[]{:S(2)}, u32[]{:S(2)}) collective-permute-start(bf16[4,56,256]{2,1,0:T(8,128)(2,1)S(1)} %dynamic-slice_bitcast_fusion.4), channel_id=1, source_target_pairs={{0,4},{2,6},{4,0},{6,2},{8,12},{10,14},{12,8},{14,10},{16,20},{18,... | collective-permute-start | bytes 344072 | tf_op jit(solution)/shard_map/ppermute | solution.py:64
  185.9 9.0 %collective-permute-start.31 = (bf16[56,1152]{1,0:T(8,128)(2,1)S(1)}, bf16[56,1152]{1,0:T(8,128)(2,1)S(1)}, u32[]{:S(2)}, u32[]{:S(2)}) collective-permute-start(bf16[56,1152]{1,0:T(8,128)(2,1)S(1)} %get-tuple-element.129), channel_id=1, source_target_pairs={{0,8},{2,10},{4,12},{6,14},{8,0},{10,2},{12,4},{14,6},{16,24},{18,... | collective-permute-start | bytes 387080 | tf_op jit(solution)/shard_map/ppermute | solution.py:64
  187.9 12.7 %collective-permute-start.32 = (bf16[56,1152]{1,0:T(8,128)(2,1)S(1)}, bf16[56,1152]{1,0:T(8,128)(2,1)S(1)}, u32[]{:S(2)}, u32[]{:S(2)}) collective-permute-start(bf16[56,1152]{1,0:T(8,128)(2,1)S(1)} %get-tuple-element.131), channel_id=1, source_target_pairs={{0,16},{2,18},{4,20},{6,22},{8,24},{10,26},{12,28},{14,30},{16,0},... | collective-permute-start | bytes 387080 | tf_op jit(solution)/shard_map/ppermute | solution.py:64
  188.9 11.7 %collective-permute-start.33 = (bf16[56,1152]{1,0:T(8,128)(2,1)S(1)}, bf16[56,1152]{1,0:T(8,128)(2,1)S(1)}, u32[]{:S(2)}, u32[]{:S(2)}) collective-permute-start(bf16[56,1152]{1,0:T(8,128)(2,1)S(1)} %get-tuple-element.130), channel_id=1, source_target_pairs={{0,24},{2,26},{4,28},{6,30},{8,16},{10,18},{12,20},{14,22},{16,8},... | collective-permute-start | bytes 387080 | tf_op jit(solution)/shard_map/ppermute | solution.py:64
  191.3 16.0 %all-to-all-start.1 = ((bf16[4,56,1920]{2,1,0:T(8,128)(2,1)}), bf16[4,56,1920]{2,1,0:T(8,128)(2,1)S(1)}, u32[]{:S(2)}, u32[]{:S(2)}) async-start(bf16[4,56,1920]{2,1,0:T(8,128)(2,1)} %bitcast.68), calls=%async_computation.2 | async-start | bytes 1720320 | tf_op jit(solution)/shard_map/all_to_all | solution.py:67
  201.9 4.2 %collective-permute-start.34 = (f32[56]{0:T(128)S(1)}, f32[56]{0:T(128)S(1)}, u32[]{:S(2)}, u32[]{:S(2)}) collective-permute-start(f32[56]{0:T(128)S(1)} %convert_divide_fusion), channel_id=1, source_target_pairs={{0,1},{1,0},{2,3},{3,2},{4,5},{5,4},{6,7},{7,6},{8,9},{9,8},{10,11... | collective-permute-start | bytes 680 | tf_op jit(solution)/shard_map/ppermute | solution.py:728
  (38 other events, 163.9 us)
Sparse Core Ops, SparseCore 0:
  33.8 71.5 all-gather.2
  120.3 65.5 reduce-scatter.1

commit v4 on v3

--- a/solution.py
+++ b/solution.py
@@ -16,6 +16,7 @@
 LOWEST = -1e29
 BRIEF = pl.CostEstimate(flops=1, bytes_accessed=1, transcendentals=0)
 VMEM_LIMIT = 48 * 1024 * 1024
+FFN_VMEM_LIMIT = 56 * 1024 * 1024
 
 
 def rope_tables(positions, head_dim):
@@ -361,53 +362,106 @@
     )(*inputs)
 
 
-def ffn_kernel(part, token_ref, w_ref, *refs):
-    near_refs, mixed_refs, active_ref, d_gate_up_ref = refs[:2], refs[2:4], *refs[4:]
+def ffn_kernel(
+    part,
+    token_source,
+    w_source,
+    near_kept,
+    near_sent,
+    mixed_kept,
+    mixed_sent,
+    d_w_target,
+    token_ref,
+    w_ref,
+    active_ref,
+    d_gate_up_ref,
+    grad_ref,
+    model_ref,
+    semaphores,
+    sent_semaphores,
+):
+    models = (near_kept, near_sent, mixed_kept, mixed_sent)
     block = token_ref.shape[0] // 4
+    gates = slice(0, 2 * part)
+    downs = slice(2 * part, 3 * part)
+    rows_of = lambda index: pl.ds(index * block, block)
+
+    def load(source, target, index):
+        copy = pltpu.make_async_copy(source, target, semaphores.at[index])
+        copy.start()
+        return copy
+
+    copies = []
+
+    def send(source, target):
+        index = len(copies)
+        copy = pltpu.make_async_copy(source, target, sent_semaphores.at[index])
+        copy.start()
+        copies.append(copy)
+
+    def send_model(index, values):
+        model_ref[index] = values.astype(jnp.bfloat16)
+        send(model_ref.at[index], models[index])
+
+    w_gates = load(w_source.at[:, gates], w_ref.at[:, gates], 4)
+    tokens = {1: load(token_source.at[rows_of(1)], token_ref.at[rows_of(1)], 1)}
+    tokens[3] = load(token_source.at[rows_of(3)], token_ref.at[rows_of(3)], 3)
+    w_downs = load(w_source.at[:, downs], w_ref.at[:, downs], 5)
+    for index in (0, 2):
+        tokens[index] = load(token_source.at[rows_of(index)], token_ref.at[rows_of(index)], index)
     for half in (1, 0):
-        rows = pl.ds(half * block, block)
-        gate_up = dot(token_ref[rows, :], w_ref[:, : 2 * part], 1, 0)
+        rows = rows_of(half)
+        tokens[half].wait()
+        if half == 1:
+            w_gates.wait()
+        gate_up = dot(token_ref[rows, :], w_ref[:, gates], 1, 0)
         gate, up_values = gate_up[:, :part], gate_up[:, part:]
         sigma = 1.0 / (1.0 + jnp.exp(-gate))
         silu = gate * sigma
         active = (silu * up_values).astype(jnp.bfloat16)
         active_ref[rows, :] = active
-        d_active = dot(token_ref[pl.ds((2 + half) * block, block), :], w_ref[:, 2 * part :], 1, 0)
+        tokens[2 + half].wait()
+        if half == 1:
+            w_downs.wait()
+        d_active = dot(token_ref[rows_of(2 + half), :], w_ref[:, downs], 1, 0)
         d_gate = d_active * up_values * sigma * (1.0 + gate * (1.0 - sigma))
         d_gate_up = jnp.concatenate([d_gate, d_active * silu], axis=1).astype(jnp.bfloat16)
         d_gate_up_ref[rows, :] = d_gate_up
-        near_refs[half][...] = dot(d_gate_up, w_ref[:, : 2 * part], 1, 1).astype(jnp.bfloat16)
-        mixed_refs[half][...] = dot(active, w_ref[:, 2 * part :], 1, 1).astype(jnp.bfloat16)
+        send_model(half, dot(d_gate_up, w_ref[:, gates], 1, 1))
+        send_model(2 + half, dot(active, w_ref[:, downs], 1, 1))
+    for index in range(3):
+        columns = slice(index * part, (index + 1) * part)
+        left = token_ref[: 2 * block, :] if index < 2 else token_ref[2 * block :, :]
+        right = d_gate_up_ref[:, columns] if index < 2 else active_ref[...]
+        grad_ref[:, columns] = dot(left, right, 0, 0).astype(jnp.bfloat16)
+        send(grad_ref.at[:, columns], d_w_target.at[:, columns])
+    for copy in copies:
+        copy.wait()
 
 
 def ffn_call(part, tokens, w_ffn):
     block, width = tokens.shape[0] // 4, tokens.shape[1]
     model = jax.ShapeDtypeStruct((block, width), jnp.bfloat16)
-    units = lambda count: jax.ShapeDtypeStruct((2 * block, count * part), jnp.bfloat16)
-    return whole_call(
+    far = pl.BlockSpec(memory_space=pltpu.HBM)
+    return pl.pallas_call(
         functools.partial(ffn_kernel, part),
-        "ffn",
-        (tokens, w_ffn),
-        [model, model, model, model, units(1), units(2)],
-    )
-
-
-def ffn_grad_kernel(part, token_ref, active_ref, d_gate_up_ref, out_ref):
-    half = token_ref.shape[0] // 2
-    for index in range(3):
-        columns = slice(index * part, (index + 1) * part)
-        left = token_ref[:half, :] if index < 2 else token_ref[half:, :]
-        right = d_gate_up_ref[:, columns] if index < 2 else active_ref[...]
-        out_ref[:, columns] = dot(left, right, 0, 0).astype(jnp.bfloat16)
-
-
-def ffn_grad_call(part, tokens, active, d_gate_up):
-    return whole_call(
-        functools.partial(ffn_grad_kernel, part),
-        "ffn_grad",
-        (tokens, active, d_gate_up),
-        [jax.ShapeDtypeStruct((tokens.shape[1], 3 * part), jnp.bfloat16)],
-    )[0]
+        in_specs=[far, far],
+        out_specs=[far] * 5,
+        out_shape=[model] * 4 + [jax.ShapeDtypeStruct(w_ffn.shape, jnp.bfloat16)],
+        scratch_shapes=[
+            pltpu.VMEM(tokens.shape, jnp.bfloat16),
+            pltpu.VMEM(w_ffn.shape, jnp.bfloat16),
+            pltpu.VMEM((2 * block, part), jnp.bfloat16),
+            pltpu.VMEM((2 * block, 2 * part), jnp.bfloat16),
+            pltpu.VMEM(w_ffn.shape, jnp.bfloat16),
+            pltpu.VMEM((4, block, width), jnp.bfloat16),
+            pltpu.SemaphoreType.DMA((6,)),
+            pltpu.SemaphoreType.DMA((7,)),
+        ],
+        compiler_params=pltpu.CompilerParams(vmem_limit_bytes=FFN_VMEM_LIMIT),
+        cost_estimate=BRIEF,
+        name="ffn",
+    )(tokens, w_ffn)
 
 
 def split_rows(total, place_ref, share, kept_ref, sent_ref):
@@ -536,11 +590,15 @@
     cosine, sine = rope_tables(row_pos.reshape(count), HEAD)
     cosine, sine = jnp.tile(cosine, (1, 2)), jnp.tile(sine, (1, 2))
 
-    w_ffn, w_attn, key_pos, query_pos, cosine, sine = together(
-        w_ffn, w_attn, key_pos, query_pos, cosine, sine
+    qkv_width = query_width + 2 * HEAD
+    row = jnp.arange(width)[:, None] % share
+    unit = jnp.arange(qkv_width)[None, :]
+    same = (row == unit % share).astype(jnp.bfloat16)
+    column = (unit.T // share + 2 == jnp.arange(128)[None, :]).astype(jnp.float32)
+    w_ffn, w_attn, key_pos, query_pos, cosine, sine, same, column = together(
+        w_ffn, w_attn, key_pos, query_pos, cosine, sine, same, column
     )
     w_ffn = lax.all_gather(w_ffn, "ctx", axis=0, tiled=True, axis_index_groups=groups.far)
-    qkv_width = query_width + 2 * HEAD
     w_qkv = groups.spread_near(w_attn[:, :, :qkv_width])
     grads_in = cotangent.reshape(count, width)
 
@@ -592,15 +650,11 @@
     normed_two, _ = norm_apply(hidden)
     near_two = groups.gather_near(normed_two.astype(jnp.bfloat16))
     token_parts = jnp.concatenate([*near_two, *grads_near], axis=0)
-    near_kept, near_sent, mixed_kept, mixed_sent, active, d_gate_up = ffn_call(
-        part, token_parts, w_ffn
-    )
-    d_w_ffn = ffn_grad_call(part, token_parts, active, d_gate_up)
-    crossed = groups.flip(near_sent, 1)
-    crossed, d_w_ffn = together(crossed, d_w_ffn)
+    near_kept, near_sent, mixed_kept, mixed_sent, d_w_ffn = ffn_call(part, token_parts, w_ffn)
     d_w_ffn = lax.psum_scatter(
         d_w_ffn, "ctx", scatter_dimension=0, tiled=True, axis_index_groups=groups.far
     )
+    crossed = groups.flip(near_sent, 1)
     near_sent = groups.flip(add(near_kept[count:], crossed[count:]), 2)
     d_own = add(add(near_kept[:count], crossed[:count]), near_sent)
     mixed_sent = groups.flip(mixed_sent, 1)
@@ -665,21 +719,21 @@
     d_pairs = add(d_pairs[0], crossed).reshape(2, groups.high * count, 2 * HEAD)
     d_pairs = add(d_pairs[0], groups.flip(d_pairs[1], 2)).reshape(groups.high, count, 2 * HEAD)
     d_pairs, wide_crossed = together(d_pairs, wide_crossed)
-    near_half = lambda kept, crossed: halve(
-        groups, add(kept, crossed).reshape((groups.high, 2) + kept.shape[1:]), 2, device, 1
-    )
-    d_w_wide = near_half(wide_kept, wide_crossed)
+
+    def near_half(kept, crossed):
+        pieces = add(kept, crossed).reshape((groups.high, 2) + kept.shape[1:])
+        mine = device // 2 % 2
+        sent = lax.dynamic_index_in_dim(pieces, 1 - mine, 1, False)
+        return lax.dynamic_index_in_dim(pieces, mine, 1, False), groups.flip(sent, 2)
+
+    wide_kept, wide_beside = near_half(wide_kept, wide_crossed)
     pair_grads = d_pairs[0].astype(jnp.float32)
     for m in range(1, groups.high):
         pair_grads = pair_grads + groups.flip(d_pairs[m], groups.far_bits[m]).astype(jnp.float32)
-    pair_grads, d_w_wide = together(pair_grads, d_w_wide)
+    pair_grads, wide_beside = together(pair_grads, wide_beside)
     mixed = hidden + mixed_own.astype(jnp.float32) + mixed_other.astype(jnp.float32)
     mixed = mixed.astype(jnp.bfloat16)
 
-    row = jnp.arange(width)[:, None] % share
-    unit = jnp.arange(qkv_width)[None, :]
-    same = (row == unit % share).astype(jnp.bfloat16)
-    column = (unit.T // share + 2 == jnp.arange(128)[None, :]).astype(jnp.float32)
     d_weighted_low, narrow_kept, narrow_sent = whole_call(
         functools.partial(finish_kernel, share),
         "finish",
@@ -703,11 +757,14 @@
         ],
         place=device,
     )
+    narrow_kept, narrow_beside = near_half(narrow_kept, groups.flip(narrow_sent, 1))
+    narrow = jnp.concatenate(
+        [add(wide_kept, wide_beside), add(narrow_kept, narrow_beside)], axis=2
+    )
+    narrow, d_w_ffn, d_weighted_low, mixed = together(narrow, d_w_ffn, d_weighted_low, mixed)
     d_weighted = sum_tp(d_weighted_low)
     _, scale_one = norm_apply(inputs)
     tokens_grad = (d_hidden + norm_back(inputs, scale_one, d_weighted)).astype(jnp.bfloat16)
-    narrow = near_half(narrow_kept, groups.flip(narrow_sent, 1))
-    narrow, d_w_ffn = together(jnp.concatenate([d_w_wide, narrow], axis=2), d_w_ffn)
     d_w_ffn = groups.swap_near(d_w_ffn.reshape(low, share, 3 * part))
     narrow = groups.far_owner(narrow, device)
     d_w_wide, narrow = narrow[:, : 2 * query_width], narrow[:, 2 * query_width :]

time: 217 us -> 214 us (0.986)
  waiting for transfers between devices: 75.3 us -> 71.7 us
    pallas_call x7 -> x5, Pallas kernels: 21.8 us -> 10 us  [whole_call(): pl.pallas_call(kernel, in_specs=in_specs, out_specs=[whole] * len(out_sha...]
    pallas_call x0 -> x1, Pallas kernels: none -> 10.8 us  [ffn_call(): pl.pallas_call(functools.partial(ffn_kernel, part), in_specs=[far, far],...]
    ppermute x2, waiting for transfers between devices: 9.94 us -> 5.07 us  [sum_tp(): other = lax.ppermute(values, 'tp', [(0, 1), (1, 0)])]
    unnamed x98 -> x96, local copies, waits for them, and re-layouts: 11.9 us -> 9.88 us
    convert_element_type x8 -> x10, other arithmetic: 6.03 us -> 7.75 us  [add(): (one.astype(jnp.float32) + two.astype(jnp.float32)).astype(jnp.bfloat16)]
  transfers between devices with their start and end apart: 39 -> 39, of which waited for: 23 -> 22; matrix products, arithmetic and copies ran while one was open for 13% -> 16% of each run, Pallas kernels for 7% -> 5%
where the time goes in v4:
time: 214 us
  waiting for transfers between devices  71.7 us (34%)
  starting transfers between devices  44.9 us (21%)
  other arithmetic  29 us (14%)
  Pallas kernels  20.9 us (10%)
  local copies, waits for them, and re-layouts  18 us (8%)
  between operations  15.1 us (7%)
  blocking collectives  14.1 us (7%)
    ppermute x30, waiting for transfers between devices, flip(): lax.ppermute(values, 'ctx', [(i, i ^ bit) for i in range(self.count)])  42.6 us
    ppermute x30, starting transfers between devices, flip(): lax.ppermute(values, 'ctx', [(i, i ^ bit) for i in range(self.count)])  30 us
    all_gather x1, blocking collectives, spread_near(): whole = lax.all_gather(values, 'ctx', axis=0, axis_index_groups=self.near)  14.1 us
    pallas_call x1, Pallas kernels, ffn_call(): pl.pallas_call(functools.partial(ffn_kernel, part), in_specs=[far, far],...  10.8 us
    pallas_call x5, Pallas kernels, whole_call(): pl.pallas_call(kernel, in_specs=in_specs, out_specs=[whole] * len(out_sha...  10 us
    unnamed x96, local copies, waits for them, and re-layouts  9.88 us
    all_gather x1, waiting for transfers between devices, local(): lax.all_gather(w_ffn, 'ctx', axis=0, tiled=True, axis_index_groups=groups...  8.36 us
    convert_element_type x10, other arithmetic, add(): (one.astype(jnp.float32) + two.astype(jnp.float32)).astype(jnp.bfloat16)  7.75 us
  transfers between devices with their start and end apart: 39, of which 22 were waited for; matrix products, arithmetic and copies ran while one was open for 16% of the time, Pallas kernels for 5%

profile of v4, /device:TPU:0, one launch (start us, length us, event | category | flops | bytes accessed | tf_op | source)
XLA Modules:
  0.0 213.6 jit_solution(5478467268765848497)
XLA Ops:
  7.9 1.2 multiply_convert_fusion.1
  11.1 3.0 %collective-permute-start = (bf16[56,1024]{1,0:T(8,128)(2,1)S(1)}, bf16[56,1024]{1,0:T(8,128)(2,1)S(1)}, u32[]{:S(2)}, u32[]{:S(2)}) collective-permute-start(bf16[56,1024]{1,0:T(8,128)(2,1)S(1)} %pad_maximum_fusion.9), channel_id=1, source_target_pairs={{0,8},{2,10},{4,12},{6,14},{8,0},{10,2},{12,4},{14,6},{16,24},{18,... | collective-permute-start | bytes 344072 | tf_op jit(solution)/shard_map/ppermute | solution.py:65
  14.2 2.6 %collective-permute-start.1 = (bf16[56,1024]{1,0:T(8,128)(2,1)S(1)}, bf16[56,1024]{1,0:T(8,128)(2,1)S(1)}, u32[]{:S(2)}, u32[]{:S(2)}) collective-permute-start(bf16[56,1024]{1,0:T(8,128)(2,1)S(1)} %pad_maximum_fusion.9), channel_id=1, source_target_pairs={{0,16},{2,18},{4,20},{6,22},{8,24},{10,26},{12,28},{14,30},{16,0},... | collective-permute-start | bytes 344072 | tf_op jit(solution)/shard_map/ppermute | solution.py:65
  16.8 3.5 %all-to-all-start = ((bf16[4,56,1920]{2,1,0:T(8,128)(2,1)}), bf16[4,56,1920]{2,1,0:T(8,128)(2,1)S(1)}, u32[]{:S(2)}, u32[]{:S(2)}) async-start(bf16[4,56,1920]{2,1,0:T(8,128)(2,1)} %maximum_bitcast_fusion), calls=%async_computation | async-start | bytes 1720320 | tf_op jit(solution)/shard_map/all_to_all | solution.py:68
  24.1 1.3 compare_convert_fusion.same_ref
  27.1 5.6 %all-to-all-done = bf16[4,56,1920]{2,1,0:T(8,128)(2,1)S(1)} async-done(((bf16[4,56,1920]{2,1,0:T(8,128)(2,1)}), bf16[4,56,1920]{2,1,0:T(8,128)(2,1)S(1)}, u32[]{:S(2)}, u32[]{:S(2)}) %all-to-all-start) | async-done | bytes 860192 | tf_op jit(solution)/shard_map/all_to_all | solution.py:68
  35.1 14.1 %all-gather = bf16[16,56,576]{2,1,0:T(8,128)(2,1)S(1)} all-gather(bf16[4,56,576]{2,1,0:T(8,128)(2,1)S(1)} %slice.114), channel_id=2, replica_groups={{0,2,4,6},{8,10,12,14},{16,18,20,22},{24,26,28,30},{1,3,5,7},{9,11,13,1..., dimensions={0}, use_global_device_ids=true | all-gather | bytes 1290240 | tf_op jit(solution)/shard_map/all_gather | solution.py:87
  52.3 3.5 %collective-permute-start.4 = (bf16[128,128]{1,0:T(8,128)(2,1)S(1)}, bf16[128,128]{1,0:T(8,128)(2,1)S(1)}, u32[]{:S(2)}, u32[]{:S(2)}) collective-permute-start(bf16[128,128]{1,0:T(8,128)(2,1)S(1)} %get-tuple-element.73), channel_id=1, source_target_pairs={{0,16},{2,18},{4,20},{6,22},{8,24},{10,26},{12,28},{14,30},{16,0},... | collective-permute-start | bytes 98312 | tf_op jit(solution)/shard_map/ppermute | solution.py:65
  55.8 2.5 %collective-permute-done.3 = bf16[128,128]{1,0:T(8,128)(2,1)S(1)} collective-permute-done((bf16[128,128]{1,0:T(8,128)(2,1)S(1)}, bf16[128,128]{1,0:T(8,128)(2,1)S(1)}, u32[]{:S(2)}, u32[]{:S(2)}) %collective-permute-start.3) | collective-permute-done | bytes 32800 | tf_op jit(solution)/shard_map/ppermute | solution.py:65
  58.3 3.1 %collective-permute-done.4 = bf16[128,128]{1,0:T(8,128)(2,1)S(1)} collective-permute-done((bf16[128,128]{1,0:T(8,128)(2,1)S(1)}, bf16[128,128]{1,0:T(8,128)(2,1)S(1)}, u32[]{:S(2)}, u32[]{:S(2)}) %collective-permute-start.4) | collective-permute-done | bytes 32800 | tf_op jit(solution)/shard_map/ppermute | solution.py:65
  65.1 2.2 %collective-permute-done.6 = bf16[4,128,128]{2,1,0:T(8,128)(2,1)S(1)} collective-permute-done((bf16[4,128,128]{2,1,0:T(8,128)(2,1)S(1)}, bf16[4,128,128]{2,1,0:T(8,128)(2,1)S(1)}, u32[]{:S(2)}, u32[]{:S(2)}) %collective-permute-start.6) | collective-permute-done | bytes 131104 | tf_op jit(solution)/shard_map/ppermute | solution.py:65
  71.3 1.3 select_bitcast_fusion.1
  73.5 3.4 %forward.1 = (bf16[2,64,448]{2,1,0:T(8,128)(2,1)S(1)}, bf16[2,64,896]{2,1,0:T(8,128)(2,1)S(1)}, f32[1,8,128]{2,1,0:T(8,128)S(1)}, f32[2,1,448]{2,1,0:T(1,128)S(1)}) custom-call(bf16[2,64,448]{2,1,0:T(8,128)(2,1)S(1)} %bitcast.161, bf16[16,2,64,128]{3,2,1,0:T(8,128)(2,1)S(1)} %bitcast.153, s32[2,1024,1]{2,1,0:T(8,128)S(1)} %broadcast_add_fusion.key_pos_ref, ...), custom_call_target="tpu_custom_call" | custom-call | flops 1 | bytes 1 | tf_op jit(solution)/shard_map/forward/pallas_call | solution.py:183
  76.9 1.6 collective-permute-start.10
  79.6 5.1 %collective-permute-done.10 = bf16[128,896]{1,0:T(8,128)(2,1)S(1)} collective-permute-done((bf16[128,896]{1,0:T(8,128)(2,1)S(1)}, bf16[128,896]{1,0:T(8,128)(2,1)S(1)}, u32[]{:S(2)}, u32[]{:S(2)}) %collective-permute-start.10) | collective-permute-done | bytes 229408 | tf_op jit(solution)/shard_map/ppermute | solution.py:47
  86.5 6.1 %collective-permute-done.13 = bf16[128,896]{1,0:T(8,128)(2,1)S(1)} collective-permute-done((bf16[128,896]{1,0:T(8,128)(2,1)S(1)}, bf16[128,896]{1,0:T(8,128)(2,1)S(1)}, u32[]{:S(2)}, u32[]{:S(2)}) %collective-permute-start.13) | collective-permute-done | bytes 229408 | tf_op jit(solution)/shard_map/ppermute | solution.py:65
  97.0 8.4 %all-gather.3.cloned.1.call-done.w_source = bf16[896,1920]{1,0:T(8,128)(2,1)} async-done(((bf16[224,1920]{1,0:T(8,128)(2,1)}), bf16[896,1920]{1,0:T(8,128)(2,1)}) %all-gather.3.cloned.1.call-update) | async-done | bytes 3440656 | tf_op jit(solution)/shard_map/all_gather | solution.py:601
  105.4 10.8 %ffn.1 = (bf16[256,896]{1,0:T(8,128)(2,1)}, bf16[256,896]{1,0:T(8,128)(2,1)}, bf16[256,896]{1,0:T(8,128)(2,1)}, bf16[256,896]{1,0:T(8,128)(2,1)}, bf16[896,1920]{1,0:T(8,128)(2,1)}) custom-call(bf16[1024,896]{1,0:T(8,128)(2,1)} %constant_dynamic-update-slice_fusion.token_source, bf16[896,1920]{1,0:T(8,128)(2,1)} %all-gather.3.cloned.1.call-done.w_source), custom_call_target="tpu_custom_call" | custom-call | flops 1 | bytes 1 | tf_op jit(solution)/shard_map/ffn/pallas_call | solution.py:446
  116.6 2.0 collective-permute-done.15
  119.6 1.5 collective-permute-start.16
  121.1 6.2 %collective-permute-done.16 = bf16[128,896]{1,0:T(8,128)(2,1)S(1)} collective-permute-done((bf16[128,896]{1,0:T(8,128)(2,1)S(1)}, bf16[128,896]{1,0:T(8,128)(2,1)S(1)}, u32[]{:S(2)}, u32[]{:S(2)}) %collective-permute-start.16) | collective-permute-done | bytes 229408 | tf_op jit(solution)/shard_map/ppermute | solution.py:65
  128.4 1.5 collective-permute-start.18
  129.9 1.1 add_convert_fusion.1
  131.0 4.3 %collective-permute-done.18.other_ref = bf16[128,896]{1,0:T(8,128)(2,1)S(1)} collective-permute-done((bf16[128,896]{1,0:T(8,128)(2,1)S(1)}, bf16[128,896]{1,0:T(8,128)(2,1)S(1)}, u32[]{:S(2)}, u32[]{:S(2)}) %collective-permute-start.18) | collective-permute-done | bytes 229408 | tf_op jit(solution)/shard_map/ppermute | solution.py:662
  135.4 1.5 collective-permute-start.19
  136.9 4.2 %backward.1 = (f32[2,64,896]{2,1,0:T(8,128)S(1)}, bf16[2,64,896]{2,1,0:T(8,128)(2,1)S(1)}, bf16[2,64,448]{2,1,0:T(8,128)(2,1)S(1)}, bf16[16,2,64,128]{3,2,1,0:T(8,128)(2,1)S(1)}) custom-call(bf16[2,64,448]{2,1,0:T(8,128)(2,1)S(1)} %bitcast.162, bf16[16,2,64,128]{3,2,1,0:T(8,128)(2,1)S(1)} %bitcast.154, s32[2,1024,1]{2,1,0:T(8,128)S(1)} %broadcast_add_fusion.key_pos_ref, ...), custom_call_target="tpu_custom_call" | custom-call | flops 1 | bytes 1 | tf_op jit(solution)/shard_map/backward/pallas_call | solution.py:183
  142.4 1.5 collective-permute-done.20
  145.9 1.6 collective-permute-start.21
  147.4 4.4 %collective-permute-done.21 = bf16[512,128]{1,0:T(8,128)(2,1)} collective-permute-done((bf16[512,128]{1,0:T(8,128)(2,1)S(1)}, bf16[512,128]{1,0:T(8,128)(2,1)}, u32[]{:S(2)}, u32[]{:S(2)}) %collective-permute-start.21) | collective-permute-done | bytes 131104 | tf_op jit(solution)/shard_map/ppermute | solution.py:65
  152.8 1.6 add_convert_fusion
  156.1 1.5 collective-permute-start.26
  157.7 1.5 collective-permute-start.24
  159.2 2.9 %collective-permute-start.25 = (bf16[128,128]{1,0:T(8,128)(2,1)S(1)}, bf16[128,128]{1,0:T(8,128)(2,1)S(1)}, u32[]{:S(2)}, u32[]{:S(2)}) collective-permute-start(bf16[128,128]{1,0:T(8,128)(2,1)S(1)} %get-tuple-element.139), channel_id=1, source_target_pairs={{0,24},{2,26},{4,28},{6,30},{8,16},{10,18},{12,20},{14,22},{16,8},... | collective-permute-start | bytes 98312 | tf_op jit(solution)/shard_map/ppermute | solution.py:65
  162.2 1.5 collective-permute-start.29
  163.8 3.4 %collective-permute-done.24 = bf16[128,128]{1,0:T(8,128)(2,1)S(1)} collective-permute-done((bf16[128,128]{1,0:T(8,128)(2,1)S(1)}, bf16[128,128]{1,0:T(8,128)(2,1)S(1)}, u32[]{:S(2)}, u32[]{:S(2)}) %collective-permute-start.24) | collective-permute-done | bytes 32800 | tf_op jit(solution)/shard_map/ppermute | solution.py:65
  167.3 1.3 copy-done.3
  168.6 1.1 finish.1
  169.8 1.8 add_convert_fusion.2
  171.7 1.5 collective-permute-start.28
  174.2 3.0 %collective-permute-done.28 = bf16[4,56,256]{2,1,0:T(8,128)(2,1)S(1)} collective-permute-done((bf16[4,56,256]{2,1,0:T(8,128)(2,1)S(1)}, bf16[4,56,256]{2,1,0:T(8,128)(2,1)S(1)}, u32[]{:S(2)}, u32[]{:S(2)}) %collective-permute-start.28) | collective-permute-done | bytes 114720 | tf_op jit(solution)/shard_map/ppermute | solution.py:65
  177.3 4.7 %reduce-scatter.2.cloned.1.call-done = bf16[224,1920]{1,0:T(8,128)(2,1)} async-done(((bf16[896,1920]{1,0:T(8,128)(2,1)}), bf16[224,1920]{1,0:T(8,128)(2,1)}) %reduce-scatter.2.cloned.1.call-update) | async-done | bytes 860176 | tf_op jit(solution)/shard_map/reduce_scatter | solution.py:654
  182.1 2.0 collective-permute-start.31
  185.1 1.4 collective-permute-start.33
  186.7 3.6 %all-to-all-start.1 = ((bf16[4,56,1920]{2,1,0:T(8,128)(2,1)}), bf16[4,56,1920]{2,1,0:T(8,128)(2,1)S(1)}, u32[]{:S(2)}, u32[]{:S(2)}) async-start(bf16[4,56,1920]{2,1,0:T(8,128)(2,1)} %bitcast.186), calls=%async_computation.2 | async-start | bytes 1720320 | tf_op jit(solution)/shard_map/all_to_all | solution.py:68
  190.3 1.5 collective-permute-start.30
  191.8 5.0 %collective-permute-done.32 = bf16[56,1152]{1,0:T(8,128)(2,1)S(1)} collective-permute-done((bf16[56,1152]{1,0:T(8,128)(2,1)S(1)}, bf16[56,1152]{1,0:T(8,128)(2,1)S(1)}, u32[]{:S(2)}, u32[]{:S(2)}) %collective-permute-start.32) | collective-permute-done | bytes 129056 | tf_op jit(solution)/shard_map/ppermute | solution.py:65
  199.4 1.5 collective-permute-start.34
  205.6 1.1 convert_multiply_fusion
  (248 shorter events, 47.5 us)
Async XLA Ops:
  11.1 14.4 %collective-permute-start = (bf16[56,1024]{1,0:T(8,128)(2,1)S(1)}, bf16[56,1024]{1,0:T(8,128)(2,1)S(1)}, u32[]{:S(2)}, u32[]{:S(2)}) collective-permute-start(bf16[56,1024]{1,0:T(8,128)(2,1)S(1)} %pad_maximum_fusion.9), channel_id=1, source_target_pairs={{0,8},{2,10},{4,12},{6,14},{8,0},{10,2},{12,4},{14,6},{16,24},{18,... | collective-permute-start | bytes 344072 | tf_op jit(solution)/shard_map/ppermute | solution.py:65
  14.2 11.7 %collective-permute-start.1 = (bf16[56,1024]{1,0:T(8,128)(2,1)S(1)}, bf16[56,1024]{1,0:T(8,128)(2,1)S(1)}, u32[]{:S(2)}, u32[]{:S(2)}) collective-permute-start(bf16[56,1024]{1,0:T(8,128)(2,1)S(1)} %pad_maximum_fusion.9), channel_id=1, source_target_pairs={{0,16},{2,18},{4,20},{6,22},{8,24},{10,26},{12,28},{14,30},{16,0},... | collective-permute-start | bytes 344072 | tf_op jit(solution)/shard_map/ppermute | solution.py:65
  16.7 9.1 %collective-permute-start.2 = (bf16[56,1024]{1,0:T(8,128)(2,1)S(1)}, bf16[56,1024]{1,0:T(8,128)(2,1)}, u32[]{:S(2)}, u32[]{:S(2)}) collective-permute-start(bf16[56,1024]{1,0:T(8,128)(2,1)S(1)} %pad_maximum_fusion.9), channel_id=1, source_target_pairs={{0,24},{2,26},{4,28},{6,30},{8,16},{10,18},{12,20},{14,22},{16,8},... | collective-permute-start | bytes 344072 | tf_op jit(solution)/shard_map/ppermute | solution.py:65
  16.8 15.9 %all-to-all-start = ((bf16[4,56,1920]{2,1,0:T(8,128)(2,1)}), bf16[4,56,1920]{2,1,0:T(8,128)(2,1)S(1)}, u32[]{:S(2)}, u32[]{:S(2)}) async-start(bf16[4,56,1920]{2,1,0:T(8,128)(2,1)} %maximum_bitcast_fusion), calls=%async_computation | async-start | bytes 1720320 | tf_op jit(solution)/shard_map/all_to_all | solution.py:68
  20.3 85.1 %all-gather.3.cloned.1.call-start = ((), (), s32[]{:S(2)}) async-start(), calls=%async_computation.3 | async-start | bytes 4300800 | tf_op jit(solution)/shard_map/all_gather | solution.py:601
  27.1 22.1 %copy-start.26 = (bf16[2,2,56,1024]{3,2,1,0:T(8,128)(2,1)}, bf16[2,2,56,1024]{3,2,1,0:T(8,128)(2,1)S(1)}, u32[]{:S(2)}) copy-start(bf16[2,2,56,1024]{3,2,1,0:T(8,128)(2,1)S(1)} %reverse_select_fusion) | copy-start | bytes 1376260
  33.6 148.4 %reduce-scatter.2.cloned.1.call-start = ((), (), s32[]{:S(2)}) async-start(), calls=%async_computation.4 | async-start | bytes 4300800 | tf_op jit(solution)/shard_map/reduce_scatter | solution.py:654
  34.7 28.4 %collective-permute-start.8 = (bf16[4,56,448]{2,1,0:T(8,128)(2,1)}, bf16[4,56,448]{2,1,0:T(8,128)(2,1)}, u32[]{:S(2)}, u32[]{:S(2)}) collective-permute-start(bf16[4,56,448]{2,1,0:T(8,128)(2,1)} %slice.115), channel_id=1, source_target_pairs={{0,4},{2,6},{4,0},{6,2},{8,12},{10,14},{12,8},{14,10},{16,20},{18,... | collective-permute-start | bytes 602120 | tf_op jit(solution)/shard_map/ppermute | solution.py:65
  51.4 16.6 %copy-start.7 = (bf16[2,64,896]{2,1,0:T(8,128)(2,1)S(1)}, bf16[2,64,896]{2,1,0:T(8,128)(2,1)}, u32[]{:S(2)}) copy-start(bf16[2,64,896]{2,1,0:T(8,128)(2,1)} %cotangent_ref.1) | copy-start | bytes 688132
  51.4 6.9 %collective-permute-start.3 = (bf16[128,128]{1,0:T(8,128)(2,1)S(1)}, bf16[128,128]{1,0:T(8,128)(2,1)S(1)}, u32[]{:S(2)}, u32[]{:S(2)}) collective-permute-start(bf16[128,128]{1,0:T(8,128)(2,1)S(1)} %get-tuple-element.73), channel_id=1, source_target_pairs={{0,8},{2,10},{4,12},{6,14},{8,0},{10,2},{12,4},{14,6},{16,24},{18,... | collective-permute-start | bytes 98312 | tf_op jit(solution)/shard_map/ppermute | solution.py:65
  52.3 9.1 %collective-permute-start.4 = (bf16[128,128]{1,0:T(8,128)(2,1)S(1)}, bf16[128,128]{1,0:T(8,128)(2,1)S(1)}, u32[]{:S(2)}, u32[]{:S(2)}) collective-permute-start(bf16[128,128]{1,0:T(8,128)(2,1)S(1)} %get-tuple-element.73), channel_id=1, source_target_pairs={{0,16},{2,18},{4,20},{6,22},{8,24},{10,26},{12,28},{14,30},{16,0},... | collective-permute-start | bytes 98312 | tf_op jit(solution)/shard_map/ppermute | solution.py:65
  55.8 6.4 %collective-permute-start.5 = (bf16[128,128]{1,0:T(8,128)(2,1)S(1)}, bf16[128,128]{1,0:T(8,128)(2,1)S(1)}, u32[]{:S(2)}, u32[]{:S(2)}) collective-permute-start(bf16[128,128]{1,0:T(8,128)(2,1)S(1)} %get-tuple-element.73), channel_id=1, source_target_pairs={{0,24},{2,26},{4,28},{6,30},{8,16},{10,18},{12,20},{14,22},{16,8},... | collective-permute-start | bytes 98312 | tf_op jit(solution)/shard_map/ppermute | solution.py:65
  62.2 5.0 %collective-permute-start.6 = (bf16[4,128,128]{2,1,0:T(8,128)(2,1)S(1)}, bf16[4,128,128]{2,1,0:T(8,128)(2,1)S(1)}, u32[]{:S(2)}, u32[]{:S(2)}) collective-permute-start(bf16[4,128,128]{2,1,0:T(8,128)(2,1)S(1)} %get-tuple-element.142), channel_id=1, source_target_pairs={{0,4},{2,6},{4,0},{6,2},{8,12},{10,14},{12,8},{14,10},{16,20},{18,... | collective-permute-start | bytes 393224 | tf_op jit(solution)/shard_map/ppermute | solution.py:65
  65.1 6.2 %collective-permute-start.9 = (bf16[4,2,56,448]{3,2,0,1:T(8,128)(2,1)}, bf16[4,2,56,448]{3,2,0,1:T(8,128)(2,1)}, u32[]{:S(2)}, u32[]{:S(2)}) collective-permute-start(bf16[4,2,56,448]{3,2,0,1:T(8,128)(2,1)} %pad_maximum_fusion.4), channel_id=1, source_target_pairs={{0,2},{2,0},{4,6},{6,4},{8,10},{10,8},{12,14},{14,12},{16,18},{18,... | collective-permute-start | bytes 1204232 | tf_op jit(solution)/shard_map/ppermute | solution.py:65
  68.0 1.5 collective-permute-start.7
  68.0 10.5 %collective-permute-start.11 = (bf16[128,896]{1,0:T(8,128)(2,1)S(1)}, bf16[128,896]{1,0:T(8,128)(2,1)}, u32[]{:S(2)}, u32[]{:S(2)}) collective-permute-start(bf16[128,896]{1,0:T(8,128)(2,1)S(1)} %bitcast.158), channel_id=1, source_target_pairs={{0,4},{2,6},{4,0},{6,2},{8,12},{10,14},{12,8},{14,10},{16,20},{18,... | collective-permute-start | bytes 688136 | tf_op jit(solution)/shard_map/ppermute | solution.py:65
  76.9 15.7 %copy-start.21 = (bf16[2,64,448]{2,1,0:T(8,128)(2,1)}, bf16[2,64,448]{2,1,0:T(8,128)(2,1)S(1)}, u32[]{:S(2)}) copy-start(bf16[2,64,448]{2,1,0:T(8,128)(2,1)S(1)} %get-tuple-element.98) | copy-start | bytes 344068
  76.9 7.7 %collective-permute-start.10 = (bf16[128,896]{1,0:T(8,128)(2,1)S(1)}, bf16[128,896]{1,0:T(8,128)(2,1)S(1)}, u32[]{:S(2)}, u32[]{:S(2)}) collective-permute-start(bf16[128,896]{1,0:T(8,128)(2,1)S(1)} %bitcast.166), channel_id=1, source_target_pairs={{0,1},{1,0},{2,3},{3,2},{4,5},{5,4},{6,7},{7,6},{8,9},{9,8},{10,11... | collective-permute-start | bytes 688136 | tf_op jit(solution)/shard_map/ppermute | solution.py:47
  79.5 5.3 %collective-permute-start.12 = (bf16[256,896]{1,0:T(8,128)(2,1)S(1)}, bf16[256,896]{1,0:T(8,128)(2,1)S(1)}, u32[]{:S(2)}, u32[]{:S(2)}) collective-permute-start(bf16[256,896]{1,0:T(8,128)(2,1)S(1)} %pad_maximum_fusion.5), channel_id=1, source_target_pairs={{0,2},{2,0},{4,6},{6,4},{8,10},{10,8},{12,14},{14,12},{16,18},{18,... | collective-permute-start | bytes 1376264 | tf_op jit(solution)/shard_map/ppermute | solution.py:65
  85.7 6.9 %collective-permute-start.13 = (bf16[128,896]{1,0:T(8,128)(2,1)S(1)}, bf16[128,896]{1,0:T(8,128)(2,1)S(1)}, u32[]{:S(2)}, u32[]{:S(2)}) collective-permute-start(bf16[128,896]{1,0:T(8,128)(2,1)S(1)} %get-tuple-element.121), channel_id=1, source_target_pairs={{0,4},{2,6},{4,0},{6,2},{8,12},{10,14},{12,8},{14,10},{16,20},{18,... | collective-permute-start | bytes 688136 | tf_op jit(solution)/shard_map/ppermute | solution.py:65
  92.7 1.9 collective-permute-start.14
  116.5 20.4 %copy-start.1 = (bf16[4,2,2,56,448]{4,3,2,1,0:T(8,128)(2,1)S(1)}, bf16[4,2,2,56,448]{4,3,2,1,0:T(8,128)(2,1)}, u32[]{:S(2)}) copy-start(bf16[4,2,2,56,448]{4,3,2,1,0:T(8,128)(2,1)} %copy-done) | copy-start | bytes 2408452
  116.5 20.4 %copy-start.8 = (bf16[2,64,896]{2,1,0:T(8,128)(2,1)S(1)}, bf16[2,64,896]{2,1,0:T(8,128)(2,1)}, u32[]{:S(2)}) copy-start(bf16[2,64,896]{2,1,0:T(8,128)(2,1)} %cotangent_ref.1) | copy-start | bytes 688132
  116.5 20.4 %copy-start.16 = (bf16[128,448]{1,0:T(8,128)(2,1)S(1)}, bf16[128,448]{1,0:T(8,128)(2,1)}, u32[]{:S(2)}) copy-start(bf16[128,448]{1,0:T(8,128)(2,1)} %copy-done.14) | copy-start | bytes 344068
  116.5 2.1 collective-permute-start.15
  119.6 7.7 %collective-permute-start.16 = (bf16[128,896]{1,0:T(8,128)(2,1)S(1)}, bf16[128,896]{1,0:T(8,128)(2,1)S(1)}, u32[]{:S(2)}, u32[]{:S(2)}) collective-permute-start(bf16[128,896]{1,0:T(8,128)(2,1)S(1)} %add_convert_fusion.6), channel_id=1, source_target_pairs={{0,4},{2,6},{4,0},{6,2},{8,12},{10,14},{12,8},{14,10},{16,20},{18,... | collective-permute-start | bytes 688136 | tf_op jit(solution)/shard_map/ppermute | solution.py:65
  121.1 7.2 %collective-permute-start.17 = (bf16[256,896]{1,0:T(8,128)(2,1)}, bf16[256,896]{1,0:T(8,128)(2,1)S(1)}, u32[]{:S(2)}, u32[]{:S(2)}) collective-permute-start(bf16[256,896]{1,0:T(8,128)(2,1)} %get-tuple-element.87), channel_id=1, source_target_pairs={{0,2},{2,0},{4,6},{6,4},{8,10},{10,8},{12,14},{14,12},{16,18},{18,... | collective-permute-start | bytes 1376264 | tf_op jit(solution)/shard_map/ppermute | solution.py:65
  128.4 7.0 %collective-permute-start.18 = (bf16[128,896]{1,0:T(8,128)(2,1)S(1)}, bf16[128,896]{1,0:T(8,128)(2,1)S(1)}, u32[]{:S(2)}, u32[]{:S(2)}) collective-permute-start(bf16[128,896]{1,0:T(8,128)(2,1)S(1)} %add_convert_fusion.5.own_ref), channel_id=1, source_target_pairs={{0,1},{1,0},{2,3},{3,2},{4,5},{5,4},{6,7},{7,6},{8,9},{9,8},{10,11... | collective-permute-start | bytes 688136 | tf_op jit(solution)/shard_map/ppermute | solution.py:662
  135.4 6.2 %collective-permute-start.19 = (bf16[128,896]{1,0:T(8,128)(2,1)S(1)}, bf16[128,896]{1,0:T(8,128)(2,1)S(1)}, u32[]{:S(2)}, u32[]{:S(2)}) collective-permute-start(bf16[128,896]{1,0:T(8,128)(2,1)S(1)} %slice.121), channel_id=1, source_target_pairs={{0,4},{2,6},{4,0},{6,2},{8,12},{10,14},{12,8},{14,10},{16,20},{18,... | collective-permute-start | bytes 688136 | tf_op jit(solution)/shard_map/ppermute | solution.py:65
  142.3 1.6 collective-permute-start.20
  145.6 7.1 %collective-permute-start.22 = (bf16[8,56,896]{2,1,0:T(8,128)(2,1)S(1)}, bf16[8,56,896]{2,1,0:T(8,128)(2,1)}, u32[]{:S(2)}, u32[]{:S(2)}) collective-permute-start(bf16[8,56,896]{2,1,0:T(8,128)(2,1)S(1)} %get-tuple-element.101), channel_id=1, source_target_pairs={{0,2},{2,0},{4,6},{6,4},{8,10},{10,8},{12,14},{14,12},{16,18},{18,... | collective-permute-start | bytes 2408456 | tf_op jit(solution)/shard_map/ppermute | solution.py:65
  145.9 5.9 %collective-permute-start.21 = (bf16[512,128]{1,0:T(8,128)(2,1)S(1)}, bf16[512,128]{1,0:T(8,128)(2,1)}, u32[]{:S(2)}, u32[]{:S(2)}) collective-permute-start(bf16[512,128]{1,0:T(8,128)(2,1)S(1)} %slice.153), channel_id=1, source_target_pairs={{0,4},{2,6},{4,0},{6,2},{8,12},{10,14},{12,8},{14,10},{16,20},{18,... | collective-permute-start | bytes 393224 | tf_op jit(solution)/shard_map/ppermute | solution.py:65
  156.1 11.1 %collective-permute-start.26 = (bf16[4,56,896]{2,1,0:T(8,128)(2,1)}, bf16[4,56,896]{2,1,0:T(8,128)(2,1)}, u32[]{:S(2)}, u32[]{:S(2)}) collective-permute-start(bf16[4,56,896]{2,1,0:T(8,128)(2,1)} %dynamic-slice_bitcast_fusion), channel_id=1, source_target_pairs={{0,4},{2,6},{4,0},{6,2},{8,12},{10,14},{12,8},{14,10},{16,20},{18,... | collective-permute-start | bytes 1204232 | tf_op jit(solution)/shard_map/ppermute | solution.py:65
  157.6 6.1 %collective-permute-start.23 = (bf16[128,128]{1,0:T(8,128)(2,1)S(1)}, bf16[128,128]{1,0:T(8,128)(2,1)S(1)}, u32[]{:S(2)}, u32[]{:S(2)}) collective-permute-start(bf16[128,128]{1,0:T(8,128)(2,1)S(1)} %get-tuple-element.138), channel_id=1, source_target_pairs={{0,8},{2,10},{4,12},{6,14},{8,0},{10,2},{12,4},{14,6},{16,24},{18,... | collective-permute-start | bytes 98312 | tf_op jit(solution)/shard_map/ppermute | solution.py:65
  157.7 9.5 %collective-permute-start.24 = (bf16[128,128]{1,0:T(8,128)(2,1)S(1)}, bf16[128,128]{1,0:T(8,128)(2,1)S(1)}, u32[]{:S(2)}, u32[]{:S(2)}) collective-permute-start(bf16[128,128]{1,0:T(8,128)(2,1)S(1)} %get-tuple-element.140), channel_id=1, source_target_pairs={{0,16},{2,18},{4,20},{6,22},{8,24},{10,26},{12,28},{14,30},{16,0},... | collective-permute-start | bytes 98312 | tf_op jit(solution)/shard_map/ppermute | solution.py:65
  159.2 8.0 %collective-permute-start.25 = (bf16[128,128]{1,0:T(8,128)(2,1)S(1)}, bf16[128,128]{1,0:T(8,128)(2,1)S(1)}, u32[]{:S(2)}, u32[]{:S(2)}) collective-permute-start(bf16[128,128]{1,0:T(8,128)(2,1)S(1)} %get-tuple-element.139), channel_id=1, source_target_pairs={{0,24},{2,26},{4,28},{6,30},{8,16},{10,18},{12,20},{14,22},{16,8},... | collective-permute-start | bytes 98312 | tf_op jit(solution)/shard_map/ppermute | solution.py:65
  162.2 7.6 %collective-permute-start.29 = (bf16[128,896]{1,0:T(8,128)(2,1)}, bf16[128,896]{1,0:T(8,128)(2,1)S(1)}, u32[]{:S(2)}, u32[]{:S(2)}) collective-permute-start(bf16[128,896]{1,0:T(8,128)(2,1)} %add_convert_fusion.4), channel_id=1, source_target_pairs={{0,1},{1,0},{2,3},{3,2},{4,5},{5,4},{6,7},{7,6},{8,9},{9,8},{10,11... | collective-permute-start | bytes 688136 | tf_op jit(solution)/shard_map/ppermute | solution.py:706
  169.7 1.9 collective-permute-start.27
  171.7 5.6 %collective-permute-start.28 = (bf16[4,56,256]{2,1,0:T(8,128)(2,1)S(1)}, bf16[4,56,256]{2,1,0:T(8,128)(2,1)S(1)}, u32[]{:S(2)}, u32[]{:S(2)}) collective-permute-start(bf16[4,56,256]{2,1,0:T(8,128)(2,1)S(1)} %dynamic-slice_bitcast_fusion.4), channel_id=1, source_target_pairs={{0,4},{2,6},{4,0},{6,2},{8,12},{10,14},{12,8},{14,10},{16,20},{18,... | collective-permute-start | bytes 344072 | tf_op jit(solution)/shard_map/ppermute | solution.py:65
  182.1 17.3 %copy-start.43 = (bf16[56]{0:T(256)(128)(2,1)S(1)}, bf16[56]{0:T(256)(128)(2,1)}, u32[]{:S(2)}) copy-start(bf16[56]{0:T(256)(128)(2,1)} %param.19) | copy-start | bytes 340
  182.1 18.9 %copy-start.44 = (bf16[56]{0:T(256)(128)(2,1)S(1)}, bf16[56]{0:T(256)(128)(2,1)}, u32[]{:S(2)}) copy-start(bf16[56]{0:T(256)(128)(2,1)} %param.20) | copy-start | bytes 340
  182.1 9.7 %collective-permute-start.31 = (bf16[56,1152]{1,0:T(8,128)(2,1)S(1)}, bf16[56,1152]{1,0:T(8,128)(2,1)S(1)}, u32[]{:S(2)}, u32[]{:S(2)}) collective-permute-start(bf16[56,1152]{1,0:T(8,128)(2,1)S(1)} %get-tuple-element.131), channel_id=1, source_target_pairs={{0,8},{2,10},{4,12},{6,14},{8,0},{10,2},{12,4},{14,6},{16,24},{18,... | collective-permute-start | bytes 387080 | tf_op jit(solution)/shard_map/ppermute | solution.py:65
  184.1 12.7 %collective-permute-start.32 = (bf16[56,1152]{1,0:T(8,128)(2,1)S(1)}, bf16[56,1152]{1,0:T(8,128)(2,1)S(1)}, u32[]{:S(2)}, u32[]{:S(2)}) collective-permute-start(bf16[56,1152]{1,0:T(8,128)(2,1)S(1)} %get-tuple-element.133), channel_id=1, source_target_pairs={{0,16},{2,18},{4,20},{6,22},{8,24},{10,26},{12,28},{14,30},{16,0},... | collective-permute-start | bytes 387080 | tf_op jit(solution)/shard_map/ppermute | solution.py:65
  185.1 11.7 %collective-permute-start.33 = (bf16[56,1152]{1,0:T(8,128)(2,1)S(1)}, bf16[56,1152]{1,0:T(8,128)(2,1)S(1)}, u32[]{:S(2)}, u32[]{:S(2)}) collective-permute-start(bf16[56,1152]{1,0:T(8,128)(2,1)S(1)} %get-tuple-element.132), channel_id=1, source_target_pairs={{0,24},{2,26},{4,28},{6,30},{8,16},{10,18},{12,20},{14,22},{16,8},... | collective-permute-start | bytes 387080 | tf_op jit(solution)/shard_map/ppermute | solution.py:65
  186.6 17.1 %copy-start.20 = (f32[2,64,896]{2,1,0:T(8,128)S(1)}, f32[2,64,896]{2,1,0:T(8,128)}, u32[]{:S(2)}) copy-start(f32[2,64,896]{2,1,0:T(8,128)} %copy-done.19) | copy-start | bytes 1376260
  186.7 18.0 %all-to-all-start.1 = ((bf16[4,56,1920]{2,1,0:T(8,128)(2,1)}), bf16[4,56,1920]{2,1,0:T(8,128)(2,1)S(1)}, u32[]{:S(2)}, u32[]{:S(2)}) async-start(bf16[4,56,1920]{2,1,0:T(8,128)(2,1)} %bitcast.186), calls=%async_computation.2 | async-start | bytes 1720320 | tf_op jit(solution)/shard_map/all_to_all | solution.py:68
  190.3 13.2 %collective-permute-start.30 = (bf16[128,896]{1,0:T(8,128)(2,1)S(1)}, bf16[128,896]{1,0:T(8,128)(2,1)S(1)}, u32[]{:S(2)}, u32[]{:S(2)}) collective-permute-start(bf16[128,896]{1,0:T(8,128)(2,1)S(1)} %get-tuple-element.115), channel_id=1, source_target_pairs={{0,1},{1,0},{2,3},{3,2},{4,5},{5,4},{6,7},{7,6},{8,9},{9,8},{10,11... | collective-permute-start | bytes 688136 | tf_op jit(solution)/shard_map/ppermute | solution.py:47
  199.4 3.6 %collective-permute-start.34 = (f32[56]{0:T(128)S(1)}, f32[56]{0:T(128)S(1)}, u32[]{:S(2)}, u32[]{:S(2)}) collective-permute-start(f32[56]{0:T(128)S(1)} %convert_divide_fusion), channel_id=1, source_target_pairs={{0,1},{1,0},{2,3},{3,2},{4,5},{5,4},{6,7},{7,6},{8,9},{9,8},{10,11... | collective-permute-start | bytes 680 | tf_op jit(solution)/shard_map/ppermute | solution.py:785
  (37 other events, 203.3 us)
Sparse Core Ops, SparseCore 0:
  33.7 71.5 all-gather.2
  116.6 65.3 reduce-scatter.1

commit v5 on v4

--- a/solution.py
+++ b/solution.py
@@ -758,8 +758,13 @@
         place=device,
     )
     narrow_kept, narrow_beside = near_half(narrow_kept, groups.flip(narrow_sent, 1))
+    narrow = add(narrow_kept, narrow_beside)
+    extra = narrow[:, :, 2 * HEAD :]
+    other = lax.ppermute(extra, "tp", [(0, 1), (1, 0)])
+    first = lax.broadcasted_iota(jnp.int32, extra.shape, 2) == 0
+    extra = jnp.where(first, add(extra, other), extra)
     narrow = jnp.concatenate(
-        [add(wide_kept, wide_beside), add(narrow_kept, narrow_beside)], axis=2
+        [add(wide_kept, wide_beside), narrow[:, :, : 2 * HEAD], extra], axis=2
     )
     narrow, d_w_ffn, d_weighted_low, mixed = together(narrow, d_w_ffn, d_weighted_low, mixed)
     d_weighted = sum_tp(d_weighted_low)
@@ -782,7 +787,6 @@
     g_pair = narrow[:, : 2 * HEAD] * own_gain_one
     g_two = narrow[:, 2 * HEAD + 1] / own_gain_two[:, 0]
     g_one = narrow[:, 2 * HEAD] / own_gain_one[:, 0]
-    g_one = g_one + lax.ppermute(g_one, "tp", [(0, 1), (1, 0)])
     return (
         mixed.reshape(tokens.shape),
         tokens_grad.reshape(tokens.shape),

time: 214 us -> 213 us (level)
    ppermute x1, waiting for transfers between devices: 0.01 us -> 4.89 us  [local(): mixed_other = lax.ppermute(mixed_own, 'tp', [(0, 1), (1, 0)])]
    reduce_scatter x1, waiting for transfers between devices: 4.73 us -> 0.02 us  [local(): lax.psum_scatter(d_w_ffn, 'ctx', scatter_dimension=0, tiled=True, axis_in...]
    all_to_all x2, waiting for transfers between devices: 5.6 us -> 7.9 us  [swap_near(): lax.all_to_all(values, 'ctx', 0, 0, tiled=True, axis_index_groups=self.near)]
    unnamed x96 -> x98, local copies, waits for them, and re-layouts: 9.88 us -> 9.91 us
  transfers between devices with their start and end apart: 39 -> 39, of which waited for: 22 -> 22; matrix products, arithmetic and copies ran while one was open for 16% -> 15% of each run, Pallas kernels for 5% -> 5%
where the time goes in v5:
time: 213 us
  waiting for transfers between devices  73.1 us (34%)
  starting transfers between devices  44.4 us (21%)
  other arithmetic  27 us (13%)
  Pallas kernels  22 us (10%)
  local copies, waits for them, and re-layouts  17.3 us (8%)
  between operations  15.1 us (7%)
  blocking collectives  13.8 us (6%)
    ppermute x30, waiting for transfers between devices, flip(): lax.ppermute(values, 'ctx', [(i, i ^ bit) for i in range(self.count)])  41.1 us
    ppermute x30, starting transfers between devices, flip(): lax.ppermute(values, 'ctx', [(i, i ^ bit) for i in range(self.count)])  29.4 us
    all_gather x1, blocking collectives, spread_near(): whole = lax.all_gather(values, 'ctx', axis=0, axis_index_groups=self.near)  13.8 us
    pallas_call x1, Pallas kernels, ffn_call(): pl.pallas_call(functools.partial(ffn_kernel, part), in_specs=[far, far],...  11 us
    pallas_call x5, Pallas kernels, whole_call(): pl.pallas_call(kernel, in_specs=in_specs, out_specs=[whole] * len(out_sha...  11 us
    unnamed x98, local copies, waits for them, and re-layouts  9.91 us
    all_gather x1, waiting for transfers between devices, local(): lax.all_gather(w_ffn, 'ctx', axis=0, tiled=True, axis_index_groups=groups...  8.13 us
    all_to_all x2, waiting for transfers between devices, swap_near(): lax.all_to_all(values, 'ctx', 0, 0, tiled=True, axis_index_groups=self.near)  7.9 us
  transfers between devices with their start and end apart: 39, of which 22 were waited for; matrix products, arithmetic and copies ran while one was open for 15% of the time, Pallas kernels for 5%

profile of v5, /device:TPU:0, one launch (start us, length us, event | category | flops | bytes accessed | tf_op | source)
XLA Modules:
  0.0 212.7 jit_solution(10560361473780100797)
XLA Ops:
  7.9 1.2 multiply_convert_fusion.1
  11.1 3.0 %collective-permute-start = (bf16[56,1024]{1,0:T(8,128)(2,1)S(1)}, bf16[56,1024]{1,0:T(8,128)(2,1)S(1)}, u32[]{:S(2)}, u32[]{:S(2)}) collective-permute-start(bf16[56,1024]{1,0:T(8,128)(2,1)S(1)} %pad_maximum_fusion.9), channel_id=1, source_target_pairs={{0,8},{2,10},{4,12},{6,14},{8,0},{10,2},{12,4},{14,6},{16,24},{18,... | collective-permute-start | bytes 344072 | tf_op jit(solution)/shard_map/ppermute | solution.py:65
  14.2 2.6 %collective-permute-start.1 = (bf16[56,1024]{1,0:T(8,128)(2,1)S(1)}, bf16[56,1024]{1,0:T(8,128)(2,1)S(1)}, u32[]{:S(2)}, u32[]{:S(2)}) collective-permute-start(bf16[56,1024]{1,0:T(8,128)(2,1)S(1)} %pad_maximum_fusion.9), channel_id=1, source_target_pairs={{0,16},{2,18},{4,20},{6,22},{8,24},{10,26},{12,28},{14,30},{16,0},... | collective-permute-start | bytes 344072 | tf_op jit(solution)/shard_map/ppermute | solution.py:65
  16.7 3.5 %all-to-all-start = ((bf16[4,56,1920]{2,1,0:T(8,128)(2,1)}), bf16[4,56,1920]{2,1,0:T(8,128)(2,1)S(1)}, u32[]{:S(2)}, u32[]{:S(2)}) async-start(bf16[4,56,1920]{2,1,0:T(8,128)(2,1)} %maximum_bitcast_fusion), calls=%async_computation | async-start | bytes 1720320 | tf_op jit(solution)/shard_map/all_to_all | solution.py:68
  24.1 1.3 compare_convert_fusion.same_ref
  26.1 6.5 %all-to-all-done = bf16[4,56,1920]{2,1,0:T(8,128)(2,1)S(1)} async-done(((bf16[4,56,1920]{2,1,0:T(8,128)(2,1)}), bf16[4,56,1920]{2,1,0:T(8,128)(2,1)S(1)}, u32[]{:S(2)}, u32[]{:S(2)}) %all-to-all-start) | async-done | bytes 860192 | tf_op jit(solution)/shard_map/all_to_all | solution.py:68
  34.4 13.8 %all-gather = bf16[16,56,576]{2,1,0:T(8,128)(2,1)S(1)} all-gather(bf16[4,56,576]{2,1,0:T(8,128)(2,1)S(1)} %slice.120), channel_id=2, replica_groups={{0,2,4,6},{8,10,12,14},{16,18,20,22},{24,26,28,30},{1,3,5,7},{9,11,13,1..., dimensions={0}, use_global_device_ids=true | all-gather | bytes 1290240 | tf_op jit(solution)/shard_map/all_gather | solution.py:87
  51.4 3.5 %collective-permute-start.4 = (bf16[128,128]{1,0:T(8,128)(2,1)S(1)}, bf16[128,128]{1,0:T(8,128)(2,1)}, u32[]{:S(2)}, u32[]{:S(2)}) collective-permute-start(bf16[128,128]{1,0:T(8,128)(2,1)S(1)} %get-tuple-element.73), channel_id=1, source_target_pairs={{0,16},{2,18},{4,20},{6,22},{8,24},{10,26},{12,28},{14,30},{16,0},... | collective-permute-start | bytes 98312 | tf_op jit(solution)/shard_map/ppermute | solution.py:65
  54.9 3.2 %collective-permute-done.3 = bf16[128,128]{1,0:T(8,128)(2,1)S(1)} collective-permute-done((bf16[128,128]{1,0:T(8,128)(2,1)S(1)}, bf16[128,128]{1,0:T(8,128)(2,1)S(1)}, u32[]{:S(2)}, u32[]{:S(2)}) %collective-permute-start.3) | collective-permute-done | bytes 32800 | tf_op jit(solution)/shard_map/ppermute | solution.py:65
  58.2 3.4 %collective-permute-done.4 = bf16[128,128]{1,0:T(8,128)(2,1)} collective-permute-done((bf16[128,128]{1,0:T(8,128)(2,1)S(1)}, bf16[128,128]{1,0:T(8,128)(2,1)}, u32[]{:S(2)}, u32[]{:S(2)}) %collective-permute-start.4) | collective-permute-done | bytes 32800 | tf_op jit(solution)/shard_map/ppermute | solution.py:65
  65.0 2.5 %collective-permute-done.6 = bf16[4,128,128]{2,1,0:T(8,128)(2,1)S(1)} collective-permute-done((bf16[4,128,128]{2,1,0:T(8,128)(2,1)S(1)}, bf16[4,128,128]{2,1,0:T(8,128)(2,1)S(1)}, u32[]{:S(2)}, u32[]{:S(2)}) %collective-permute-start.6) | collective-permute-done | bytes 131104 | tf_op jit(solution)/shard_map/ppermute | solution.py:65
  71.5 1.3 select_bitcast_fusion.1
  73.7 3.4 %forward.1 = (bf16[2,64,448]{2,1,0:T(8,128)(2,1)S(1)}, bf16[2,64,896]{2,1,0:T(8,128)(2,1)S(1)}, f32[1,8,128]{2,1,0:T(8,128)S(1)}, f32[2,1,448]{2,1,0:T(1,128)S(1)}) custom-call(bf16[2,64,448]{2,1,0:T(8,128)(2,1)S(1)} %bitcast.161, bf16[16,2,64,128]{3,2,1,0:T(8,128)(2,1)S(1)} %bitcast.153, s32[2,1024,1]{2,1,0:T(8,128)S(1)} %broadcast_add_fusion.key_pos_ref, ...), custom_call_target="tpu_custom_call" | custom-call | flops 1 | bytes 1 | tf_op jit(solution)/shard_map/forward/pallas_call | solution.py:183
  77.1 1.6 collective-permute-start.10
  79.8 5.1 %collective-permute-done.10 = bf16[128,896]{1,0:T(8,128)(2,1)S(1)} collective-permute-done((bf16[128,896]{1,0:T(8,128)(2,1)S(1)}, bf16[128,896]{1,0:T(8,128)(2,1)S(1)}, u32[]{:S(2)}, u32[]{:S(2)}) %collective-permute-start.10) | collective-permute-done | bytes 229408 | tf_op jit(solution)/shard_map/ppermute | solution.py:47
  86.6 6.2 %collective-permute-done.13 = bf16[128,896]{1,0:T(8,128)(2,1)S(1)} collective-permute-done((bf16[128,896]{1,0:T(8,128)(2,1)S(1)}, bf16[128,896]{1,0:T(8,128)(2,1)S(1)}, u32[]{:S(2)}, u32[]{:S(2)}) %collective-permute-start.13) | collective-permute-done | bytes 229408 | tf_op jit(solution)/shard_map/ppermute | solution.py:65
  97.2 8.1 %all-gather.3.cloned.1.call-done.w_source = bf16[896,1920]{1,0:T(8,128)(2,1)} async-done(((bf16[224,1920]{1,0:T(8,128)(2,1)}), bf16[896,1920]{1,0:T(8,128)(2,1)}) %all-gather.3.cloned.1.call-update) | async-done | bytes 3440656 | tf_op jit(solution)/shard_map/all_gather | solution.py:601
  105.3 11.0 %ffn.1 = (bf16[256,896]{1,0:T(8,128)(2,1)}, bf16[256,896]{1,0:T(8,128)(2,1)}, bf16[256,896]{1,0:T(8,128)(2,1)}, bf16[256,896]{1,0:T(8,128)(2,1)}, bf16[896,1920]{1,0:T(8,128)(2,1)}) custom-call(bf16[1024,896]{1,0:T(8,128)(2,1)} %constant_dynamic-update-slice_fusion.token_source, bf16[896,1920]{1,0:T(8,128)(2,1)} %all-gather.3.cloned.1.call-done.w_source), custom_call_target="tpu_custom_call" | custom-call | flops 1 | bytes 1 | tf_op jit(solution)/shard_map/ffn/pallas_call | solution.py:446
  116.5 2.0 collective-permute-done.15
  119.5 1.6 collective-permute-start.16
  121.1 6.1 %collective-permute-done.16 = bf16[128,896]{1,0:T(8,128)(2,1)S(1)} collective-permute-done((bf16[128,896]{1,0:T(8,128)(2,1)S(1)}, bf16[128,896]{1,0:T(8,128)(2,1)S(1)}, u32[]{:S(2)}, u32[]{:S(2)}) %collective-permute-start.16) | collective-permute-done | bytes 229408 | tf_op jit(solution)/shard_map/ppermute | solution.py:65
  128.3 1.6 collective-permute-start.18
  129.8 1.1 add_convert_fusion.1
  131.0 4.3 %collective-permute-done.18.other_ref = bf16[128,896]{1,0:T(8,128)(2,1)S(1)} collective-permute-done((bf16[128,896]{1,0:T(8,128)(2,1)S(1)}, bf16[128,896]{1,0:T(8,128)(2,1)S(1)}, u32[]{:S(2)}, u32[]{:S(2)}) %collective-permute-start.18) | collective-permute-done | bytes 229408 | tf_op jit(solution)/shard_map/ppermute | solution.py:662
  135.3 1.6 collective-permute-start.19
  136.9 4.2 %backward.1 = (f32[2,64,896]{2,1,0:T(8,128)S(1)}, bf16[2,64,896]{2,1,0:T(8,128)(2,1)S(1)}, bf16[2,64,448]{2,1,0:T(8,128)(2,1)S(1)}, bf16[16,2,64,128]{3,2,1,0:T(8,128)(2,1)S(1)}) custom-call(bf16[2,64,448]{2,1,0:T(8,128)(2,1)S(1)} %bitcast.162, bf16[16,2,64,128]{3,2,1,0:T(8,128)(2,1)S(1)} %bitcast.154, s32[2,1024,1]{2,1,0:T(8,128)S(1)} %broadcast_add_fusion.key_pos_ref, ...), custom_call_target="tpu_custom_call" | custom-call | flops 1 | bytes 1 | tf_op jit(solution)/shard_map/backward/pallas_call | solution.py:183
  142.3 1.5 collective-permute-done.20
  143.8 1.7 wide.1
  146.7 1.6 collective-permute-start.21
  148.2 4.2 %collective-permute-done.21 = bf16[512,128]{1,0:T(8,128)(2,1)S(1)} collective-permute-done((bf16[512,128]{1,0:T(8,128)(2,1)S(1)}, bf16[512,128]{1,0:T(8,128)(2,1)S(1)}, u32[]{:S(2)}, u32[]{:S(2)}) %collective-permute-start.21) | collective-permute-done | bytes 131104 | tf_op jit(solution)/shard_map/ppermute | solution.py:65
  152.6 1.6 add_convert_fusion
  155.9 1.5 collective-permute-start.26
  157.5 1.5 collective-permute-start.24
  159.0 2.9 %collective-permute-start.25 = (bf16[128,128]{1,0:T(8,128)(2,1)S(1)}, bf16[128,128]{1,0:T(8,128)(2,1)S(1)}, u32[]{:S(2)}, u32[]{:S(2)}) collective-permute-start(bf16[128,128]{1,0:T(8,128)(2,1)S(1)} %get-tuple-element.139), channel_id=1, source_target_pairs={{0,24},{2,26},{4,28},{6,30},{8,16},{10,18},{12,20},{14,22},{16,8},... | collective-permute-start | bytes 98312 | tf_op jit(solution)/shard_map/ppermute | solution.py:65
  162.4 4.7 %collective-permute-done.24 = bf16[128,128]{1,0:T(8,128)(2,1)S(1)} collective-permute-done((bf16[128,128]{1,0:T(8,128)(2,1)S(1)}, bf16[128,128]{1,0:T(8,128)(2,1)S(1)}, u32[]{:S(2)}, u32[]{:S(2)}) %collective-permute-start.24) | collective-permute-done | bytes 32800 | tf_op jit(solution)/shard_map/ppermute | solution.py:65
  167.2 1.3 copy-done.3
  169.8 1.5 collective-permute-start.30
  171.4 1.5 collective-permute-start.28
  173.0 4.9 %collective-permute-done.30 = bf16[128,896]{1,0:T(8,128)(2,1)S(1)} collective-permute-done((bf16[128,896]{1,0:T(8,128)(2,1)S(1)}, bf16[128,896]{1,0:T(8,128)(2,1)S(1)}, u32[]{:S(2)}, u32[]{:S(2)}) %collective-permute-start.30) | collective-permute-done | bytes 229408 | tf_op jit(solution)/shard_map/ppermute | solution.py:706
  178.7 1.5 collective-permute-start.29
  181.3 1.6 collective-permute-done.29
  183.1 1.6 collective-permute-start.32
  185.2 2.4 %collective-permute-start.34 = (bf16[56,1152]{1,0:T(8,128)(2,1)S(1)}, bf16[56,1152]{1,0:T(8,128)(2,1)S(1)}, u32[]{:S(2)}, u32[]{:S(2)}) collective-permute-start(bf16[56,1152]{1,0:T(8,128)(2,1)S(1)} %get-tuple-element.132), channel_id=1, source_target_pairs={{0,24},{2,26},{4,28},{6,30},{8,16},{10,18},{12,20},{14,22},{16,8},... | collective-permute-start | bytes 387080 | tf_op jit(solution)/shard_map/ppermute | solution.py:65
  187.7 3.6 %all-to-all-start.1 = ((bf16[4,56,1920]{2,1,0:T(8,128)(2,1)}), bf16[4,56,1920]{2,1,0:T(8,128)(2,1)S(1)}, u32[]{:S(2)}, u32[]{:S(2)}) async-start(bf16[4,56,1920]{2,1,0:T(8,128)(2,1)} %bitcast.186), calls=%async_computation.2 | async-start | bytes 1720320 | tf_op jit(solution)/shard_map/all_to_all | solution.py:68
  191.3 1.5 collective-permute-start.31
  192.9 4.0 %collective-permute-done.33 = bf16[56,1152]{1,0:T(8,128)(2,1)S(1)} collective-permute-done((bf16[56,1152]{1,0:T(8,128)(2,1)S(1)}, bf16[56,1152]{1,0:T(8,128)(2,1)S(1)}, u32[]{:S(2)}, u32[]{:S(2)}) %collective-permute-start.33) | collective-permute-done | bytes 129056 | tf_op jit(solution)/shard_map/ppermute | solution.py:65
  202.3 1.4 all-to-all-done.1
  204.8 1.1 convert_multiply_fusion
  (252 shorter events, 44.5 us)
Async XLA Ops:
  11.1 14.4 %collective-permute-start = (bf16[56,1024]{1,0:T(8,128)(2,1)S(1)}, bf16[56,1024]{1,0:T(8,128)(2,1)S(1)}, u32[]{:S(2)}, u32[]{:S(2)}) collective-permute-start(bf16[56,1024]{1,0:T(8,128)(2,1)S(1)} %pad_maximum_fusion.9), channel_id=1, source_target_pairs={{0,8},{2,10},{4,12},{6,14},{8,0},{10,2},{12,4},{14,6},{16,24},{18,... | collective-permute-start | bytes 344072 | tf_op jit(solution)/shard_map/ppermute | solution.py:65
  14.2 11.7 %collective-permute-start.1 = (bf16[56,1024]{1,0:T(8,128)(2,1)S(1)}, bf16[56,1024]{1,0:T(8,128)(2,1)S(1)}, u32[]{:S(2)}, u32[]{:S(2)}) collective-permute-start(bf16[56,1024]{1,0:T(8,128)(2,1)S(1)} %pad_maximum_fusion.9), channel_id=1, source_target_pairs={{0,16},{2,18},{4,20},{6,22},{8,24},{10,26},{12,28},{14,30},{16,0},... | collective-permute-start | bytes 344072 | tf_op jit(solution)/shard_map/ppermute | solution.py:65
  16.7 9.1 %collective-permute-start.2 = (bf16[56,1024]{1,0:T(8,128)(2,1)S(1)}, bf16[56,1024]{1,0:T(8,128)(2,1)S(1)}, u32[]{:S(2)}, u32[]{:S(2)}) collective-permute-start(bf16[56,1024]{1,0:T(8,128)(2,1)S(1)} %pad_maximum_fusion.9), channel_id=1, source_target_pairs={{0,24},{2,26},{4,28},{6,30},{8,16},{10,18},{12,20},{14,22},{16,8},... | collective-permute-start | bytes 344072 | tf_op jit(solution)/shard_map/ppermute | solution.py:65
  16.7 15.9 %all-to-all-start = ((bf16[4,56,1920]{2,1,0:T(8,128)(2,1)}), bf16[4,56,1920]{2,1,0:T(8,128)(2,1)S(1)}, u32[]{:S(2)}, u32[]{:S(2)}) async-start(bf16[4,56,1920]{2,1,0:T(8,128)(2,1)} %maximum_bitcast_fusion), calls=%async_computation | async-start | bytes 1720320 | tf_op jit(solution)/shard_map/all_to_all | solution.py:68
  20.3 85.1 %all-gather.3.cloned.1.call-start = ((), (), s32[]{:S(2)}) async-start(), calls=%async_computation.3 | async-start | bytes 4300800 | tf_op jit(solution)/shard_map/all_gather | solution.py:601
  26.1 22.1 %copy-start.26 = (bf16[2,2,56,1024]{3,2,1,0:T(8,128)(2,1)}, bf16[2,2,56,1024]{3,2,1,0:T(8,128)(2,1)S(1)}, u32[]{:S(2)}) copy-start(bf16[2,2,56,1024]{3,2,1,0:T(8,128)(2,1)S(1)} %reverse_select_fusion) | copy-start | bytes 1376260
  33.6 149.4 %reduce-scatter.2.cloned.1.call-start = ((), (), s32[]{:S(2)}) async-start(), calls=%async_computation.4 | async-start | bytes 4300800 | tf_op jit(solution)/shard_map/reduce_scatter | solution.py:654
  34.0 29.0 %collective-permute-start.8 = (bf16[4,56,448]{2,1,0:T(8,128)(2,1)S(1)}, bf16[4,56,448]{2,1,0:T(8,128)(2,1)}, u32[]{:S(2)}, u32[]{:S(2)}) collective-permute-start(bf16[4,56,448]{2,1,0:T(8,128)(2,1)S(1)} %slice.121), channel_id=1, source_target_pairs={{0,4},{2,6},{4,0},{6,2},{8,12},{10,14},{12,8},{14,10},{16,20},{18,... | collective-permute-start | bytes 602120 | tf_op jit(solution)/shard_map/ppermute | solution.py:65
  48.3 14.7 %copy-start.27 = (bf16[2,2,56,1024]{3,2,1,0:T(8,128)(2,1)S(1)}, bf16[2,2,56,1024]{3,2,1,0:T(8,128)(2,1)}, u32[]{:S(2)}) copy-start(bf16[2,2,56,1024]{3,2,1,0:T(8,128)(2,1)} %copy-done.26) | copy-start | bytes 1376260
  50.5 17.7 %copy-start.7 = (bf16[2,64,896]{2,1,0:T(8,128)(2,1)S(1)}, bf16[2,64,896]{2,1,0:T(8,128)(2,1)}, u32[]{:S(2)}) copy-start(bf16[2,64,896]{2,1,0:T(8,128)(2,1)} %cotangent_ref.1) | copy-start | bytes 688132
  50.5 7.6 %collective-permute-start.3 = (bf16[128,128]{1,0:T(8,128)(2,1)S(1)}, bf16[128,128]{1,0:T(8,128)(2,1)S(1)}, u32[]{:S(2)}, u32[]{:S(2)}) collective-permute-start(bf16[128,128]{1,0:T(8,128)(2,1)S(1)} %get-tuple-element.73), channel_id=1, source_target_pairs={{0,8},{2,10},{4,12},{6,14},{8,0},{10,2},{12,4},{14,6},{16,24},{18,... | collective-permute-start | bytes 98312 | tf_op jit(solution)/shard_map/ppermute | solution.py:65
  51.4 10.2 %collective-permute-start.4 = (bf16[128,128]{1,0:T(8,128)(2,1)S(1)}, bf16[128,128]{1,0:T(8,128)(2,1)}, u32[]{:S(2)}, u32[]{:S(2)}) collective-permute-start(bf16[128,128]{1,0:T(8,128)(2,1)S(1)} %get-tuple-element.73), channel_id=1, source_target_pairs={{0,16},{2,18},{4,20},{6,22},{8,24},{10,26},{12,28},{14,30},{16,0},... | collective-permute-start | bytes 98312 | tf_op jit(solution)/shard_map/ppermute | solution.py:65
  54.9 6.7 %collective-permute-start.5 = (bf16[128,128]{1,0:T(8,128)(2,1)S(1)}, bf16[128,128]{1,0:T(8,128)(2,1)}, u32[]{:S(2)}, u32[]{:S(2)}) collective-permute-start(bf16[128,128]{1,0:T(8,128)(2,1)S(1)} %get-tuple-element.73), channel_id=1, source_target_pairs={{0,24},{2,26},{4,28},{6,30},{8,16},{10,18},{12,20},{14,22},{16,8},... | collective-permute-start | bytes 98312 | tf_op jit(solution)/shard_map/ppermute | solution.py:65
  62.4 5.0 %collective-permute-start.6 = (bf16[4,128,128]{2,1,0:T(8,128)(2,1)S(1)}, bf16[4,128,128]{2,1,0:T(8,128)(2,1)S(1)}, u32[]{:S(2)}, u32[]{:S(2)}) collective-permute-start(bf16[4,128,128]{2,1,0:T(8,128)(2,1)S(1)} %get-tuple-element.142), channel_id=1, source_target_pairs={{0,4},{2,6},{4,0},{6,2},{8,12},{10,14},{12,8},{14,10},{16,20},{18,... | collective-permute-start | bytes 393224 | tf_op jit(solution)/shard_map/ppermute | solution.py:65
  65.0 6.5 %collective-permute-start.9 = (bf16[4,2,56,448]{3,2,0,1:T(8,128)(2,1)}, bf16[4,2,56,448]{3,2,0,1:T(8,128)(2,1)}, u32[]{:S(2)}, u32[]{:S(2)}) collective-permute-start(bf16[4,2,56,448]{3,2,0,1:T(8,128)(2,1)} %pad_maximum_fusion.4), channel_id=1, source_target_pairs={{0,2},{2,0},{4,6},{6,4},{8,10},{10,8},{12,14},{14,12},{16,18},{18,... | collective-permute-start | bytes 1204232 | tf_op jit(solution)/shard_map/ppermute | solution.py:65
  68.2 1.5 collective-permute-start.7
  68.2 10.5 %collective-permute-start.11 = (bf16[128,896]{1,0:T(8,128)(2,1)S(1)}, bf16[128,896]{1,0:T(8,128)(2,1)}, u32[]{:S(2)}, u32[]{:S(2)}) collective-permute-start(bf16[128,896]{1,0:T(8,128)(2,1)S(1)} %bitcast.158), channel_id=1, source_target_pairs={{0,4},{2,6},{4,0},{6,2},{8,12},{10,14},{12,8},{14,10},{16,20},{18,... | collective-permute-start | bytes 688136 | tf_op jit(solution)/shard_map/ppermute | solution.py:65
  77.1 15.7 %copy-start.21 = (bf16[2,64,448]{2,1,0:T(8,128)(2,1)}, bf16[2,64,448]{2,1,0:T(8,128)(2,1)S(1)}, u32[]{:S(2)}) copy-start(bf16[2,64,448]{2,1,0:T(8,128)(2,1)S(1)} %get-tuple-element.98) | copy-start | bytes 344068
  77.1 7.7 %collective-permute-start.10 = (bf16[128,896]{1,0:T(8,128)(2,1)S(1)}, bf16[128,896]{1,0:T(8,128)(2,1)S(1)}, u32[]{:S(2)}, u32[]{:S(2)}) collective-permute-start(bf16[128,896]{1,0:T(8,128)(2,1)S(1)} %bitcast.166), channel_id=1, source_target_pairs={{0,1},{1,0},{2,3},{3,2},{4,5},{5,4},{6,7},{7,6},{8,9},{9,8},{10,11... | collective-permute-start | bytes 688136 | tf_op jit(solution)/shard_map/ppermute | solution.py:47
  79.7 5.3 %collective-permute-start.12 = (bf16[256,896]{1,0:T(8,128)(2,1)S(1)}, bf16[256,896]{1,0:T(8,128)(2,1)S(1)}, u32[]{:S(2)}, u32[]{:S(2)}) collective-permute-start(bf16[256,896]{1,0:T(8,128)(2,1)S(1)} %pad_maximum_fusion.5), channel_id=1, source_target_pairs={{0,2},{2,0},{4,6},{6,4},{8,10},{10,8},{12,14},{14,12},{16,18},{18,... | collective-permute-start | bytes 1376264 | tf_op jit(solution)/shard_map/ppermute | solution.py:65
  85.9 6.9 %collective-permute-start.13 = (bf16[128,896]{1,0:T(8,128)(2,1)S(1)}, bf16[128,896]{1,0:T(8,128)(2,1)S(1)}, u32[]{:S(2)}, u32[]{:S(2)}) collective-permute-start(bf16[128,896]{1,0:T(8,128)(2,1)S(1)} %get-tuple-element.121), channel_id=1, source_target_pairs={{0,4},{2,6},{4,0},{6,2},{8,12},{10,14},{12,8},{14,10},{16,20},{18,... | collective-permute-start | bytes 688136 | tf_op jit(solution)/shard_map/ppermute | solution.py:65
  92.8 1.9 collective-permute-start.14
  116.4 20.5 %copy-start.1 = (bf16[4,2,2,56,448]{4,3,2,1,0:T(8,128)(2,1)S(1)}, bf16[4,2,2,56,448]{4,3,2,1,0:T(8,128)(2,1)}, u32[]{:S(2)}) copy-start(bf16[4,2,2,56,448]{4,3,2,1,0:T(8,128)(2,1)} %copy-done) | copy-start | bytes 2408452
  116.4 20.5 %copy-start.8 = (bf16[2,64,896]{2,1,0:T(8,128)(2,1)S(1)}, bf16[2,64,896]{2,1,0:T(8,128)(2,1)}, u32[]{:S(2)}) copy-start(bf16[2,64,896]{2,1,0:T(8,128)(2,1)} %cotangent_ref.1) | copy-start | bytes 688132
  116.4 20.5 %copy-start.16 = (bf16[128,448]{1,0:T(8,128)(2,1)S(1)}, bf16[128,448]{1,0:T(8,128)(2,1)}, u32[]{:S(2)}) copy-start(bf16[128,448]{1,0:T(8,128)(2,1)} %copy-done.14) | copy-start | bytes 344068
  116.4 2.1 collective-permute-start.15
  119.5 7.7 %collective-permute-start.16 = (bf16[128,896]{1,0:T(8,128)(2,1)S(1)}, bf16[128,896]{1,0:T(8,128)(2,1)S(1)}, u32[]{:S(2)}, u32[]{:S(2)}) collective-permute-start(bf16[128,896]{1,0:T(8,128)(2,1)S(1)} %add_convert_fusion.6), channel_id=1, source_target_pairs={{0,4},{2,6},{4,0},{6,2},{8,12},{10,14},{12,8},{14,10},{16,20},{18,... | collective-permute-start | bytes 688136 | tf_op jit(solution)/shard_map/ppermute | solution.py:65
  121.1 7.2 %collective-permute-start.17 = (bf16[256,896]{1,0:T(8,128)(2,1)}, bf16[256,896]{1,0:T(8,128)(2,1)S(1)}, u32[]{:S(2)}, u32[]{:S(2)}) collective-permute-start(bf16[256,896]{1,0:T(8,128)(2,1)} %get-tuple-element.87), channel_id=1, source_target_pairs={{0,2},{2,0},{4,6},{6,4},{8,10},{10,8},{12,14},{14,12},{16,18},{18,... | collective-permute-start | bytes 1376264 | tf_op jit(solution)/shard_map/ppermute | solution.py:65
  128.3 7.0 %collective-permute-start.18 = (bf16[128,896]{1,0:T(8,128)(2,1)S(1)}, bf16[128,896]{1,0:T(8,128)(2,1)S(1)}, u32[]{:S(2)}, u32[]{:S(2)}) collective-permute-start(bf16[128,896]{1,0:T(8,128)(2,1)S(1)} %add_convert_fusion.5.own_ref), channel_id=1, source_target_pairs={{0,1},{1,0},{2,3},{3,2},{4,5},{5,4},{6,7},{7,6},{8,9},{9,8},{10,11... | collective-permute-start | bytes 688136 | tf_op jit(solution)/shard_map/ppermute | solution.py:662
  135.3 6.2 %collective-permute-start.19 = (bf16[128,896]{1,0:T(8,128)(2,1)S(1)}, bf16[128,896]{1,0:T(8,128)(2,1)S(1)}, u32[]{:S(2)}, u32[]{:S(2)}) collective-permute-start(bf16[128,896]{1,0:T(8,128)(2,1)S(1)} %slice.127), channel_id=1, source_target_pairs={{0,4},{2,6},{4,0},{6,2},{8,12},{10,14},{12,8},{14,10},{16,20},{18,... | collective-permute-start | bytes 688136 | tf_op jit(solution)/shard_map/ppermute | solution.py:65
  142.2 1.6 collective-permute-start.20
  146.4 6.2 %collective-permute-start.22 = (bf16[8,56,896]{2,1,0:T(8,128)(2,1)}, bf16[8,56,896]{2,1,0:T(8,128)(2,1)}, u32[]{:S(2)}, u32[]{:S(2)}) collective-permute-start(bf16[8,56,896]{2,1,0:T(8,128)(2,1)} %get-tuple-element.101), channel_id=1, source_target_pairs={{0,2},{2,0},{4,6},{6,4},{8,10},{10,8},{12,14},{14,12},{16,18},{18,... | collective-permute-start | bytes 2408456 | tf_op jit(solution)/shard_map/ppermute | solution.py:65
  146.7 5.8 %collective-permute-start.21 = (bf16[512,128]{1,0:T(8,128)(2,1)S(1)}, bf16[512,128]{1,0:T(8,128)(2,1)S(1)}, u32[]{:S(2)}, u32[]{:S(2)}) collective-permute-start(bf16[512,128]{1,0:T(8,128)(2,1)S(1)} %slice.161), channel_id=1, source_target_pairs={{0,4},{2,6},{4,0},{6,2},{8,12},{10,14},{12,8},{14,10},{16,20},{18,... | collective-permute-start | bytes 393224 | tf_op jit(solution)/shard_map/ppermute | solution.py:65
  155.9 11.2 %collective-permute-start.26 = (bf16[4,56,896]{2,1,0:T(8,128)(2,1)}, bf16[4,56,896]{2,1,0:T(8,128)(2,1)}, u32[]{:S(2)}, u32[]{:S(2)}) collective-permute-start(bf16[4,56,896]{2,1,0:T(8,128)(2,1)} %dynamic-slice_bitcast_fusion), channel_id=1, source_target_pairs={{0,4},{2,6},{4,0},{6,2},{8,12},{10,14},{12,8},{14,10},{16,20},{18,... | collective-permute-start | bytes 1204232 | tf_op jit(solution)/shard_map/ppermute | solution.py:65
  157.4 5.0 %collective-permute-start.23 = (bf16[128,128]{1,0:T(8,128)(2,1)S(1)}, bf16[128,128]{1,0:T(8,128)(2,1)S(1)}, u32[]{:S(2)}, u32[]{:S(2)}) collective-permute-start(bf16[128,128]{1,0:T(8,128)(2,1)S(1)} %get-tuple-element.138), channel_id=1, source_target_pairs={{0,8},{2,10},{4,12},{6,14},{8,0},{10,2},{12,4},{14,6},{16,24},{18,... | collective-permute-start | bytes 98312 | tf_op jit(solution)/shard_map/ppermute | solution.py:65
  157.5 9.6 %collective-permute-start.24 = (bf16[128,128]{1,0:T(8,128)(2,1)S(1)}, bf16[128,128]{1,0:T(8,128)(2,1)S(1)}, u32[]{:S(2)}, u32[]{:S(2)}) collective-permute-start(bf16[128,128]{1,0:T(8,128)(2,1)S(1)} %get-tuple-element.140), channel_id=1, source_target_pairs={{0,16},{2,18},{4,20},{6,22},{8,24},{10,26},{12,28},{14,30},{16,0},... | collective-permute-start | bytes 98312 | tf_op jit(solution)/shard_map/ppermute | solution.py:65
  159.0 8.1 %collective-permute-start.25 = (bf16[128,128]{1,0:T(8,128)(2,1)S(1)}, bf16[128,128]{1,0:T(8,128)(2,1)S(1)}, u32[]{:S(2)}, u32[]{:S(2)}) collective-permute-start(bf16[128,128]{1,0:T(8,128)(2,1)S(1)} %get-tuple-element.139), channel_id=1, source_target_pairs={{0,24},{2,26},{4,28},{6,30},{8,16},{10,18},{12,20},{14,22},{16,8},... | collective-permute-start | bytes 98312 | tf_op jit(solution)/shard_map/ppermute | solution.py:65
  169.6 1.8 collective-permute-start.27
  169.8 8.1 %collective-permute-start.30 = (bf16[128,896]{1,0:T(8,128)(2,1)S(1)}, bf16[128,896]{1,0:T(8,128)(2,1)S(1)}, u32[]{:S(2)}, u32[]{:S(2)}) collective-permute-start(bf16[128,896]{1,0:T(8,128)(2,1)S(1)} %copy-done.30), channel_id=1, source_target_pairs={{0,1},{1,0},{2,3},{3,2},{4,5},{5,4},{6,7},{7,6},{8,9},{9,8},{10,11... | collective-permute-start | bytes 688136 | tf_op jit(solution)/shard_map/ppermute | solution.py:706
  171.4 7.2 %collective-permute-start.28 = (bf16[4,56,256]{2,1,0:T(8,128)(2,1)S(1)}, bf16[4,56,256]{2,1,0:T(8,128)(2,1)S(1)}, u32[]{:S(2)}, u32[]{:S(2)}) collective-permute-start(bf16[4,56,256]{2,1,0:T(8,128)(2,1)S(1)} %dynamic-slice_bitcast_fusion.4), channel_id=1, source_target_pairs={{0,4},{2,6},{4,0},{6,2},{8,12},{10,14},{12,8},{14,10},{16,20},{18,... | collective-permute-start | bytes 344072 | tf_op jit(solution)/shard_map/ppermute | solution.py:65
  178.7 4.2 %collective-permute-start.29 = (bf16[4,56,128]{2,1,0:T(8,128)(2,1)S(1)}, bf16[4,56,128]{2,1,0:T(8,128)(2,1)S(1)}, u32[]{:S(2)}, u32[]{:S(2)}) collective-permute-start(bf16[4,56,128]{2,1,0:T(8,128)(2,1)S(1)} %slice.163), channel_id=1, source_target_pairs={{0,1},{1,0},{2,3},{3,2},{4,5},{5,4},{6,7},{7,6},{8,9},{9,8},{10,11... | collective-permute-start | bytes 172040 | tf_op jit(solution)/shard_map/ppermute | solution.py:763
  183.1 16.4 %copy-start.44 = (bf16[56]{0:T(256)(128)(2,1)S(1)}, bf16[56]{0:T(256)(128)(2,1)}, u32[]{:S(2)}) copy-start(bf16[56]{0:T(256)(128)(2,1)} %param.19) | copy-start | bytes 340
  183.1 16.9 %copy-start.45 = (bf16[56]{0:T(256)(128)(2,1)S(1)}, bf16[56]{0:T(256)(128)(2,1)}, u32[]{:S(2)}) copy-start(bf16[56]{0:T(256)(128)(2,1)} %param.20) | copy-start | bytes 340
  183.1 9.7 %collective-permute-start.32 = (bf16[56,1152]{1,0:T(8,128)(2,1)S(1)}, bf16[56,1152]{1,0:T(8,128)(2,1)S(1)}, u32[]{:S(2)}, u32[]{:S(2)}) collective-permute-start(bf16[56,1152]{1,0:T(8,128)(2,1)S(1)} %get-tuple-element.131), channel_id=1, source_target_pairs={{0,8},{2,10},{4,12},{6,14},{8,0},{10,2},{12,4},{14,6},{16,24},{18,... | collective-permute-start | bytes 387080 | tf_op jit(solution)/shard_map/ppermute | solution.py:65
  184.8 12.1 %collective-permute-start.33 = (bf16[56,1152]{1,0:T(8,128)(2,1)S(1)}, bf16[56,1152]{1,0:T(8,128)(2,1)S(1)}, u32[]{:S(2)}, u32[]{:S(2)}) collective-permute-start(bf16[56,1152]{1,0:T(8,128)(2,1)S(1)} %get-tuple-element.133), channel_id=1, source_target_pairs={{0,16},{2,18},{4,20},{6,22},{8,24},{10,26},{12,28},{14,30},{16,0},... | collective-permute-start | bytes 387080 | tf_op jit(solution)/shard_map/ppermute | solution.py:65
  185.2 11.6 %collective-permute-start.34 = (bf16[56,1152]{1,0:T(8,128)(2,1)S(1)}, bf16[56,1152]{1,0:T(8,128)(2,1)S(1)}, u32[]{:S(2)}, u32[]{:S(2)}) collective-permute-start(bf16[56,1152]{1,0:T(8,128)(2,1)S(1)} %get-tuple-element.132), channel_id=1, source_target_pairs={{0,24},{2,26},{4,28},{6,30},{8,16},{10,18},{12,20},{14,22},{16,8},... | collective-permute-start | bytes 387080 | tf_op jit(solution)/shard_map/ppermute | solution.py:65
  187.7 16.1 %all-to-all-start.1 = ((bf16[4,56,1920]{2,1,0:T(8,128)(2,1)}), bf16[4,56,1920]{2,1,0:T(8,128)(2,1)S(1)}, u32[]{:S(2)}, u32[]{:S(2)}) async-start(bf16[4,56,1920]{2,1,0:T(8,128)(2,1)} %bitcast.186), calls=%async_computation.2 | async-start | bytes 1720320 | tf_op jit(solution)/shard_map/all_to_all | solution.py:68
  191.3 9.9 %collective-permute-start.31 = (bf16[128,896]{1,0:T(8,128)(2,1)S(1)}, bf16[128,896]{1,0:T(8,128)(2,1)S(1)}, u32[]{:S(2)}, u32[]{:S(2)}) collective-permute-start(bf16[128,896]{1,0:T(8,128)(2,1)S(1)} %get-tuple-element.115), channel_id=1, source_target_pairs={{0,1},{1,0},{2,3},{3,2},{4,5},{5,4},{6,7},{7,6},{8,9},{9,8},{10,11... | collective-permute-start | bytes 688136 | tf_op jit(solution)/shard_map/ppermute | solution.py:47
  (38 other events, 215.6 us)
Sparse Core Ops, SparseCore 0:
  33.7 71.5 all-gather.2
  116.5 65.4 reduce-scatter.1

commit v6 on v5

--- a/solution.py
+++ b/solution.py
@@ -15,7 +15,7 @@
 MASKED = -1e30
 LOWEST = -1e29
 BRIEF = pl.CostEstimate(flops=1, bytes_accessed=1, transcendentals=0)
-VMEM_LIMIT = 48 * 1024 * 1024
+VMEM_LIMIT = 32 * 1024 * 1024
 FFN_VMEM_LIMIT = 56 * 1024 * 1024
 
 

time: 213 us -> 213 us (level)
  no operation moved by 1% of the time
where the time goes in v6:
time: 213 us
  waiting for transfers between devices  73.1 us (34%)
  starting transfers between devices  44.4 us (21%)
  other arithmetic  27 us (13%)
  Pallas kernels  22 us (10%)
  local copies, waits for them, and re-layouts  17.3 us (8%)
  between operations  15.1 us (7%)
  blocking collectives  13.8 us (6%)
    ppermute x30, waiting for transfers between devices, flip(): lax.ppermute(values, 'ctx', [(i, i ^ bit) for i in range(self.count)])  41.1 us
    ppermute x30, starting transfers between devices, flip(): lax.ppermute(values, 'ctx', [(i, i ^ bit) for i in range(self.count)])  29.4 us
    all_gather x1, blocking collectives, spread_near(): whole = lax.all_gather(values, 'ctx', axis=0, axis_index_groups=self.near)  13.8 us
    pallas_call x1, Pallas kernels, ffn_call(): pl.pallas_call(functools.partial(ffn_kernel, part), in_specs=[far, far],...  11 us
    pallas_call x5, Pallas kernels, whole_call(): pl.pallas_call(kernel, in_specs=in_specs, out_specs=[whole] * len(out_sha...  11 us
    unnamed x98, local copies, waits for them, and re-layouts  9.92 us
    all_gather x1, waiting for transfers between devices, local(): lax.all_gather(w_ffn, 'ctx', axis=0, tiled=True, axis_index_groups=groups...  8.13 us
    all_to_all x2, waiting for transfers between devices, swap_near(): lax.all_to_all(values, 'ctx', 0, 0, tiled=True, axis_index_groups=self.near)  7.9 us
  transfers between devices with their start and end apart: 39, of which 22 were waited for; matrix products, arithmetic and copies ran while one was open for 15% of the time, Pallas kernels for 5%

profile of v6, /device:TPU:0, one launch (start us, length us, event | category | flops | bytes accessed | tf_op | source)
XLA Modules:
  0.0 212.7 jit_solution(8333766336924896072)
XLA Ops:
  7.9 1.2 multiply_convert_fusion.1
  11.1 3.0 %collective-permute-start = (bf16[56,1024]{1,0:T(8,128)(2,1)S(1)}, bf16[56,1024]{1,0:T(8,128)(2,1)S(1)}, u32[]{:S(2)}, u32[]{:S(2)}) collective-permute-start(bf16[56,1024]{1,0:T(8,128)(2,1)S(1)} %pad_maximum_fusion.9), channel_id=1, source_target_pairs={{0,8},{2,10},{4,12},{6,14},{8,0},{10,2},{12,4},{14,6},{16,24},{18,... | collective-permute-start | bytes 344072 | tf_op jit(solution)/shard_map/ppermute | solution.py:65
  14.2 2.6 %collective-permute-start.1 = (bf16[56,1024]{1,0:T(8,128)(2,1)S(1)}, bf16[56,1024]{1,0:T(8,128)(2,1)S(1)}, u32[]{:S(2)}, u32[]{:S(2)}) collective-permute-start(bf16[56,1024]{1,0:T(8,128)(2,1)S(1)} %pad_maximum_fusion.9), channel_id=1, source_target_pairs={{0,16},{2,18},{4,20},{6,22},{8,24},{10,26},{12,28},{14,30},{16,0},... | collective-permute-start | bytes 344072 | tf_op jit(solution)/shard_map/ppermute | solution.py:65
  16.7 3.5 %all-to-all-start = ((bf16[4,56,1920]{2,1,0:T(8,128)(2,1)}), bf16[4,56,1920]{2,1,0:T(8,128)(2,1)S(1)}, u32[]{:S(2)}, u32[]{:S(2)}) async-start(bf16[4,56,1920]{2,1,0:T(8,128)(2,1)} %maximum_bitcast_fusion), calls=%async_computation | async-start | bytes 1720320 | tf_op jit(solution)/shard_map/all_to_all | solution.py:68
  24.1 1.3 compare_convert_fusion.same_ref
  26.1 6.5 %all-to-all-done = bf16[4,56,1920]{2,1,0:T(8,128)(2,1)S(1)} async-done(((bf16[4,56,1920]{2,1,0:T(8,128)(2,1)}), bf16[4,56,1920]{2,1,0:T(8,128)(2,1)S(1)}, u32[]{:S(2)}, u32[]{:S(2)}) %all-to-all-start) | async-done | bytes 860192 | tf_op jit(solution)/shard_map/all_to_all | solution.py:68
  34.4 13.8 %all-gather = bf16[16,56,576]{2,1,0:T(8,128)(2,1)S(1)} all-gather(bf16[4,56,576]{2,1,0:T(8,128)(2,1)S(1)} %slice.120), channel_id=2, replica_groups={{0,2,4,6},{8,10,12,14},{16,18,20,22},{24,26,28,30},{1,3,5,7},{9,11,13,1..., dimensions={0}, use_global_device_ids=true | all-gather | bytes 1290240 | tf_op jit(solution)/shard_map/all_gather | solution.py:87
  51.4 3.5 %collective-permute-start.4 = (bf16[128,128]{1,0:T(8,128)(2,1)S(1)}, bf16[128,128]{1,0:T(8,128)(2,1)}, u32[]{:S(2)}, u32[]{:S(2)}) collective-permute-start(bf16[128,128]{1,0:T(8,128)(2,1)S(1)} %get-tuple-element.73), channel_id=1, source_target_pairs={{0,16},{2,18},{4,20},{6,22},{8,24},{10,26},{12,28},{14,30},{16,0},... | collective-permute-start | bytes 98312 | tf_op jit(solution)/shard_map/ppermute | solution.py:65
  54.9 3.2 %collective-permute-done.3 = bf16[128,128]{1,0:T(8,128)(2,1)S(1)} collective-permute-done((bf16[128,128]{1,0:T(8,128)(2,1)S(1)}, bf16[128,128]{1,0:T(8,128)(2,1)S(1)}, u32[]{:S(2)}, u32[]{:S(2)}) %collective-permute-start.3) | collective-permute-done | bytes 32800 | tf_op jit(solution)/shard_map/ppermute | solution.py:65
  58.2 3.4 %collective-permute-done.4 = bf16[128,128]{1,0:T(8,128)(2,1)} collective-permute-done((bf16[128,128]{1,0:T(8,128)(2,1)S(1)}, bf16[128,128]{1,0:T(8,128)(2,1)}, u32[]{:S(2)}, u32[]{:S(2)}) %collective-permute-start.4) | collective-permute-done | bytes 32800 | tf_op jit(solution)/shard_map/ppermute | solution.py:65
  65.0 2.5 %collective-permute-done.6 = bf16[4,128,128]{2,1,0:T(8,128)(2,1)S(1)} collective-permute-done((bf16[4,128,128]{2,1,0:T(8,128)(2,1)S(1)}, bf16[4,128,128]{2,1,0:T(8,128)(2,1)S(1)}, u32[]{:S(2)}, u32[]{:S(2)}) %collective-permute-start.6) | collective-permute-done | bytes 131104 | tf_op jit(solution)/shard_map/ppermute | solution.py:65
  71.5 1.3 select_bitcast_fusion.1
  73.7 3.4 %forward.1 = (bf16[2,64,448]{2,1,0:T(8,128)(2,1)S(1)}, bf16[2,64,896]{2,1,0:T(8,128)(2,1)S(1)}, f32[1,8,128]{2,1,0:T(8,128)S(1)}, f32[2,1,448]{2,1,0:T(1,128)S(1)}) custom-call(bf16[2,64,448]{2,1,0:T(8,128)(2,1)S(1)} %bitcast.161, bf16[16,2,64,128]{3,2,1,0:T(8,128)(2,1)S(1)} %bitcast.153, s32[2,1024,1]{2,1,0:T(8,128)S(1)} %broadcast_add_fusion.key_pos_ref, ...), custom_call_target="tpu_custom_call" | custom-call | flops 1 | bytes 1 | tf_op jit(solution)/shard_map/forward/pallas_call | solution.py:183
  77.1 1.6 collective-permute-start.10
  79.8 5.1 %collective-permute-done.10 = bf16[128,896]{1,0:T(8,128)(2,1)S(1)} collective-permute-done((bf16[128,896]{1,0:T(8,128)(2,1)S(1)}, bf16[128,896]{1,0:T(8,128)(2,1)S(1)}, u32[]{:S(2)}, u32[]{:S(2)}) %collective-permute-start.10) | collective-permute-done | bytes 229408 | tf_op jit(solution)/shard_map/ppermute | solution.py:47
  86.6 6.2 %collective-permute-done.13 = bf16[128,896]{1,0:T(8,128)(2,1)S(1)} collective-permute-done((bf16[128,896]{1,0:T(8,128)(2,1)S(1)}, bf16[128,896]{1,0:T(8,128)(2,1)S(1)}, u32[]{:S(2)}, u32[]{:S(2)}) %collective-permute-start.13) | collective-permute-done | bytes 229408 | tf_op jit(solution)/shard_map/ppermute | solution.py:65
  97.2 8.1 %all-gather.3.cloned.1.call-done.w_source = bf16[896,1920]{1,0:T(8,128)(2,1)} async-done(((bf16[224,1920]{1,0:T(8,128)(2,1)}), bf16[896,1920]{1,0:T(8,128)(2,1)}) %all-gather.3.cloned.1.call-update) | async-done | bytes 3440656 | tf_op jit(solution)/shard_map/all_gather | solution.py:601
  105.3 11.0 %ffn.1 = (bf16[256,896]{1,0:T(8,128)(2,1)}, bf16[256,896]{1,0:T(8,128)(2,1)}, bf16[256,896]{1,0:T(8,128)(2,1)}, bf16[256,896]{1,0:T(8,128)(2,1)}, bf16[896,1920]{1,0:T(8,128)(2,1)}) custom-call(bf16[1024,896]{1,0:T(8,128)(2,1)} %constant_dynamic-update-slice_fusion.token_source, bf16[896,1920]{1,0:T(8,128)(2,1)} %all-gather.3.cloned.1.call-done.w_source), custom_call_target="tpu_custom_call" | custom-call | flops 1 | bytes 1 | tf_op jit(solution)/shard_map/ffn/pallas_call | solution.py:446
  116.5 2.0 collective-permute-done.15
  119.5 1.6 collective-permute-start.16
  121.1 6.1 %collective-permute-done.16 = bf16[128,896]{1,0:T(8,128)(2,1)S(1)} collective-permute-done((bf16[128,896]{1,0:T(8,128)(2,1)S(1)}, bf16[128,896]{1,0:T(8,128)(2,1)S(1)}, u32[]{:S(2)}, u32[]{:S(2)}) %collective-permute-start.16) | collective-permute-done | bytes 229408 | tf_op jit(solution)/shard_map/ppermute | solution.py:65
  128.3 1.6 collective-permute-start.18
  129.8 1.1 add_convert_fusion.1
  131.0 4.3 %collective-permute-done.18.other_ref = bf16[128,896]{1,0:T(8,128)(2,1)S(1)} collective-permute-done((bf16[128,896]{1,0:T(8,128)(2,1)S(1)}, bf16[128,896]{1,0:T(8,128)(2,1)S(1)}, u32[]{:S(2)}, u32[]{:S(2)}) %collective-permute-start.18) | collective-permute-done | bytes 229408 | tf_op jit(solution)/shard_map/ppermute | solution.py:662
  135.3 1.6 collective-permute-start.19
  136.9 4.2 %backward.1 = (f32[2,64,896]{2,1,0:T(8,128)S(1)}, bf16[2,64,896]{2,1,0:T(8,128)(2,1)S(1)}, bf16[2,64,448]{2,1,0:T(8,128)(2,1)S(1)}, bf16[16,2,64,128]{3,2,1,0:T(8,128)(2,1)S(1)}) custom-call(bf16[2,64,448]{2,1,0:T(8,128)(2,1)S(1)} %bitcast.162, bf16[16,2,64,128]{3,2,1,0:T(8,128)(2,1)S(1)} %bitcast.154, s32[2,1024,1]{2,1,0:T(8,128)S(1)} %broadcast_add_fusion.key_pos_ref, ...), custom_call_target="tpu_custom_call" | custom-call | flops 1 | bytes 1 | tf_op jit(solution)/shard_map/backward/pallas_call | solution.py:183
  142.3 1.5 collective-permute-done.20
  143.8 1.7 wide.1
  146.7 1.6 collective-permute-start.21
  148.2 4.2 %collective-permute-done.21 = bf16[512,128]{1,0:T(8,128)(2,1)S(1)} collective-permute-done((bf16[512,128]{1,0:T(8,128)(2,1)S(1)}, bf16[512,128]{1,0:T(8,128)(2,1)S(1)}, u32[]{:S(2)}, u32[]{:S(2)}) %collective-permute-start.21) | collective-permute-done | bytes 131104 | tf_op jit(solution)/shard_map/ppermute | solution.py:65
  152.6 1.6 add_convert_fusion
  155.9 1.5 collective-permute-start.26
  157.5 1.5 collective-permute-start.24
  159.0 2.9 %collective-permute-start.25 = (bf16[128,128]{1,0:T(8,128)(2,1)S(1)}, bf16[128,128]{1,0:T(8,128)(2,1)S(1)}, u32[]{:S(2)}, u32[]{:S(2)}) collective-permute-start(bf16[128,128]{1,0:T(8,128)(2,1)S(1)} %get-tuple-element.139), channel_id=1, source_target_pairs={{0,24},{2,26},{4,28},{6,30},{8,16},{10,18},{12,20},{14,22},{16,8},... | collective-permute-start | bytes 98312 | tf_op jit(solution)/shard_map/ppermute | solution.py:65
  162.4 4.7 %collective-permute-done.24 = bf16[128,128]{1,0:T(8,128)(2,1)S(1)} collective-permute-done((bf16[128,128]{1,0:T(8,128)(2,1)S(1)}, bf16[128,128]{1,0:T(8,128)(2,1)S(1)}, u32[]{:S(2)}, u32[]{:S(2)}) %collective-permute-start.24) | collective-permute-done | bytes 32800 | tf_op jit(solution)/shard_map/ppermute | solution.py:65
  167.2 1.3 copy-done.3
  169.8 1.5 collective-permute-start.30
  171.4 1.5 collective-permute-start.28
  173.0 4.9 %collective-permute-done.30 = bf16[128,896]{1,0:T(8,128)(2,1)S(1)} collective-permute-done((bf16[128,896]{1,0:T(8,128)(2,1)S(1)}, bf16[128,896]{1,0:T(8,128)(2,1)S(1)}, u32[]{:S(2)}, u32[]{:S(2)}) %collective-permute-start.30) | collective-permute-done | bytes 229408 | tf_op jit(solution)/shard_map/ppermute | solution.py:706
  178.7 1.5 collective-permute-start.29
  181.3 1.6 collective-permute-done.29
  183.1 1.6 collective-permute-start.32
  185.2 2.4 %collective-permute-start.34 = (bf16[56,1152]{1,0:T(8,128)(2,1)S(1)}, bf16[56,1152]{1,0:T(8,128)(2,1)S(1)}, u32[]{:S(2)}, u32[]{:S(2)}) collective-permute-start(bf16[56,1152]{1,0:T(8,128)(2,1)S(1)} %get-tuple-element.132), channel_id=1, source_target_pairs={{0,24},{2,26},{4,28},{6,30},{8,16},{10,18},{12,20},{14,22},{16,8},... | collective-permute-start | bytes 387080 | tf_op jit(solution)/shard_map/ppermute | solution.py:65
  187.7 3.6 %all-to-all-start.1 = ((bf16[4,56,1920]{2,1,0:T(8,128)(2,1)}), bf16[4,56,1920]{2,1,0:T(8,128)(2,1)S(1)}, u32[]{:S(2)}, u32[]{:S(2)}) async-start(bf16[4,56,1920]{2,1,0:T(8,128)(2,1)} %bitcast.186), calls=%async_computation.2 | async-start | bytes 1720320 | tf_op jit(solution)/shard_map/all_to_all | solution.py:68
  191.3 1.5 collective-permute-start.31
  192.9 4.0 %collective-permute-done.33 = bf16[56,1152]{1,0:T(8,128)(2,1)S(1)} collective-permute-done((bf16[56,1152]{1,0:T(8,128)(2,1)S(1)}, bf16[56,1152]{1,0:T(8,128)(2,1)S(1)}, u32[]{:S(2)}, u32[]{:S(2)}) %collective-permute-start.33) | collective-permute-done | bytes 129056 | tf_op jit(solution)/shard_map/ppermute | solution.py:65
  202.3 1.4 all-to-all-done.1
  204.8 1.1 convert_multiply_fusion
  (252 shorter events, 44.5 us)
Async XLA Ops:
  11.1 14.4 %collective-permute-start = (bf16[56,1024]{1,0:T(8,128)(2,1)S(1)}, bf16[56,1024]{1,0:T(8,128)(2,1)S(1)}, u32[]{:S(2)}, u32[]{:S(2)}) collective-permute-start(bf16[56,1024]{1,0:T(8,128)(2,1)S(1)} %pad_maximum_fusion.9), channel_id=1, source_target_pairs={{0,8},{2,10},{4,12},{6,14},{8,0},{10,2},{12,4},{14,6},{16,24},{18,... | collective-permute-start | bytes 344072 | tf_op jit(solution)/shard_map/ppermute | solution.py:65
  14.2 11.7 %collective-permute-start.1 = (bf16[56,1024]{1,0:T(8,128)(2,1)S(1)}, bf16[56,1024]{1,0:T(8,128)(2,1)S(1)}, u32[]{:S(2)}, u32[]{:S(2)}) collective-permute-start(bf16[56,1024]{1,0:T(8,128)(2,1)S(1)} %pad_maximum_fusion.9), channel_id=1, source_target_pairs={{0,16},{2,18},{4,20},{6,22},{8,24},{10,26},{12,28},{14,30},{16,0},... | collective-permute-start | bytes 344072 | tf_op jit(solution)/shard_map/ppermute | solution.py:65
  16.7 9.1 %collective-permute-start.2 = (bf16[56,1024]{1,0:T(8,128)(2,1)S(1)}, bf16[56,1024]{1,0:T(8,128)(2,1)S(1)}, u32[]{:S(2)}, u32[]{:S(2)}) collective-permute-start(bf16[56,1024]{1,0:T(8,128)(2,1)S(1)} %pad_maximum_fusion.9), channel_id=1, source_target_pairs={{0,24},{2,26},{4,28},{6,30},{8,16},{10,18},{12,20},{14,22},{16,8},... | collective-permute-start | bytes 344072 | tf_op jit(solution)/shard_map/ppermute | solution.py:65
  16.7 15.9 %all-to-all-start = ((bf16[4,56,1920]{2,1,0:T(8,128)(2,1)}), bf16[4,56,1920]{2,1,0:T(8,128)(2,1)S(1)}, u32[]{:S(2)}, u32[]{:S(2)}) async-start(bf16[4,56,1920]{2,1,0:T(8,128)(2,1)} %maximum_bitcast_fusion), calls=%async_computation | async-start | bytes 1720320 | tf_op jit(solution)/shard_map/all_to_all | solution.py:68
  20.3 85.1 %all-gather.3.cloned.1.call-start = ((), (), s32[]{:S(2)}) async-start(), calls=%async_computation.3 | async-start | bytes 4300800 | tf_op jit(solution)/shard_map/all_gather | solution.py:601
  26.1 22.1 %copy-start.26 = (bf16[2,2,56,1024]{3,2,1,0:T(8,128)(2,1)}, bf16[2,2,56,1024]{3,2,1,0:T(8,128)(2,1)S(1)}, u32[]{:S(2)}) copy-start(bf16[2,2,56,1024]{3,2,1,0:T(8,128)(2,1)S(1)} %reverse_select_fusion) | copy-start | bytes 1376260
  33.6 149.4 %reduce-scatter.2.cloned.1.call-start = ((), (), s32[]{:S(2)}) async-start(), calls=%async_computation.4 | async-start | bytes 4300800 | tf_op jit(solution)/shard_map/reduce_scatter | solution.py:654
  34.0 29.0 %collective-permute-start.8 = (bf16[4,56,448]{2,1,0:T(8,128)(2,1)S(1)}, bf16[4,56,448]{2,1,0:T(8,128)(2,1)}, u32[]{:S(2)}, u32[]{:S(2)}) collective-permute-start(bf16[4,56,448]{2,1,0:T(8,128)(2,1)S(1)} %slice.121), channel_id=1, source_target_pairs={{0,4},{2,6},{4,0},{6,2},{8,12},{10,14},{12,8},{14,10},{16,20},{18,... | collective-permute-start | bytes 602120 | tf_op jit(solution)/shard_map/ppermute | solution.py:65
  48.3 14.7 %copy-start.27 = (bf16[2,2,56,1024]{3,2,1,0:T(8,128)(2,1)S(1)}, bf16[2,2,56,1024]{3,2,1,0:T(8,128)(2,1)}, u32[]{:S(2)}) copy-start(bf16[2,2,56,1024]{3,2,1,0:T(8,128)(2,1)} %copy-done.26) | copy-start | bytes 1376260
  50.5 17.7 %copy-start.7 = (bf16[2,64,896]{2,1,0:T(8,128)(2,1)S(1)}, bf16[2,64,896]{2,1,0:T(8,128)(2,1)}, u32[]{:S(2)}) copy-start(bf16[2,64,896]{2,1,0:T(8,128)(2,1)} %cotangent_ref.1) | copy-start | bytes 688132
  50.5 7.6 %collective-permute-start.3 = (bf16[128,128]{1,0:T(8,128)(2,1)S(1)}, bf16[128,128]{1,0:T(8,128)(2,1)S(1)}, u32[]{:S(2)}, u32[]{:S(2)}) collective-permute-start(bf16[128,128]{1,0:T(8,128)(2,1)S(1)} %get-tuple-element.73), channel_id=1, source_target_pairs={{0,8},{2,10},{4,12},{6,14},{8,0},{10,2},{12,4},{14,6},{16,24},{18,... | collective-permute-start | bytes 98312 | tf_op jit(solution)/shard_map/ppermute | solution.py:65
  51.4 10.2 %collective-permute-start.4 = (bf16[128,128]{1,0:T(8,128)(2,1)S(1)}, bf16[128,128]{1,0:T(8,128)(2,1)}, u32[]{:S(2)}, u32[]{:S(2)}) collective-permute-start(bf16[128,128]{1,0:T(8,128)(2,1)S(1)} %get-tuple-element.73), channel_id=1, source_target_pairs={{0,16},{2,18},{4,20},{6,22},{8,24},{10,26},{12,28},{14,30},{16,0},... | collective-permute-start | bytes 98312 | tf_op jit(solution)/shard_map/ppermute | solution.py:65
  54.9 6.7 %collective-permute-start.5 = (bf16[128,128]{1,0:T(8,128)(2,1)S(1)}, bf16[128,128]{1,0:T(8,128)(2,1)}, u32[]{:S(2)}, u32[]{:S(2)}) collective-permute-start(bf16[128,128]{1,0:T(8,128)(2,1)S(1)} %get-tuple-element.73), channel_id=1, source_target_pairs={{0,24},{2,26},{4,28},{6,30},{8,16},{10,18},{12,20},{14,22},{16,8},... | collective-permute-start | bytes 98312 | tf_op jit(solution)/shard_map/ppermute | solution.py:65
  62.4 5.0 %collective-permute-start.6 = (bf16[4,128,128]{2,1,0:T(8,128)(2,1)S(1)}, bf16[4,128,128]{2,1,0:T(8,128)(2,1)S(1)}, u32[]{:S(2)}, u32[]{:S(2)}) collective-permute-start(bf16[4,128,128]{2,1,0:T(8,128)(2,1)S(1)} %get-tuple-element.142), channel_id=1, source_target_pairs={{0,4},{2,6},{4,0},{6,2},{8,12},{10,14},{12,8},{14,10},{16,20},{18,... | collective-permute-start | bytes 393224 | tf_op jit(solution)/shard_map/ppermute | solution.py:65
  65.0 6.5 %collective-permute-start.9 = (bf16[4,2,56,448]{3,2,0,1:T(8,128)(2,1)}, bf16[4,2,56,448]{3,2,0,1:T(8,128)(2,1)}, u32[]{:S(2)}, u32[]{:S(2)}) collective-permute-start(bf16[4,2,56,448]{3,2,0,1:T(8,128)(2,1)} %pad_maximum_fusion.4), channel_id=1, source_target_pairs={{0,2},{2,0},{4,6},{6,4},{8,10},{10,8},{12,14},{14,12},{16,18},{18,... | collective-permute-start | bytes 1204232 | tf_op jit(solution)/shard_map/ppermute | solution.py:65
  68.2 1.5 collective-permute-start.7
  68.2 10.5 %collective-permute-start.11 = (bf16[128,896]{1,0:T(8,128)(2,1)S(1)}, bf16[128,896]{1,0:T(8,128)(2,1)}, u32[]{:S(2)}, u32[]{:S(2)}) collective-permute-start(bf16[128,896]{1,0:T(8,128)(2,1)S(1)} %bitcast.158), channel_id=1, source_target_pairs={{0,4},{2,6},{4,0},{6,2},{8,12},{10,14},{12,8},{14,10},{16,20},{18,... | collective-permute-start | bytes 688136 | tf_op jit(solution)/shard_map/ppermute | solution.py:65
  77.1 15.7 %copy-start.21 = (bf16[2,64,448]{2,1,0:T(8,128)(2,1)}, bf16[2,64,448]{2,1,0:T(8,128)(2,1)S(1)}, u32[]{:S(2)}) copy-start(bf16[2,64,448]{2,1,0:T(8,128)(2,1)S(1)} %get-tuple-element.98) | copy-start | bytes 344068
  77.1 7.7 %collective-permute-start.10 = (bf16[128,896]{1,0:T(8,128)(2,1)S(1)}, bf16[128,896]{1,0:T(8,128)(2,1)S(1)}, u32[]{:S(2)}, u32[]{:S(2)}) collective-permute-start(bf16[128,896]{1,0:T(8,128)(2,1)S(1)} %bitcast.166), channel_id=1, source_target_pairs={{0,1},{1,0},{2,3},{3,2},{4,5},{5,4},{6,7},{7,6},{8,9},{9,8},{10,11... | collective-permute-start | bytes 688136 | tf_op jit(solution)/shard_map/ppermute | solution.py:47
  79.7 5.3 %collective-permute-start.12 = (bf16[256,896]{1,0:T(8,128)(2,1)S(1)}, bf16[256,896]{1,0:T(8,128)(2,1)S(1)}, u32[]{:S(2)}, u32[]{:S(2)}) collective-permute-start(bf16[256,896]{1,0:T(8,128)(2,1)S(1)} %pad_maximum_fusion.5), channel_id=1, source_target_pairs={{0,2},{2,0},{4,6},{6,4},{8,10},{10,8},{12,14},{14,12},{16,18},{18,... | collective-permute-start | bytes 1376264 | tf_op jit(solution)/shard_map/ppermute | solution.py:65
  85.9 6.9 %collective-permute-start.13 = (bf16[128,896]{1,0:T(8,128)(2,1)S(1)}, bf16[128,896]{1,0:T(8,128)(2,1)S(1)}, u32[]{:S(2)}, u32[]{:S(2)}) collective-permute-start(bf16[128,896]{1,0:T(8,128)(2,1)S(1)} %get-tuple-element.121), channel_id=1, source_target_pairs={{0,4},{2,6},{4,0},{6,2},{8,12},{10,14},{12,8},{14,10},{16,20},{18,... | collective-permute-start | bytes 688136 | tf_op jit(solution)/shard_map/ppermute | solution.py:65
  92.8 1.9 collective-permute-start.14
  116.4 20.5 %copy-start.1 = (bf16[4,2,2,56,448]{4,3,2,1,0:T(8,128)(2,1)S(1)}, bf16[4,2,2,56,448]{4,3,2,1,0:T(8,128)(2,1)}, u32[]{:S(2)}) copy-start(bf16[4,2,2,56,448]{4,3,2,1,0:T(8,128)(2,1)} %copy-done) | copy-start | bytes 2408452
  116.4 20.5 %copy-start.8 = (bf16[2,64,896]{2,1,0:T(8,128)(2,1)S(1)}, bf16[2,64,896]{2,1,0:T(8,128)(2,1)}, u32[]{:S(2)}) copy-start(bf16[2,64,896]{2,1,0:T(8,128)(2,1)} %cotangent_ref.1) | copy-start | bytes 688132
  116.4 20.5 %copy-start.16 = (bf16[128,448]{1,0:T(8,128)(2,1)S(1)}, bf16[128,448]{1,0:T(8,128)(2,1)}, u32[]{:S(2)}) copy-start(bf16[128,448]{1,0:T(8,128)(2,1)} %copy-done.14) | copy-start | bytes 344068
  116.4 2.1 collective-permute-start.15
  119.5 7.7 %collective-permute-start.16 = (bf16[128,896]{1,0:T(8,128)(2,1)S(1)}, bf16[128,896]{1,0:T(8,128)(2,1)S(1)}, u32[]{:S(2)}, u32[]{:S(2)}) collective-permute-start(bf16[128,896]{1,0:T(8,128)(2,1)S(1)} %add_convert_fusion.6), channel_id=1, source_target_pairs={{0,4},{2,6},{4,0},{6,2},{8,12},{10,14},{12,8},{14,10},{16,20},{18,... | collective-permute-start | bytes 688136 | tf_op jit(solution)/shard_map/ppermute | solution.py:65
  121.1 7.2 %collective-permute-start.17 = (bf16[256,896]{1,0:T(8,128)(2,1)}, bf16[256,896]{1,0:T(8,128)(2,1)S(1)}, u32[]{:S(2)}, u32[]{:S(2)}) collective-permute-start(bf16[256,896]{1,0:T(8,128)(2,1)} %get-tuple-element.87), channel_id=1, source_target_pairs={{0,2},{2,0},{4,6},{6,4},{8,10},{10,8},{12,14},{14,12},{16,18},{18,... | collective-permute-start | bytes 1376264 | tf_op jit(solution)/shard_map/ppermute | solution.py:65
  128.3 7.0 %collective-permute-start.18 = (bf16[128,896]{1,0:T(8,128)(2,1)S(1)}, bf16[128,896]{1,0:T(8,128)(2,1)S(1)}, u32[]{:S(2)}, u32[]{:S(2)}) collective-permute-start(bf16[128,896]{1,0:T(8,128)(2,1)S(1)} %add_convert_fusion.5.own_ref), channel_id=1, source_target_pairs={{0,1},{1,0},{2,3},{3,2},{4,5},{5,4},{6,7},{7,6},{8,9},{9,8},{10,11... | collective-permute-start | bytes 688136 | tf_op jit(solution)/shard_map/ppermute | solution.py:662
  135.3 6.2 %collective-permute-start.19 = (bf16[128,896]{1,0:T(8,128)(2,1)S(1)}, bf16[128,896]{1,0:T(8,128)(2,1)S(1)}, u32[]{:S(2)}, u32[]{:S(2)}) collective-permute-start(bf16[128,896]{1,0:T(8,128)(2,1)S(1)} %slice.127), channel_id=1, source_target_pairs={{0,4},{2,6},{4,0},{6,2},{8,12},{10,14},{12,8},{14,10},{16,20},{18,... | collective-permute-start | bytes 688136 | tf_op jit(solution)/shard_map/ppermute | solution.py:65
  142.2 1.6 collective-permute-start.20
  146.4 6.2 %collective-permute-start.22 = (bf16[8,56,896]{2,1,0:T(8,128)(2,1)}, bf16[8,56,896]{2,1,0:T(8,128)(2,1)}, u32[]{:S(2)}, u32[]{:S(2)}) collective-permute-start(bf16[8,56,896]{2,1,0:T(8,128)(2,1)} %get-tuple-element.101), channel_id=1, source_target_pairs={{0,2},{2,0},{4,6},{6,4},{8,10},{10,8},{12,14},{14,12},{16,18},{18,... | collective-permute-start | bytes 2408456 | tf_op jit(solution)/shard_map/ppermute | solution.py:65
  146.7 5.8 %collective-permute-start.21 = (bf16[512,128]{1,0:T(8,128)(2,1)S(1)}, bf16[512,128]{1,0:T(8,128)(2,1)S(1)}, u32[]{:S(2)}, u32[]{:S(2)}) collective-permute-start(bf16[512,128]{1,0:T(8,128)(2,1)S(1)} %slice.161), channel_id=1, source_target_pairs={{0,4},{2,6},{4,0},{6,2},{8,12},{10,14},{12,8},{14,10},{16,20},{18,... | collective-permute-start | bytes 393224 | tf_op jit(solution)/shard_map/ppermute | solution.py:65
  155.9 11.2 %collective-permute-start.26 = (bf16[4,56,896]{2,1,0:T(8,128)(2,1)}, bf16[4,56,896]{2,1,0:T(8,128)(2,1)}, u32[]{:S(2)}, u32[]{:S(2)}) collective-permute-start(bf16[4,56,896]{2,1,0:T(8,128)(2,1)} %dynamic-slice_bitcast_fusion), channel_id=1, source_target_pairs={{0,4},{2,6},{4,0},{6,2},{8,12},{10,14},{12,8},{14,10},{16,20},{18,... | collective-permute-start | bytes 1204232 | tf_op jit(solution)/shard_map/ppermute | solution.py:65
  157.4 5.0 %collective-permute-start.23 = (bf16[128,128]{1,0:T(8,128)(2,1)S(1)}, bf16[128,128]{1,0:T(8,128)(2,1)S(1)}, u32[]{:S(2)}, u32[]{:S(2)}) collective-permute-start(bf16[128,128]{1,0:T(8,128)(2,1)S(1)} %get-tuple-element.138), channel_id=1, source_target_pairs={{0,8},{2,10},{4,12},{6,14},{8,0},{10,2},{12,4},{14,6},{16,24},{18,... | collective-permute-start | bytes 98312 | tf_op jit(solution)/shard_map/ppermute | solution.py:65
  157.5 9.6 %collective-permute-start.24 = (bf16[128,128]{1,0:T(8,128)(2,1)S(1)}, bf16[128,128]{1,0:T(8,128)(2,1)S(1)}, u32[]{:S(2)}, u32[]{:S(2)}) collective-permute-start(bf16[128,128]{1,0:T(8,128)(2,1)S(1)} %get-tuple-element.140), channel_id=1, source_target_pairs={{0,16},{2,18},{4,20},{6,22},{8,24},{10,26},{12,28},{14,30},{16,0},... | collective-permute-start | bytes 98312 | tf_op jit(solution)/shard_map/ppermute | solution.py:65
  159.0 8.1 %collective-permute-start.25 = (bf16[128,128]{1,0:T(8,128)(2,1)S(1)}, bf16[128,128]{1,0:T(8,128)(2,1)S(1)}, u32[]{:S(2)}, u32[]{:S(2)}) collective-permute-start(bf16[128,128]{1,0:T(8,128)(2,1)S(1)} %get-tuple-element.139), channel_id=1, source_target_pairs={{0,24},{2,26},{4,28},{6,30},{8,16},{10,18},{12,20},{14,22},{16,8},... | collective-permute-start | bytes 98312 | tf_op jit(solution)/shard_map/ppermute | solution.py:65
  169.6 1.8 collective-permute-start.27
  169.8 8.1 %collective-permute-start.30 = (bf16[128,896]{1,0:T(8,128)(2,1)S(1)}, bf16[128,896]{1,0:T(8,128)(2,1)S(1)}, u32[]{:S(2)}, u32[]{:S(2)}) collective-permute-start(bf16[128,896]{1,0:T(8,128)(2,1)S(1)} %copy-done.30), channel_id=1, source_target_pairs={{0,1},{1,0},{2,3},{3,2},{4,5},{5,4},{6,7},{7,6},{8,9},{9,8},{10,11... | collective-permute-start | bytes 688136 | tf_op jit(solution)/shard_map/ppermute | solution.py:706
  171.4 7.2 %collective-permute-start.28 = (bf16[4,56,256]{2,1,0:T(8,128)(2,1)S(1)}, bf16[4,56,256]{2,1,0:T(8,128)(2,1)S(1)}, u32[]{:S(2)}, u32[]{:S(2)}) collective-permute-start(bf16[4,56,256]{2,1,0:T(8,128)(2,1)S(1)} %dynamic-slice_bitcast_fusion.4), channel_id=1, source_target_pairs={{0,4},{2,6},{4,0},{6,2},{8,12},{10,14},{12,8},{14,10},{16,20},{18,... | collective-permute-start | bytes 344072 | tf_op jit(solution)/shard_map/ppermute | solution.py:65
  178.7 4.2 %collective-permute-start.29 = (bf16[4,56,128]{2,1,0:T(8,128)(2,1)S(1)}, bf16[4,56,128]{2,1,0:T(8,128)(2,1)S(1)}, u32[]{:S(2)}, u32[]{:S(2)}) collective-permute-start(bf16[4,56,128]{2,1,0:T(8,128)(2,1)S(1)} %slice.163), channel_id=1, source_target_pairs={{0,1},{1,0},{2,3},{3,2},{4,5},{5,4},{6,7},{7,6},{8,9},{9,8},{10,11... | collective-permute-start | bytes 172040 | tf_op jit(solution)/shard_map/ppermute | solution.py:763
  183.1 16.4 %copy-start.44 = (bf16[56]{0:T(256)(128)(2,1)S(1)}, bf16[56]{0:T(256)(128)(2,1)}, u32[]{:S(2)}) copy-start(bf16[56]{0:T(256)(128)(2,1)} %param.19) | copy-start | bytes 340
  183.1 16.9 %copy-start.45 = (bf16[56]{0:T(256)(128)(2,1)S(1)}, bf16[56]{0:T(256)(128)(2,1)}, u32[]{:S(2)}) copy-start(bf16[56]{0:T(256)(128)(2,1)} %param.20) | copy-start | bytes 340
  183.1 9.7 %collective-permute-start.32 = (bf16[56,1152]{1,0:T(8,128)(2,1)S(1)}, bf16[56,1152]{1,0:T(8,128)(2,1)S(1)}, u32[]{:S(2)}, u32[]{:S(2)}) collective-permute-start(bf16[56,1152]{1,0:T(8,128)(2,1)S(1)} %get-tuple-element.131), channel_id=1, source_target_pairs={{0,8},{2,10},{4,12},{6,14},{8,0},{10,2},{12,4},{14,6},{16,24},{18,... | collective-permute-start | bytes 387080 | tf_op jit(solution)/shard_map/ppermute | solution.py:65
  184.8 12.1 %collective-permute-start.33 = (bf16[56,1152]{1,0:T(8,128)(2,1)S(1)}, bf16[56,1152]{1,0:T(8,128)(2,1)S(1)}, u32[]{:S(2)}, u32[]{:S(2)}) collective-permute-start(bf16[56,1152]{1,0:T(8,128)(2,1)S(1)} %get-tuple-element.133), channel_id=1, source_target_pairs={{0,16},{2,18},{4,20},{6,22},{8,24},{10,26},{12,28},{14,30},{16,0},... | collective-permute-start | bytes 387080 | tf_op jit(solution)/shard_map/ppermute | solution.py:65
  185.2 11.6 %collective-permute-start.34 = (bf16[56,1152]{1,0:T(8,128)(2,1)S(1)}, bf16[56,1152]{1,0:T(8,128)(2,1)S(1)}, u32[]{:S(2)}, u32[]{:S(2)}) collective-permute-start(bf16[56,1152]{1,0:T(8,128)(2,1)S(1)} %get-tuple-element.132), channel_id=1, source_target_pairs={{0,24},{2,26},{4,28},{6,30},{8,16},{10,18},{12,20},{14,22},{16,8},... | collective-permute-start | bytes 387080 | tf_op jit(solution)/shard_map/ppermute | solution.py:65
  187.7 16.1 %all-to-all-start.1 = ((bf16[4,56,1920]{2,1,0:T(8,128)(2,1)}), bf16[4,56,1920]{2,1,0:T(8,128)(2,1)S(1)}, u32[]{:S(2)}, u32[]{:S(2)}) async-start(bf16[4,56,1920]{2,1,0:T(8,128)(2,1)} %bitcast.186), calls=%async_computation.2 | async-start | bytes 1720320 | tf_op jit(solution)/shard_map/all_to_all | solution.py:68
  191.3 9.9 %collective-permute-start.31 = (bf16[128,896]{1,0:T(8,128)(2,1)S(1)}, bf16[128,896]{1,0:T(8,128)(2,1)S(1)}, u32[]{:S(2)}, u32[]{:S(2)}) collective-permute-start(bf16[128,896]{1,0:T(8,128)(2,1)S(1)} %get-tuple-element.115), channel_id=1, source_target_pairs={{0,1},{1,0},{2,3},{3,2},{4,5},{5,4},{6,7},{7,6},{8,9},{9,8},{10,11... | collective-permute-start | bytes 688136 | tf_op jit(solution)/shard_map/ppermute | solution.py:47
  (38 other events, 215.6 us)
Sparse Core Ops, SparseCore 0:
  33.7 71.5 all-gather.2
  116.5 65.4 reduce-scatter.1
